TPU v7x, 32 devices: a whole 2x2x4 slice. The times are simulated.
32 devices in a mesh: rows: 4 (over y, x), tp: 8 (over z, core).
Axes of the slice: x: 2, y: 2, z: 4, core: 2. Of those that a mesh axis runs over, the one named last changes fastest.
Arguments:
- block_input: bfloat16 [4096, 2048], P(('rows', 'tp')), may hold values from -6 to 6
- norm_gain: bfloat16 [2048], replicated, may hold values from 0.5 to 1.5
- norm_bias: bfloat16 [2048], replicated, may hold values from -1.5 to 1.5
- qkv_weight: bfloat16 [3, 2048, 2048], P(None, 'tp'), may hold values from -0.125 to 0.125
- qkv_bias: bfloat16 [3, 2048], P(None, 'tp'), may hold values from -1 to 1
- out_weight: bfloat16 [2048, 2048], P('tp'), may hold values from -0.75 to 0.75
- gate_weight: bfloat16 [5632, 2048], P('tp'), may hold values from -0.125 to 0.125
- up_weight: bfloat16 [5632, 2048], P('tp'), may hold values from -0.125 to 0.125
- down_weight: bfloat16 [5632, 2048], P('tp'), may hold values from -0.078125 to 0.078125
- cotangent: bfloat16 [4096, 2048], P(('rows', 'tp')), may hold values from -6 to 6
- doc_lengths: int32 [4, 8], P('rows'), may hold values from 1 to 512, 1024 in all within a row
Outputs:
- output: bfloat16 [4096, 2048], P(('rows', 'tp'))
- input_grad: float32 [4096, 2048], P(('rows', 'tp'))
- gain_grad: float32 [2048], replicated
- bias_grad: float32 [2048], replicated
- qkv_grad: float32 [3, 2048, 2048], P(None, 'tp')
- qkv_bias_grad: float32 [3, 2048], P(None, 'tp')
- out_grad: float32 [2048, 2048], P('tp')
- gate_grad: float32 [5632, 2048], P('tp')
- up_grad: float32 [5632, 2048], P('tp')
- down_grad: float32 [5632, 2048], P('tp')
Inputs may be any that keep to these rules, and one draw needn't show every extreme that they name: `doc_lengths`: each row holds the lengths of the 8 consecutive pieces of one packed row in order, summing to 1024; the last piece is padding; in every row the longest piece has exactly 512 tokens.
All inputs are finite; a program needn't handle non-finite values.
Results may differ from a plain program's by a relative error of at most 0.0099.
Values may be sent and summed in bfloat16 or wider, within the bound.
No kernel may reach another device: no remote copies, remote signals or barrier semaphores. Data moves between devices by JAX's collectives and lax.ppermute only.
A program may use at most 192 MiB of HBM per device.

v0:
```python
import functools
import jax
import jax.numpy as jnp
from jax import lax
from jax.experimental import pallas as pl
from jax.experimental.pallas import tpu as pltpu
from jax.sharding import PartitionSpec as P

HEAD = 64
ROT = 16
MASKED = -1e30
LONG = 1000
EPSILON = 1e-05
ROOM = 16 * 2**20
IN_VMEM = pl.BlockSpec(memory_space=pltpu.VMEM)
IN_SMEM = pl.BlockSpec(memory_space=pltpu.SMEM)


def dot_rows(a, b):
    return lax.dot_general(a, b, (((1,), (0,)), ((), ())), preferred_element_type=jnp.float32)


def dot_lanes(a, b):
    return lax.dot_general(a, b, (((1,), (1,)), ((), ())), preferred_element_type=jnp.float32)


def dot_tall(a, b):
    return lax.dot_general(a, b, (((0,), (0,)), ((), ())), preferred_element_type=jnp.float32)


def turn(values, tables, sign):
    half = ROT // 2
    width = values.shape[1]
    tables = [jnp.concatenate([part] * (width // 128), axis=1) for part in tables]
    up = pltpu.roll(values, width - half, 1)
    down = pltpu.roll(values, half, 1)
    return values * tables[0] + sign * (up * tables[1] + down * tables[2])


def of_head(head, shape):
    return lax.broadcasted_iota(jnp.int32, shape, 1) // HEAD == head


def over_blocks(row_len, block, body):
    longest = row_len // 2
    blocks = row_len // block
    if blocks <= 8:
        for index in range(blocks):
            first = index * block
            start = max(0, first + block - (longest + block))
            body(first, start, first + block - start)
    else:
        size = longest + block

        def step(index, carry):
            first = pl.multiple_of(index * block, block)
            start = pl.multiple_of(jnp.maximum(first - longest, 0), block)
            body(first, start, size)
            return carry

        lax.fori_loop(0, blocks, step, 0)


def mask_of(seg_col, seg_row, first, start, block, size):
    rows = first + lax.broadcasted_iota(jnp.int32, (block, size), 0)
    keys = start + lax.broadcasted_iota(jnp.int32, (block, size), 1)
    same = seg_col[pl.ds(first, block), 0:1] == seg_row[0:1, pl.ds(start, size)]
    return jnp.where(same & (keys <= rows), 0.0, MASKED)


def forward_kernel(
    heads,
    hidden_in,
    projection,
    shift,
    tables,
    seg_col,
    seg_row,
    query,
    key,
    value,
    context,
    context_t,
    logsum,
):
    row_len, width = query.shape
    block = 256
    scale = HEAD ** (-0.5)
    for first in range(0, row_len, block):
        here = slice(first, first + block)
        lines = dot_lanes(hidden_in[here, :], projection[...]) + shift[...]
        turning = [tables[part, here, :] for part in range(3)]
        asked = turn(lines[:, 0:width], turning, 1.0).astype(jnp.bfloat16)
        query[here, :] = asked * jnp.bfloat16(scale)
        key[here, :] = turn(lines[:, width : 2 * width], turning, 1.0).astype(jnp.bfloat16)
        value[here, :] = lines[:, 2 * width : 3 * width].astype(jnp.bfloat16)

    def one_block(first, start, size):
        bias = mask_of(seg_col, seg_row, first, start, block, size)
        here = query[pl.ds(first, block), :]
        keys = key[pl.ds(start, size), :]
        values = value[pl.ds(start, size), :]
        total = jnp.zeros((block, width), jnp.float32)
        lane = lax.broadcasted_iota(jnp.int32, (block, 128), 1)
        sums = jnp.zeros((block, 128), jnp.float32)
        for head in range(heads):
            mine = of_head(head, (block, width))
            scores = dot_lanes(jnp.where(mine, here, jnp.bfloat16(0)), keys) + bias
            highest = jnp.max(scores, axis=1, keepdims=True)
            raised = jnp.exp(scores - highest)
            amount = jnp.sum(raised, axis=1, keepdims=True)
            weights = (raised * (1.0 / amount)).astype(jnp.bfloat16)
            total = jnp.where(mine, dot_rows(weights, values), total)
            sums = jnp.where(lane == head, highest + jnp.log(amount), sums)
        context[pl.ds(first, block), :] = total.astype(jnp.bfloat16)
        context_t[:, pl.ds(first, block)] = total.T.astype(jnp.bfloat16)
        logsum[pl.ds(first, block), :] = sums

    over_blocks(row_len, block, one_block)


def attend_forward(hidden_in, projection, shift, tables, seg_col, seg_row, heads):
    row_len, width = hidden_in.shape[0], projection.shape[0] // 3
    low = jax.ShapeDtypeStruct((row_len, width), jnp.bfloat16)
    return pl.pallas_call(
        functools.partial(forward_kernel, heads),
        in_specs=[IN_VMEM] * 6,
        out_shape=(
            low,
            low,
            low,
            low,
            jax.ShapeDtypeStruct((width, row_len), jnp.bfloat16),
            jax.ShapeDtypeStruct((row_len, 128), jnp.float32),
        ),
        compiler_params=pltpu.CompilerParams(vmem_limit_bytes=ROOM + 4096 * row_len),
        cost_estimate=busy(8.5),
        name="attend_forward",
    )(hidden_in, projection, shift, tables, seg_col, seg_row)


def backward_kernel(
    heads,
    query,
    key,
    value,
    grad_left,
    grad_right,
    out_weight,
    logsum,
    tables,
    seg_col,
    seg_row,
    lines_low,
    lines_low_t,
    bias_grad,
    key_grad,
    value_grad,
):
    row_len, width = query.shape
    block = 256
    scale = HEAD ** (-0.5)
    half = grad_left.shape[1]
    key_grad[...] = jnp.zeros_like(key_grad)
    value_grad[...] = jnp.zeros_like(value_grad)
    bias_grad[...] = jnp.zeros_like(bias_grad)

    def put(part, first, grads):
        low = grads.astype(jnp.bfloat16)
        wide = low.astype(jnp.float32)
        columns = slice(part * width, (part + 1) * width)
        lines_low[pl.ds(first, block), columns] = low
        lines_low_t[columns, pl.ds(first, block)] = wide.T.astype(jnp.bfloat16)
        bias_grad[0:1, columns] += jnp.sum(wide, axis=0, keepdims=True)

    def one_block(first, start, size):
        bias = mask_of(seg_col, seg_row, first, start, block, size)
        here = query[pl.ds(first, block), :]
        here_rows = pl.ds(first, block)
        grad_here = dot_lanes(grad_left[here_rows, :], out_weight[:, 0:half])
        grad_here = grad_here + dot_lanes(grad_right[here_rows, :], out_weight[:, half:])
        grad_here = grad_here.astype(jnp.bfloat16)
        keys = key[pl.ds(start, size), :]
        values = value[pl.ds(start, size), :]
        sums = logsum[pl.ds(first, block), :]
        total = jnp.zeros((block, width), jnp.float32)
        for head in range(heads):
            mine = of_head(head, (block, width))
            asked = jnp.where(mine, here, jnp.bfloat16(0))
            pulled = jnp.where(mine, grad_here, jnp.bfloat16(0))
            scores = dot_lanes(asked, keys) + bias
            probs = jnp.exp(scores - sums[:, head : head + 1])
            prob_grad = dot_lanes(pulled, values)
            value_grad[pl.ds(start, size), :] += dot_tall(probs.astype(jnp.bfloat16), pulled)
            inner = jnp.sum(probs * prob_grad, axis=1, keepdims=True)
            score_low = (probs * (prob_grad - inner)).astype(jnp.bfloat16)
            total = jnp.where(mine, dot_rows(score_low, keys), total)
            key_grad[pl.ds(start, size), :] += dot_tall(score_low, asked)
        here_tables = [tables[part, pl.ds(first, block), :] for part in range(3)]
        put(0, first, turn(total * scale, here_tables, -1.0))

    over_blocks(row_len, block, one_block)
    for index in range(row_len // block):
        first = index * block
        here_tables = [tables[part, pl.ds(first, block), :] for part in range(3)]
        put(1, first, turn(key_grad[pl.ds(first, block), :], here_tables, -1.0))
        put(2, first, value_grad[pl.ds(first, block), :])


def attend_backward(
    query, key, value, grads, out_weight, logsum, tables, seg_col, seg_row, heads
):
    row_len, width = query.shape
    return pl.pallas_call(
        functools.partial(backward_kernel, heads),
        in_specs=[IN_VMEM] * 10,
        out_shape=(
            jax.ShapeDtypeStruct((row_len, 3 * width), jnp.bfloat16),
            jax.ShapeDtypeStruct((3 * width, row_len), jnp.bfloat16),
            jax.ShapeDtypeStruct((8, 3 * width), jnp.float32),
        ),
        scratch_shapes=[
            pltpu.VMEM((row_len, width), jnp.float32),
            pltpu.VMEM((row_len, width), jnp.float32),
        ],
        compiler_params=pltpu.CompilerParams(vmem_limit_bytes=ROOM + 4096 * row_len),
        cost_estimate=busy(13.3),
        name="attend_backward",
    )(query, key, value, *grads, out_weight, logsum, tables, seg_col, seg_row)


def layout(doc_lengths, row_len):
    ends = jnp.cumsum(doc_lengths[0])
    starts = ends - doc_lengths[0]
    places = jnp.arange(row_len, dtype=jnp.int32)
    segment = jnp.sum((places[:, None] >= ends[None, :]).astype(jnp.int32), axis=1)
    chosen = segment[:, None] == jnp.arange(ends.shape[0], dtype=jnp.int32)[None, :]
    first = jnp.sum(jnp.where(chosen, starts[None, :], 0), axis=1)
    return segment, places - first, segment < ends.shape[0] - 1


def turns(position):
    half = ROT // 2
    lane = lax.broadcasted_iota(jnp.int32, (position.shape[0], 128), 1) % HEAD
    freq = 10000.0 ** (-((lane % half).astype(jnp.float32) * (2.0 / ROT)))
    angle = position.astype(jnp.float32)[:, None] * freq
    cosine, sine = jnp.cos(angle), jnp.sin(angle)
    return jnp.stack(
        [
            jnp.where(lane < ROT, cosine, 1.0),
            jnp.where(lane < half, -sine, 0.0),
            jnp.where((lane >= half) & (lane < ROT), sine, 0.0),
        ]
    )


def busy(time):
    return pl.CostEstimate(flops=int(time * 1.5 * 10**9), bytes_accessed=0, transcendentals=0)


def blocks_of(tokens):
    return min(512, tokens)


def gated_kernel(hidden_in, gate_weight, up_weight, gate, up, mixed, mixed_t):
    gate_here = dot_lanes(gate_weight[...], hidden_in[...])
    up_here = dot_lanes(up_weight[...], hidden_in[...])
    gate[...] = gate_here
    up[...] = up_here
    total = gate_here * jax.nn.sigmoid(gate_here) * up_here
    mixed_t[...] = total.astype(jnp.bfloat16)
    mixed[...] = total.T.astype(jnp.bfloat16)


def gated_forward(hidden_in, gate_weight, up_weight):
    (tokens, features), units = hidden_in.shape, gate_weight.shape[0]
    block = blocks_of(tokens)
    tall = pl.BlockSpec((units, block), lambda step: (0, step))
    flat = pl.BlockSpec((block, units), lambda step: (step, 0))
    return pl.pallas_call(
        gated_kernel,
        grid=(tokens // block,),
        in_specs=[pl.BlockSpec((block, features), lambda step: (step, 0)), IN_VMEM, IN_VMEM],
        out_specs=[tall, tall, flat, tall],
        out_shape=[
            jax.ShapeDtypeStruct((units, tokens), jnp.float32),
            jax.ShapeDtypeStruct((units, tokens), jnp.float32),
            jax.ShapeDtypeStruct((tokens, units), jnp.bfloat16),
            jax.ShapeDtypeStruct((units, tokens), jnp.bfloat16),
        ],
        compiler_params=pltpu.CompilerParams(vmem_limit_bytes=ROOM),
        cost_estimate=busy(7.5),
        name="gated_forward",
    )(hidden_in, gate_weight, up_weight)


def gated_back_kernel(
    grad_left, grad_right, down_weight, gate, up, gate_low, gate_low_t, up_low, up_low_t
):
    half = grad_left.shape[1]
    mixed_grad = dot_lanes(down_weight[:, 0:half], grad_left[...])
    mixed_grad = mixed_grad + dot_lanes(down_weight[:, half:], grad_right[...])
    gate_here = gate[...]
    sigmoid = jax.nn.sigmoid(gate_here)
    pulled = mixed_grad * sigmoid
    gate_grad = pulled * up[...] * (1.0 + gate_here * (1.0 - sigmoid))
    up_grad = pulled * gate_here
    gate_low_t[...] = gate_grad.astype(jnp.bfloat16)
    up_low_t[...] = up_grad.astype(jnp.bfloat16)
    gate_low[...] = gate_grad.T.astype(jnp.bfloat16)
    up_low[...] = up_grad.T.astype(jnp.bfloat16)


def gated_backward(grads, down_weight, gate, up):
    (tokens, half), units = grads[0].shape, down_weight.shape[0]
    block = blocks_of(tokens)
    tall = pl.BlockSpec((units, block), lambda step: (0, step))
    flat = pl.BlockSpec((block, units), lambda step: (step, 0))
    wide = jax.ShapeDtypeStruct((tokens, units), jnp.bfloat16)
    long = jax.ShapeDtypeStruct((units, tokens), jnp.bfloat16)
    return pl.pallas_call(
        gated_back_kernel,
        grid=(tokens // block,),
        in_specs=[pl.BlockSpec((block, half), lambda step: (step, 0))] * 2 + [IN_VMEM, tall, tall],
        out_specs=[flat, tall, flat, tall],
        out_shape=[wide, long, wide, long],
        compiler_params=pltpu.CompilerParams(vmem_limit_bytes=ROOM),
        cost_estimate=busy(5.4),
        name="gated_backward",
    )(*grads, down_weight, gate, up)


def merge_kernel(count, *refs):
    total = dot_rows(refs[0][...], refs[count][...])
    for index in range(1, count):
        total = total + dot_rows(refs[index][...], refs[count + index][...])
    refs[2 * count][...] = total.astype(jnp.bfloat16)


def merge(lhs, weights):
    tokens, features, count = lhs[0].shape[0], weights[0].shape[1], len(lhs)
    block = min(256, tokens)
    return pl.pallas_call(
        functools.partial(merge_kernel, count),
        grid=(tokens // block,),
        in_specs=[
            *(pl.BlockSpec((block, part.shape[1]), lambda step: (step, 0)) for part in lhs),
            *([IN_VMEM] * count),
        ],
        out_specs=pl.BlockSpec((block, features), lambda step: (step, 0)),
        out_shape=jax.ShapeDtypeStruct((tokens, features), jnp.bfloat16),
        compiler_params=pltpu.CompilerParams(vmem_limit_bytes=ROOM),
        cost_estimate=busy(8),
        name="merge",
    )(*lhs, *weights)


def stacked(lhs, rhs, first, wide, keep):
    row = 0
    block = rhs[:, pl.ds(pl.multiple_of(first, 128), wide)]
    for part in lhs:
        keep(row, part.shape[0], dot_rows(part[...], block))
        row += part.shape[0]


def send_kernel(count, wide, order, *refs):
    lhs, rhs, outs = refs[:count], refs[count], refs[-2:]
    for half, out in enumerate(outs):

        def keep(row, rows, term, out=out):
            out[row : row + rows, :] = term.astype(jnp.bfloat16)

        stacked(lhs, rhs, order[half], wide, keep)


def join_kernel(count, parts, order, *refs):
    lhs, rhs, came = refs[:count], refs[count : count + parts], refs[count + parts : -5]
    outs, total = refs[-5:-1], refs[-1]
    for half in range(2):
        at, bit = 0, order[parts, half]
        for part in range(parts):
            here = came[2 * part + half]
            wide = here.shape[1]
            narrow = wide // 2

            def keep(row, rows, term, here=here, wide=wide):
                there = here[row : row + rows, :].astype(jnp.float32)
                total[row : row + rows, 0:wide] = (term + there).astype(jnp.bfloat16)

            stacked(lhs, rhs[part], order[part, half], wide, keep)
            for out, which in ((outs[2 * half], 1 - bit), (outs[2 * half + 1], bit)):
                columns = pl.ds(pl.multiple_of(which * narrow, narrow), narrow)
                out[:, at : at + narrow] = total[:, columns]
            at += narrow


def place_kernel(takes, olds, order, *refs):
    count = 1 + max(take[0] for take in takes)
    pieces, outs = refs[:count], refs[count + olds :]
    step = pl.program_id(0)
    for index, (which, row, column) in enumerate(takes):
        piece = pieces[which]

        @pl.when(step == index)
        def _(piece=piece, first=row, column=column):
            for out in outs:
                size, narrow = out.shape
                block = piece[first : first + size, column : column + narrow]
                out[...] = block.astype(jnp.float32)
                first += size


def place(pieces, takes, order, sizes, narrow, features, old):
    return pl.pallas_call(
        functools.partial(place_kernel, takes, len(old)),
        grid_spec=pltpu.PrefetchScalarGridSpec(
            num_scalar_prefetch=1,
            grid=(len(takes),),
            in_specs=[IN_VMEM] * len(pieces) + [pl.BlockSpec(memory_space=pl.ANY)] * len(old),
            out_specs=[
                pl.BlockSpec((size, narrow), lambda step, order: (0, order[step]))
                for size in sizes
            ],
        ),
        out_shape=[jax.ShapeDtypeStruct((size, features), jnp.float32) for size in sizes],
        input_output_aliases={1 + len(pieces) + index: index for index in range(len(old))},
        compiler_params=pltpu.CompilerParams(vmem_limit_bytes=ROOM),
        cost_estimate=busy(sum(sizes) * len(takes) * narrow / 300_000),
        name="place",
    )(jnp.stack(order).astype(jnp.int32), *pieces, *old)


def lay_kernel(where, *refs):
    mine, theirs, out, sems = refs[0:6], refs[6:12], refs[12], refs[13]
    for inner in (0, 1):

        @pl.when(where[5] == inner)
        def _(inner=inner):
            taken = (0, 1, 3 - inner, 5 - inner)
            copies = []
            for place, index in enumerate(taken):
                for side, pieces in enumerate((mine, theirs)):
                    core = where[4] if side == 0 else 1 - where[4]
                    target = out.at[where[place], core]
                    copies.append(
                        pltpu.make_async_copy(pieces[index], target, sems.at[place, side])
                    )
            for copy in copies:
                copy.start()
            for copy in copies:
                copy.wait()


def gather(values):
    line = [(2 * i + c, 2 * (i ^ 1) + c) for i in range(4) for c in range(2)]
    middle = [(2 * i + c, 2 * j + c) for i, j in ((0, 0), (1, 2), (2, 1), (3, 3)) for c in range(2)]
    core = [(i, i ^ 1) for i in range(8)]
    me = lax.axis_index("tp")
    chip = me // 2

    def move(pieces, pairs):
        return lax.ppermute(pieces, "tp", pairs)

    near = move(values, line)
    across = move(values, middle)
    far = move(across, line)
    beyond = move(near, middle)
    last = move(beyond, line)
    mine = [values, near, across, far, beyond, last]
    theirs = [move(pieces, core) for pieces in mine]
    low, inner = chip < 2, (chip == 1) | (chip == 2)
    where = [chip, chip ^ 1, 1 + low, 3 * low, me % 2, inner]
    where = jnp.stack([jnp.asarray(entry, jnp.int32) for entry in where])
    shard, features = values.shape
    out = pl.pallas_call(
        lay_kernel,
        in_specs=[IN_SMEM] + [pl.BlockSpec(memory_space=pl.ANY)] * 12,
        out_specs=pl.BlockSpec(memory_space=pl.ANY),
        out_shape=jax.ShapeDtypeStruct((4, 2, shard, features), values.dtype),
        scratch_shapes=[pltpu.SemaphoreType.DMA((4, 2))],
        compiler_params=pltpu.CompilerParams(vmem_limit_bytes=4 * 2**20),
        cost_estimate=busy(2),
        name="lay",
    )(where, *mine, *theirs)
    return out.reshape(8 * shard, features)


NEAR = [(0, 1), (1, 0), (2, 3), (3, 2)]
FAR = [(0, 2), (2, 0), (1, 3), (3, 1)]
PATHS = ((NEAR, FAR), (FAR, NEAR))


def after(value, *others):
    return lax.optimization_barrier((value, others))[0]


class Sum:
    def __init__(self, lhs, parts, time=0):
        row = lax.axis_index("rows")
        near, far = row % 2, row // 2
        self.bits = ((near, far), (far, near))
        self.lhs, self.parts, self.time = lhs, parts, time
        self.rows, self.sizes = sum(part.shape[0] for part in lhs), [part.shape[0] for part in lhs]
        self.came = []

    def first(self, part, half, bit):
        return part.shape[1] // 8 * (4 * half + 2 * bit)

    def piece(self, wide):
        return jax.ShapeDtypeStruct((self.rows, wide), jnp.bfloat16)

    def room(self):
        return pltpu.CompilerParams(vmem_limit_bytes=ROOM + 2048 * self.lhs[0].shape[1])

    def send(self, part, *earlier):
        rhs = self.parts[part]
        order = jnp.stack([self.first(rhs, half, 1 - self.bits[half][0]) for half in range(2)])
        wide = rhs.shape[1] // 4
        head = after(self.lhs[0], *earlier)
        sent = pl.pallas_call(
            functools.partial(send_kernel, len(self.lhs), wide),
            in_specs=[IN_SMEM] + [IN_VMEM] * (len(self.lhs) + 1),
            out_shape=[self.piece(wide)] * 2,
            compiler_params=self.room(),
            cost_estimate=busy(self.rows * wide / 131072),
            name="send_terms",
        )(order.astype(jnp.int32), head, *self.lhs[1:], rhs)
        self.came += [lax.ppermute(sent[half], "rows", PATHS[half][0]) for half in range(2)]
        return sent

    def join(self, *earlier):
        order = [[self.first(part, half, self.bits[half][0]) for half in range(2)] for part in self.parts]
        order.append([self.bits[0][1], self.bits[1][1]])
        wide = sum(part.shape[1] // 8 for part in self.parts)
        head = after(self.lhs[0], *earlier)
        outs = pl.pallas_call(
            functools.partial(join_kernel, len(self.lhs), len(self.parts)),
            in_specs=[IN_SMEM] + [IN_VMEM] * (len(self.lhs) + 3 * len(self.parts)),
            out_shape=[self.piece(wide)] * 4,
            scratch_shapes=[pltpu.VMEM((self.rows, 2 * wide), jnp.bfloat16)],
            compiler_params=self.room(),
            cost_estimate=busy(self.time if self.time else self.rows / 256),
            name="join_terms",
        )(jnp.array(order).astype(jnp.int32), head, *self.lhs[1:], *self.parts, *self.came)
        self.mine = [outs[1], outs[3]]
        self.came = [lax.ppermute(outs[2 * half], "rows", PATHS[half][1]) for half in range(2)]
        return outs

    def total(self, *earlier):
        mine = lax.optimization_barrier((*self.mine, *earlier))[:2]
        self.mine = [mine[half] + self.came[half] for half in range(2)]
        self.across = [lax.ppermute(self.mine[half], "rows", PATHS[half][1]) for half in range(2)]
        return self.mine

    def share(self, *earlier):
        mine = lax.optimization_barrier((*self.mine, *earlier))[:2]
        both = [jnp.concatenate([mine[half], self.across[half]]) for half in range(2)]
        self.last = [lax.ppermute(both[half], "rows", PATHS[half][0]) for half in range(2)]
        return both

    def place(self, pieces, kinds, old, *earlier):
        features = sum(part.shape[1] for part in self.parts)
        narrow = min(part.shape[1] // 8 for part in self.parts)
        takes, order = [], []
        for pair, places in enumerate(kinds):
            for half in range(2):
                a, b = self.bits[half]
                for index, (first, second) in enumerate(places):
                    block = 4 * half + 2 * jnp.abs(a - first) + jnp.abs(b - second)
                    for part in range(len(self.parts)):
                        takes.append((2 * pair + half, index * self.rows, part * narrow))
                        order.append(8 * part + block)
        pieces = lax.optimization_barrier((*pieces, *earlier))[: len(pieces)]
        return place(pieces, takes, order, self.sizes, narrow, features, old)

    def place_early(self, *earlier):
        pieces = [*self.mine, *self.across]
        return self.place(pieces, [[(0, 0)], [(0, 1)]], (), *earlier)

    def place_last(self, old, *earlier):
        return self.place(self.last, [[(1, 0), (1, 1)]], old, *earlier)


def sum_everywhere(values, axis):
    size, step = lax.axis_size(axis), 1
    while step < size:
        values = values + lax.ppermute(values, axis, [(i, i ^ step) for i in range(size)])
        step *= 2
    return values


def norm_kernel(
    place, lengths, values, gain, shift, cotangent, normed, inverse, hidden, left, right
):
    wide = values[...].astype(jnp.float32)
    centred = wide - jnp.mean(wide, axis=1, keepdims=True)
    spread = jnp.mean(centred * centred, axis=1, keepdims=True)
    scale = lax.rsqrt(spread + EPSILON)
    units = centred * scale
    normed[...] = units
    inverse[...] = jnp.broadcast_to(scale, inverse.shape)
    low = units * gain[...].astype(jnp.float32) + shift[...].astype(jnp.float32)
    hidden[...] = low.astype(jnp.bfloat16)
    alive = -place[0]
    for piece in range(lengths.shape[1] - 1):
        alive = alive + lengths[0, piece]
    rows = lax.broadcasted_iota(jnp.int32, wide.shape, 0)
    grads = jnp.where(rows < alive, cotangent[...].astype(jnp.float32), 0.0).astype(jnp.bfloat16)
    half = wide.shape[1] // 2
    left[...] = grads[:, 0:half]
    right[...] = grads[:, half:]


def norm(place, lengths, values, gain, shift, cotangent):
    shard, features = values.shape
    part = jax.ShapeDtypeStruct((shard, features // 2), jnp.bfloat16)
    return pl.pallas_call(
        norm_kernel,
        in_specs=[IN_SMEM] * 2 + [pl.BlockSpec()] * 4,
        out_shape=[
            jax.ShapeDtypeStruct((shard, features), jnp.float32),
            jax.ShapeDtypeStruct((shard, 128), jnp.float32),
            jax.ShapeDtypeStruct((shard, features), jnp.bfloat16),
            part,
            part,
        ],
        compiler_params=pltpu.CompilerParams(vmem_limit_bytes=ROOM),
        cost_estimate=busy(2),
        name="norm",
    )(place, lengths, values, gain[None], shift[None], cotangent)


def widen(weight, width):
    return jnp.pad(weight, ((0, 0), (0, width - weight.shape[1]), (0, 0)))


def per_device(
    block_input,
    norm_gain,
    norm_bias,
    qkv_weight,
    qkv_bias,
    out_weight,
    gate_weight,
    up_weight,
    down_weight,
    cotangent,
    doc_lengths,
):
    shard, features = block_input.shape
    group = lax.axis_size("tp")
    tokens = shard * group
    width = qkv_weight.shape[1]
    heads = width // HEAD
    padded = max(width, 128)
    me = lax.axis_index("tp")
    segment, position, live = layout(doc_lengths, tokens)
    first = me * shard
    normed, inverse, normed_low, left_mine, right_mine = norm(
        first[None].astype(jnp.int32), doc_lengths, block_input, norm_gain, norm_bias, cotangent
    )
    hidden_in = lax.all_gather(normed_low, "tp", axis=0, tiled=True)
    if group == 8:
        grad_left = gather(left_mine)
        hidden_in = after(hidden_in, grad_left)
    else:
        grad_left = lax.all_gather(after(left_mine, hidden_in), "tp", axis=0, tiled=True)
    grad_right = lax.all_gather(after(right_mine, hidden_in), "tp", axis=0, tiled=True)
    inverse = inverse[:, 0:1]
    live_mine = lax.dynamic_slice_in_dim(live, first, shard)[:, None]
    input_wide = block_input.astype(jnp.float32)
    gain = norm_gain.astype(jnp.float32)
    tables = turns(position)
    seg_col = jnp.broadcast_to(segment[:, None], (tokens, 128))
    seg_row = jnp.broadcast_to(segment[None, :], (8, tokens))

    projection = widen(qkv_weight, padded).reshape(3 * padded, features)
    shift_lines = widen(qkv_bias[..., None], padded).reshape(1, 3 * padded).astype(jnp.float32)
    out_wide = widen(out_weight[None], padded)[0]
    gate, up, mixed, mixed_t = gated_forward(hidden_in, gate_weight, up_weight)
    query, key, value, context, context_t, logsum = attend_forward(
        after(hidden_in, mixed), projection, shift_lines, tables, seg_col, seg_row, heads
    )
    wide_sum = Sum([mixed_t, context_t], [grad_left, grad_right])
    order = wide_sum.send(0)
    order = wide_sum.send(1, order)
    gate_low, gate_low_t, up_low, up_low_t = gated_backward(
        [grad_left, after(grad_right, order)], down_weight, gate, up
    )
    inner_sum = Sum([gate_low_t, up_low_t], [hidden_in], LONG)
    order = inner_sum.send(0)
    order = wide_sum.join(order)
    lines_low, lines_low_t, bias_grad = attend_backward(
        query,
        key,
        value,
        [grad_left, after(grad_right, order)],
        out_wide,
        logsum,
        tables,
        seg_col,
        seg_row,
        heads,
    )
    bias_grad = bias_grad[0].reshape(3, padded)[:, :width]
    outer_sum = Sum([lines_low_t], [hidden_in], LONG)
    term = merge([gate_low, up_low, lines_low], [gate_weight, up_weight, projection])
    order = wide_sum.total(term)
    order = inner_sum.join(order)
    order = wide_sum.share(order)
    order = outer_sum.send(0, order)
    merged = merge([after(context, order), mixed], [out_wide, down_weight])
    old = wide_sum.place_early(merged)
    down_grad, out_grad = wide_sum.place_last(old)
    order = inner_sum.total(down_grad)
    order = outer_sum.join(order)
    order = inner_sum.share(order)
    order = outer_sum.total(order)
    order = outer_sum.share(order)
    normed_grad = lax.psum_scatter(term, "tp", scatter_dimension=0, tiled=True).astype(jnp.float32)
    sums = jnp.concatenate([jnp.sum(normed_grad * normed, axis=0), jnp.sum(normed_grad, axis=0)])
    merged = lax.psum_scatter(merged, "tp", scatter_dimension=0, tiled=True)
    merged = merged.astype(jnp.float32)
    output = (input_wide + jnp.where(live_mine, merged, 0.0)).astype(jnp.bfloat16)
    scaled = normed_grad * gain
    input_grad = inverse * (
        scaled
        - jnp.mean(scaled, axis=1, keepdims=True)
        - normed * jnp.mean(scaled * normed, axis=1, keepdims=True)
    )
    input_grad = input_grad + cotangent.astype(jnp.float32)
    inner_old = inner_sum.place_early(order, output, input_grad)
    outer_old = outer_sum.place_early(inner_old)
    sums = sum_everywhere(after(sums, outer_old), "tp")
    gate_grad, up_grad = inner_sum.place_last(inner_old, sums)
    sums = sum_everywhere(jnp.concatenate([sums, bias_grad.reshape(-1)]), "rows")
    (qkv_grad,) = outer_sum.place_last(outer_old, gate_grad)
    return (
        output,
        input_grad,
        sums[:features],
        sums[features : 2 * features],
        qkv_grad.reshape(3, padded, features)[:, :width],
        sums[2 * features :].reshape(3, width),
        out_grad[:width],
        gate_grad,
        up_grad,
        down_grad,
    )


def solution(mesh):
    placed = (
        P(("rows", "tp"), None),
        P(),
        P(),
        P(None, "tp", None),
        P(None, "tp"),
        P("tp", None),
        P("tp", None),
        P("tp", None),
        P("tp", None),
        P(("rows", "tp"), None),
        P("rows", None),
    )
    return jax.shard_map(
        per_device,
        mesh=mesh,
        in_specs=placed,
        out_specs=(
            P(("rows", "tp"), None),
            P(("rows", "tp"), None),
            P(),
            P(),
            P(None, "tp", None),
            P(None, "tp"),
            P("tp", None),
            P("tp", None),
            P("tp", None),
            P("tp", None),
        ),
        check_vma=False,
    )
```

profile of v0, /device:TPU:0, one launch (start us, length us, event | category | flops | bytes accessed | tf_op | source)
XLA Modules:
  0.0 335.0 jit_solution(12433590196209182583)
XLA Ops:
  11.4 1.8 norm.1
  14.5 5.5 %collective-permute-start = (bf16[128,1024]{1,0:T(8,128)(2,1)S(1)}, bf16[128,1024]{1,0:T(8,128)(2,1)S(1)}, u32[]{:S(2)}, u32[]{:S(2)}) collective-permute-start(bf16[128,1024]{1,0:T(8,128)(2,1)S(1)} %get-tuple-element.103.refs_0_), channel_id=1, source_target_pairs={{0,2},{1,3},{2,0},{3,1},{4,6},{5,7},{6,4},{7,5},{8,10},{9,11},{10,... | collective-permute-start | bytes 786440 | tf_op jit(solution)/shard_map/ppermute | solution.py:462
  20.1 7.9 %collective-permute-done.refs_1_ = bf16[128,1024]{1,0:T(8,128)(2,1)S(1)} collective-permute-done((bf16[128,1024]{1,0:T(8,128)(2,1)S(1)}, bf16[128,1024]{1,0:T(8,128)(2,1)S(1)}, u32[]{:S(2)}, u32[]{:S(2)}) %collective-permute-start) | collective-permute-done | bytes 262176 | tf_op jit(solution)/shard_map/ppermute | solution.py:462
  28.8 3.8 %collective-permute-start.2 = (bf16[128,1024]{1,0:T(8,128)(2,1)S(1)}, bf16[128,1024]{1,0:T(8,128)(2,1)S(1)}, u32[]{:S(2)}, u32[]{:S(2)}) collective-permute-start(bf16[128,1024]{1,0:T(8,128)(2,1)S(1)} %collective-permute-done.1.refs_2_), channel_id=1, source_target_pairs={{0,2},{1,3},{2,0},{3,1},{4,6},{5,7},{6,4},{7,5},{8,10},{9,11},{10,... | collective-permute-start | bytes 786440 | tf_op jit(solution)/shard_map/ppermute | solution.py:462
  32.6 18.7 %collective-permute-start.4 = (bf16[128,1024]{1,0:T(8,128)(2,1)S(1)}, bf16[128,1024]{1,0:T(8,128)(2,1)S(1)}, u32[]{:S(2)}, u32[]{:S(2)}) collective-permute-start(bf16[128,1024]{1,0:T(8,128)(2,1)S(1)} %collective-permute-done.3.refs_4_), channel_id=1, source_target_pairs={{0,2},{1,3},{2,0},{3,1},{4,6},{5,7},{6,4},{7,5},{8,10},{9,11},{10,... | collective-permute-start | bytes 786440 | tf_op jit(solution)/shard_map/ppermute | solution.py:462
  52.4 18.0 %collective-permute-done.4.refs_5_ = bf16[128,1024]{1,0:T(8,128)(2,1)S(1)} collective-permute-done((bf16[128,1024]{1,0:T(8,128)(2,1)S(1)}, bf16[128,1024]{1,0:T(8,128)(2,1)S(1)}, u32[]{:S(2)}, u32[]{:S(2)}) %collective-permute-start.4) | collective-permute-done | bytes 262176 | tf_op jit(solution)/shard_map/ppermute | solution.py:462
  75.4 2.0 fusion.9
  78.0 1.8 copy-done.18
  79.9 1.9 copy-done.20
  81.7 7.6 %gated_forward.1 = (f32[704,1024]{1,0:T(8,128)S(1)}, f32[704,1024]{1,0:T(8,128)S(1)}, bf16[1024,704]{1,0:T(8,128)(2,1)S(1)}, bf16[704,1024]{1,0:T(8,128)(2,1)S(1)}) custom-call(bf16[1024,2048]{1,0:T(8,128)(2,1)S(1)} %copy-done.12, bf16[704,2048]{1,0:T(8,128)(2,1)S(1)} %copy-done.18, bf16[704,2048]{1,0:T(8,128)(2,1)S(1)} %copy-done.20), custom_call_target="tpu_custom_call" | custom-call | flops 11249999872 | tf_op jit(solution)/shard_map/gated_forward/pallas_call | solution.py:280
  92.8 8.6 %attend_forward.1 = (bf16[1024,256]{1,0:T(8,128)(2,1)S(1)}, bf16[1024,256]{1,0:T(8,128)(2,1)S(1)}, bf16[1024,256]{1,0:T(8,128)(2,1)S(1)}, bf16[1024,256]{1,0:T(8...) custom-call(bf16[1024,2048]{1,0:T(8,128)(2,1)S(1)} %copy-done.12, bf16[768,2048]{1,0:T(8,128)(2,1)S(1)} %bitcast.55, ...), custom_call_target="tpu_custom_call" | custom-call | flops 12750000128 | tf_op jit(solution)/shard_map/attend_forward/pallas_call | solution.py:125
  101.4 2.6 send_terms.4
  116.8 5.6 %gated_backward.1 = (bf16[1024,704]{1,0:T(8,128)(2,1)S(1)}, bf16[704,1024]{1,0:T(8,128)(2,1)S(1)}, bf16[1024,704]{1,0:T(8,128)(2,1)S(1)}, bf16[704,1024]{1,0:T(8,128)(2,1)S(1)}) custom-call(bf16[1024,1024]{1,0:T(8,128)(2,1)S(1)} %bitcast.59, bf16[1024,1024]{1,0:T(8,128)(2,1)S(1)} %copy-done.25, bf16[704,2048]{1,0:T(8,128)(2,1)S(1)} %copy-done.22, ...), custom_call_target="tpu_custom_call" | custom-call | flops 8099999744 | tf_op jit(solution)/shard_map/gated_backward/pallas_call | solution.py:321
  122.4 5.2 %send_terms.6 = (bf16[1408,512]{1,0:T(8,128)(2,1)}, bf16[1408,512]{1,0:T(8,128)(2,1)}) custom-call(s32[2]{0:T(128)S(1)} %pad_add_fusion.2.order, bf16[704,1024]{1,0:T(8,128)(2,1)S(1)} %get-tuple-element.140.refs_0_, bf16[704,1024]{1,0:T(8,128)(2,1)S(1)} %get-tuple-element.124.refs_1_, bf16[1024,2048]{1,0:T(8,128)(2,1)S(1)} %copy-done.13), custom_call_target="tpu_custom_call" | custom-call | flops 8249999872 | tf_op jit(solution)/shard_map/send_terms/pallas_call | solution.py:520
  129.6 4.4 %join_terms.3 = (bf16[960,256]{1,0:T(8,128)(2,1)}, bf16[960,256]{1,0:T(8,128)(2,1)S(1)}, bf16[960,256]{1,0:T(8,128)(2,1)}, bf16[960,256]{1,0:T(8,128)(2,1)S(1)}) custom-call(s32[3,2]{1,0:T(4,128)S(1)} %pad_add_fusion.order, bf16[704,1024]{1,0:T(8,128)(2,1)S(1)} %copy-done.36, bf16[256,1024]{1,0:T(8,128)(2,1)S(1)} %copy-done.41, ...), custom_call_target="tpu_custom_call" | custom-call | flops 5624999936 | tf_op jit(solution)/shard_map/join_terms/pallas_call | solution.py:536
  137.7 13.2 %attend_backward.1 = (bf16[1024,768]{1,0:T(8,128)(2,1)S(1)}, bf16[768,1024]{1,0:T(8,128)(2,1)S(1)}, f32[8,768]{1,0:T(8,128)S(1)}) custom-call(bf16[1024,256]{1,0:T(8,128)(2,1)S(1)} %copy-done.55, bf16[1024,256]{1,0:T(8,128)(2,1)S(1)} %copy-done.57, bf16[1024,256]{1,0:T(8,128)(2,1)S(1)} %copy-done.59, bf16[1024,1024]{1,0:T(8,128)(2,1)S(1)} %bitcast.61, ...), custom_call_target="tpu_custom_call" | custom-call | flops 19950000128 | tf_op jit(solution)/shard_map/attend_backward/pallas_call | solution.py:214
  152.1 10.4 %merge.2 = bf16[1024,2048]{1,0:T(8,128)(2,1)S(1)} custom-call(bf16[1024,704]{1,0:T(8,128)(2,1)S(1)} %get-tuple-element.135.refs_0_, bf16[1024,704]{1,0:T(8,128)(2,1)S(1)} %get-tuple-element.136.refs_1_, bf16[1024,768]{1,0:T(8,128)(2,1)S(1)} %get-tuple-element.137.refs_2_, bf16[704,2048]{1,0:T(8,128)(2,1)S(1)} %copy-done.19, ...), custom_call_target="tpu_custom_call" | custom-call | flops 12000000000 | tf_op jit(solution)/shard_map/merge/pallas_call | solution.py:343
  162.5 2.0 copy-done
  164.6 7.2 %collective-permute-done.15 = bf16[960,256]{1,0:T(8,128)(2,1)} collective-permute-done((bf16[960,256]{1,0:T(8,128)(2,1)}, bf16[960,256]{1,0:T(8,128)(2,1)}, u32[]{:S(2)}, u32[]{:S(2)}) %collective-permute-start.15) | collective-permute-done | bytes 491552 | tf_op jit(solution)/shard_map/ppermute | solution.py:546
  171.8 1.9 add.194.refs_0_
  174.6 2.0 add.195.refs_1_
  177.8 2.2 copy-done.14
  181.4 6.0 %join_terms.4 = (bf16[1408,256]{1,0:T(8,128)(2,1)}, bf16[1408,256]{1,0:T(8,128)(2,1)S(1)}, bf16[1408,256]{1,0:T(8,128)(2,1)}, bf16[1408,256]{1,0:T(8,128)(2,1)S(1)}) custom-call(s32[2,2]{1,0:T(2,128)S(1)} %pad_add_fusion.1.order, bf16[704,1024]{1,0:T(8,128)(2,1)S(1)} %copy-done.47, bf16[704,1024]{1,0:T(8,128)(2,1)S(1)} %copy-done.49, ...), custom_call_target="tpu_custom_call" | custom-call | flops 1500000026624 | tf_op jit(solution)/shard_map/join_terms/pallas_call | solution.py:536
  189.4 1.8 constant_dynamic-update-slice_fusion.1
  191.3 2.0 constant_dynamic-update-slice_fusion.3
  193.2 1.8 constant_dynamic-update-slice_fusion.2
  196.0 1.8 constant_dynamic-update-slice_fusion
  199.0 2.8 send_terms.7
  202.8 5.3 %merge.3 = bf16[1024,2048]{1,0:T(8,128)(2,1)S(1)} custom-call(bf16[1024,256]{1,0:T(8,128)(2,1)S(1)} %copy-done.53, bf16[1024,704]{1,0:T(8,128)(2,1)S(1)} %copy-done.51, bf16[256,2048]{1,0:T(8,128)(2,1)S(1)} %copy-done.27, bf16[704,2048]{1,0:T(8,128)(2,1)S(1)} %copy-done.23), custom_call_target="tpu_custom_call" | custom-call | flops 12000000000 | tf_op jit(solution)/shard_map/merge/pallas_call | solution.py:343
  208.1 2.0 copy-done.1
  210.1 14.7 %collective-permute-done.22.refs_1_ = bf16[1920,256]{1,0:T(8,128)(2,1)} collective-permute-done((bf16[1920,256]{1,0:T(8,128)(2,1)}, bf16[1920,256]{1,0:T(8,128)(2,1)}, u32[]{:S(2)}, u32[]{:S(2)}) %collective-permute-start.22) | collective-permute-done | bytes 983072 | tf_op jit(solution)/shard_map/ppermute | solution.py:558
  226.3 5.6 %place.6 = (f32[704,2048]{1,0:T(8,128)}, f32[256,2048]{1,0:T(8,128)}) custom-call(s32[8]{0:T(128)S(1)} %stack.165.order, bf16[960,256]{1,0:T(8,128)(2,1)} %add.194.refs_0_, bf16[960,256]{1,0:T(8,128)(2,1)} %add.195.refs_1_, bf16[960,256]{1,0:T(8,128)(2,1)} %collective-permute-done.19.refs_2_, bf16[960,256]{1,0:T(8,128)(2,1)} %collective-permute-done.20.refs_3_), custom_call_target="tpu_custom_call" | custom-call | flops 4915200000 | tf_op jit(solution)/shard_map/place/pallas_call | solution.py:414
  231.8 5.6 %place.7 = (f32[704,2048]{1,0:T(8,128)}, f32[256,2048]{1,0:T(8,128)}) custom-call(s32[8]{0:T(128)S(1)} %stack.160.order, bf16[1920,256]{1,0:T(8,128)(2,1)} %collective-permute-done.21.refs_0_, bf16[1920,256]{1,0:T(8,128)(2,1)} %collective-permute-done.22.refs_1_, ...), custom_call_target="tpu_custom_call", output_to_operand_aliasing={{0}: (3, {}), {1}: (4, {})} | custom-call | flops 4915200000 | tf_op jit(solution)/shard_map/place/pallas_call | solution.py:414
  237.4 2.3 add.217.refs_1_
  240.2 2.2 add.216.refs_0_
  242.9 3.3 collective-permute-done.25.refs_2_
  246.2 3.0 join_terms.5
  253.1 8.1 %collective-permute-done.27.refs_2_ = bf16[1408,256]{1,0:T(8,128)(2,1)} collective-permute-done((bf16[1408,256]{1,0:T(8,128)(2,1)}, bf16[1408,256]{1,0:T(8,128)(2,1)}, u32[]{:S(2)}, u32[]{:S(2)}) %collective-permute-start.27) | collective-permute-done | bytes 720928 | tf_op jit(solution)/shard_map/ppermute | solution.py:552
  272.1 6.6 %collective-permute-done.31.refs_2_ = bf16[768,256]{1,0:T(8,128)(2,1)S(1)} collective-permute-done((bf16[768,256]{1,0:T(8,128)(2,1)S(1)}, bf16[768,256]{1,0:T(8,128)(2,1)S(1)}, u32[]{:S(2)}, u32[]{:S(2)}) %collective-permute-start.31) | collective-permute-done | bytes 393248 | tf_op jit(solution)/shard_map/ppermute | solution.py:552
  283.9 2.1 add_convert_fusion
  285.9 5.2 %place.8 = (f32[704,2048]{1,0:T(8,128)}, f32[704,2048]{1,0:T(8,128)}) custom-call(s32[4]{0:T(128)S(1)} %pad_add_fusion.4.order, bf16[1408,256]{1,0:T(8,128)(2,1)} %add.216.refs_0_, bf16[1408,256]{1,0:T(8,128)(2,1)} %add.217.refs_1_, bf16[1408,256]{1,0:T(8,128)(2,1)} %collective-permute-done.27.refs_2_, bf16[1408,256]{1,0:T(8,128)(2,1)} %collective-permute-done.28.refs_3_), custom_call_target="tpu_custom_call" | custom-call | flops 7208960000 | tf_op jit(solution)/shard_map/place/pallas_call | solution.py:414
  291.1 2.7 place.9.refs_2_
  296.1 2.7 collective-permute-done.34
  303.4 3.8 %collective-permute-done.41.refs_1_ = bf16[2816,256]{1,0:T(8,128)(2,1)} collective-permute-done((bf16[2816,256]{1,0:T(8,128)(2,1)}, bf16[2816,256]{1,0:T(8,128)(2,1)}, u32[]{:S(2)}, u32[]{:S(2)}) %collective-permute-start.41) | collective-permute-done | bytes 1441824 | tf_op jit(solution)/shard_map/ppermute | solution.py:558
  307.3 2.0 collective-permute-done.40.refs_0_
  309.5 5.2 %place.10 = (f32[704,2048]{1,0:T(8,128)}, f32[704,2048]{1,0:T(8,128)}) custom-call(s32[4]{0:T(128)S(1)} %pad_add_fusion.5.order, bf16[2816,256]{1,0:T(8,128)(2,1)} %collective-permute-done.40.refs_0_, bf16[2816,256]{1,0:T(8,128)(2,1)} %collective-permute-done.41.refs_1_, ...), custom_call_target="tpu_custom_call", output_to_operand_aliasing={{0}: (3, {}), {1}: (4, {})} | custom-call | flops 7208960000 | tf_op jit(solution)/shard_map/place/pallas_call | solution.py:414
  314.7 6.8 %collective-permute-done.39.refs_1_ = bf16[1536,256]{1,0:T(8,128)(2,1)S(1)} collective-permute-done((bf16[1536,256]{1,0:T(8,128)(2,1)}, bf16[1536,256]{1,0:T(8,128)(2,1)S(1)}, u32[]{:S(2)}, u32[]{:S(2)}) %collective-permute-start.39) | collective-permute-done | bytes 786464 | tf_op jit(solution)/shard_map/ppermute | solution.py:558
  323.7 2.7 place.11
  (274 shorter events, 77.6 us)
Async XLA Ops:
  7.2 68.0 %all-gather.3.cloned.1.call-start = ((), (), s32[]{:S(2)}) async-start(), calls=%async_computation.2 | async-start | bytes 4718592 | tf_op jit(solution)/shard_map/all_gather | solution.py:662
  11.4 40.0 %copy-start.68 = (bf16[3,256]{1,0:T(4,128)(2,1)S(1)}, bf16[3,256]{1,0:T(4,128)(2,1)}, u32[]{:S(2)}) copy-start(bf16[3,256]{1,0:T(4,128)(2,1)} %param.15) | copy-start | bytes 4612
  11.4 59.1 %copy-start.30 = (s32[1,8]{1,0:T(1,128)S(1)}, s32[1,8]{1,0:T(1,128)}, u32[]{:S(2)}) copy-start(s32[1,8]{1,0:T(1,128)} %lengths.1) | copy-start | bytes 100
  13.2 93.8 %all-gather.5.cloned.1.call-start = ((), (), s32[]{:S(2)}) async-start(), calls=%async_computation.3 | async-start | bytes 2359296 | tf_op jit(solution)/shard_map/all_gather | solution.py:668
  13.3 38.6 %collective-permute-start.5 = (bf16[128,1024]{1,0:T(8,128)(2,1)S(1)}, bf16[128,1024]{1,0:T(8,128)(2,1)S(1)}, u32[]{:S(2)}, u32[]{:S(2)}) collective-permute-start(bf16[128,1024]{1,0:T(8,128)(2,1)S(1)} %get-tuple-element.103.refs_0_), channel_id=1, source_target_pairs={{0,1},{1,0},{2,3},{3,2},{4,5},{5,4},{6,7},{7,6},{8,9},{9,8},{10,11... | collective-permute-start | bytes 786440 | tf_op jit(solution)/shard_map/ppermute | solution.py:462
  13.8 15.0 %collective-permute-start.1 = (bf16[128,1024]{1,0:T(8,128)(2,1)S(1)}, bf16[128,1024]{1,0:T(8,128)(2,1)S(1)}, u32[]{:S(2)}, u32[]{:S(2)}) collective-permute-start(bf16[128,1024]{1,0:T(8,128)(2,1)S(1)} %get-tuple-element.103.refs_0_), channel_id=1, source_target_pairs={{0,0},{1,1},{2,4},{3,5},{4,2},{5,3},{6,6},{7,7},{8,8},{9,9},{10,12... | collective-permute-start | bytes 786440 | tf_op jit(solution)/shard_map/ppermute | solution.py:462
  14.5 13.6 %collective-permute-start = (bf16[128,1024]{1,0:T(8,128)(2,1)S(1)}, bf16[128,1024]{1,0:T(8,128)(2,1)S(1)}, u32[]{:S(2)}, u32[]{:S(2)}) collective-permute-start(bf16[128,1024]{1,0:T(8,128)(2,1)S(1)} %get-tuple-element.103.refs_0_), channel_id=1, source_target_pairs={{0,2},{1,3},{2,0},{3,1},{4,6},{5,7},{6,4},{7,5},{8,10},{9,11},{10,... | collective-permute-start | bytes 786440 | tf_op jit(solution)/shard_map/ppermute | solution.py:462
  28.0 4.6 %collective-permute-start.3 = (bf16[128,1024]{1,0:T(8,128)(2,1)S(1)}, bf16[128,1024]{1,0:T(8,128)(2,1)S(1)}, u32[]{:S(2)}, u32[]{:S(2)}) collective-permute-start(bf16[128,1024]{1,0:T(8,128)(2,1)S(1)} %collective-permute-done.refs_1_), channel_id=1, source_target_pairs={{0,0},{1,1},{2,4},{3,5},{4,2},{5,3},{6,6},{7,7},{8,8},{9,9},{10,12... | collective-permute-start | bytes 786440 | tf_op jit(solution)/shard_map/ppermute | solution.py:462
  28.8 23.2 %collective-permute-start.2 = (bf16[128,1024]{1,0:T(8,128)(2,1)S(1)}, bf16[128,1024]{1,0:T(8,128)(2,1)S(1)}, u32[]{:S(2)}, u32[]{:S(2)}) collective-permute-start(bf16[128,1024]{1,0:T(8,128)(2,1)S(1)} %collective-permute-done.1.refs_2_), channel_id=1, source_target_pairs={{0,2},{1,3},{2,0},{3,1},{4,6},{5,7},{6,4},{7,5},{8,10},{9,11},{10,... | collective-permute-start | bytes 786440 | tf_op jit(solution)/shard_map/ppermute | solution.py:462
  32.6 37.8 %collective-permute-start.4 = (bf16[128,1024]{1,0:T(8,128)(2,1)S(1)}, bf16[128,1024]{1,0:T(8,128)(2,1)S(1)}, u32[]{:S(2)}, u32[]{:S(2)}) collective-permute-start(bf16[128,1024]{1,0:T(8,128)(2,1)S(1)} %collective-permute-done.3.refs_4_), channel_id=1, source_target_pairs={{0,2},{1,3},{2,0},{3,1},{4,6},{5,7},{6,4},{7,5},{8,10},{9,11},{10,... | collective-permute-start | bytes 786440 | tf_op jit(solution)/shard_map/ppermute | solution.py:462
  51.4 19.7 %collective-permute-start.7 = (bf16[128,1024]{1,0:T(8,128)(2,1)S(1)}, bf16[128,1024]{1,0:T(8,128)(2,1)S(1)}, u32[]{:S(2)}, u32[]{:S(2)}) collective-permute-start(bf16[128,1024]{1,0:T(8,128)(2,1)S(1)} %collective-permute-done.1.refs_2_), channel_id=1, source_target_pairs={{0,1},{1,0},{2,3},{3,2},{4,5},{5,4},{6,7},{7,6},{8,9},{9,8},{10,11... | collective-permute-start | bytes 786440 | tf_op jit(solution)/shard_map/ppermute | solution.py:462
  51.4 19.7 %collective-permute-start.6 = (bf16[128,1024]{1,0:T(8,128)(2,1)S(1)}, bf16[128,1024]{1,0:T(8,128)(2,1)}, u32[]{:S(2)}, u32[]{:S(2)}) collective-permute-start(bf16[128,1024]{1,0:T(8,128)(2,1)S(1)} %collective-permute-done.refs_1_), channel_id=1, source_target_pairs={{0,1},{1,0},{2,3},{3,2},{4,5},{5,4},{6,7},{7,6},{8,9},{9,8},{10,11... | collective-permute-start | bytes 786440 | tf_op jit(solution)/shard_map/ppermute | solution.py:462
  51.9 19.2 %collective-permute-start.9 = (bf16[128,1024]{1,0:T(8,128)(2,1)S(1)}, bf16[128,1024]{1,0:T(8,128)(2,1)}, u32[]{:S(2)}, u32[]{:S(2)}) collective-permute-start(bf16[128,1024]{1,0:T(8,128)(2,1)S(1)} %collective-permute-done.3.refs_4_), channel_id=1, source_target_pairs={{0,1},{1,0},{2,3},{3,2},{4,5},{5,4},{6,7},{7,6},{8,9},{9,8},{10,11... | collective-permute-start | bytes 786440 | tf_op jit(solution)/shard_map/ppermute | solution.py:462
  52.0 19.1 %collective-permute-start.8 = (bf16[128,1024]{1,0:T(8,128)(2,1)S(1)}, bf16[128,1024]{1,0:T(8,128)(2,1)}, u32[]{:S(2)}, u32[]{:S(2)}) collective-permute-start(bf16[128,1024]{1,0:T(8,128)(2,1)S(1)} %collective-permute-done.2.refs_3_), channel_id=1, source_target_pairs={{0,1},{1,0},{2,3},{3,2},{4,5},{5,4},{6,7},{7,6},{8,9},{9,8},{10,11... | collective-permute-start | bytes 786440 | tf_op jit(solution)/shard_map/ppermute | solution.py:462
  70.4 1.7 collective-permute-start.10
  75.2 205.8 %reduce-scatter.5.cloned.1.call-start = ((), (), s32[]{:S(2)}) async-start(), calls=%async_computation.5 | async-start | bytes 4718592 | tf_op jit(solution)/shard_map/reduce_scatter | solution.py:720
  104.0 24.1 %collective-permute-start.11 = (bf16[960,256]{1,0:T(8,128)(2,1)}, bf16[960,256]{1,0:T(8,128)(2,1)}, u32[]{:S(2)}, u32[]{:S(2)}) collective-permute-start(bf16[960,256]{1,0:T(8,128)(2,1)} %get-tuple-element.115), channel_id=1, source_target_pairs={{0,8},{8,0},{16,24},{24,16},{1,9},{9,1},{17,25},{25,17},{2,10},{10... | collective-permute-start | bytes 1474568 | tf_op jit(solution)/shard_map/ppermute | solution.py:528
  105.5 24.1 %collective-permute-start.12 = (bf16[960,256]{1,0:T(8,128)(2,1)}, bf16[960,256]{1,0:T(8,128)(2,1)}, u32[]{:S(2)}, u32[]{:S(2)}) collective-permute-start(bf16[960,256]{1,0:T(8,128)(2,1)} %get-tuple-element.116), channel_id=1, source_target_pairs={{0,16},{16,0},{8,24},{24,8},{1,17},{17,1},{9,25},{25,9},{2,18},{18... | collective-permute-start | bytes 1474568 | tf_op jit(solution)/shard_map/ppermute | solution.py:528
  112.8 16.8 %collective-permute-start.13 = (bf16[960,256]{1,0:T(8,128)(2,1)S(1)}, bf16[960,256]{1,0:T(8,128)(2,1)S(1)}, u32[]{:S(2)}, u32[]{:S(2)}) collective-permute-start(bf16[960,256]{1,0:T(8,128)(2,1)S(1)} %get-tuple-element.118), channel_id=1, source_target_pairs={{0,8},{8,0},{16,24},{24,16},{1,9},{9,1},{17,25},{25,17},{2,10},{10... | collective-permute-start | bytes 1474568 | tf_op jit(solution)/shard_map/ppermute | solution.py:528
  113.4 16.2 %collective-permute-start.14 = (bf16[960,256]{1,0:T(8,128)(2,1)S(1)}, bf16[960,256]{1,0:T(8,128)(2,1)S(1)}, u32[]{:S(2)}, u32[]{:S(2)}) collective-permute-start(bf16[960,256]{1,0:T(8,128)(2,1)S(1)} %get-tuple-element.119), channel_id=1, source_target_pairs={{0,16},{16,0},{8,24},{24,8},{1,17},{17,1},{9,25},{25,9},{2,18},{18... | collective-permute-start | bytes 1474568 | tf_op jit(solution)/shard_map/ppermute | solution.py:528
  127.5 50.2 %collective-permute-start.17 = (bf16[1408,512]{1,0:T(8,128)(2,1)}, bf16[1408,512]{1,0:T(8,128)(2,1)}, u32[]{:S(2)}, u32[]{:S(2)}) collective-permute-start(bf16[1408,512]{1,0:T(8,128)(2,1)} %get-tuple-element.125), channel_id=1, source_target_pairs={{0,8},{8,0},{16,24},{24,16},{1,9},{9,1},{17,25},{25,17},{2,10},{10... | collective-permute-start | bytes 4325384 | tf_op jit(solution)/shard_map/ppermute | solution.py:528
  128.1 49.6 %collective-permute-start.18 = (bf16[1408,512]{1,0:T(8,128)(2,1)}, bf16[1408,512]{1,0:T(8,128)(2,1)}, u32[]{:S(2)}, u32[]{:S(2)}) collective-permute-start(bf16[1408,512]{1,0:T(8,128)(2,1)} %get-tuple-element.126), channel_id=1, source_target_pairs={{0,16},{16,0},{8,24},{24,8},{1,17},{17,1},{9,25},{25,9},{2,18},{18... | collective-permute-start | bytes 4325384 | tf_op jit(solution)/shard_map/ppermute | solution.py:528
  135.6 36.2 %collective-permute-start.15 = (bf16[960,256]{1,0:T(8,128)(2,1)}, bf16[960,256]{1,0:T(8,128)(2,1)}, u32[]{:S(2)}, u32[]{:S(2)}) collective-permute-start(bf16[960,256]{1,0:T(8,128)(2,1)} %get-tuple-element.128), channel_id=1, source_target_pairs={{0,16},{16,0},{8,24},{24,8},{1,17},{17,1},{9,25},{25,9},{2,18},{18... | collective-permute-start | bytes 1474568 | tf_op jit(solution)/shard_map/ppermute | solution.py:546
  136.7 37.9 %collective-permute-start.16 = (bf16[960,256]{1,0:T(8,128)(2,1)}, bf16[960,256]{1,0:T(8,128)(2,1)}, u32[]{:S(2)}, u32[]{:S(2)}) collective-permute-start(bf16[960,256]{1,0:T(8,128)(2,1)} %get-tuple-element.130), channel_id=1, source_target_pairs={{0,8},{8,0},{16,24},{24,16},{1,9},{9,1},{17,25},{25,17},{2,10},{10... | collective-permute-start | bytes 1474568 | tf_op jit(solution)/shard_map/ppermute | solution.py:546
  164.6 119.3 %reduce-scatter.3.cloned.1.call-start = ((), (), s32[]{:S(2)}) async-start(), calls=%async_computation.4 | async-start | bytes 4718592 | tf_op jit(solution)/shard_map/reduce_scatter | solution.py:722
  173.7 22.2 %collective-permute-start.19 = (bf16[960,256]{1,0:T(8,128)(2,1)}, bf16[960,256]{1,0:T(8,128)(2,1)}, u32[]{:S(2)}, u32[]{:S(2)}) collective-permute-start(bf16[960,256]{1,0:T(8,128)(2,1)} %add.194.refs_0_), channel_id=1, source_target_pairs={{0,16},{16,0},{8,24},{24,8},{1,17},{17,1},{9,25},{25,9},{2,18},{18... | collective-permute-start | bytes 1474568 | tf_op jit(solution)/shard_map/ppermute | solution.py:552
  176.6 16.7 %collective-permute-start.20 = (bf16[960,256]{1,0:T(8,128)(2,1)}, bf16[960,256]{1,0:T(8,128)(2,1)}, u32[]{:S(2)}, u32[]{:S(2)}) collective-permute-start(bf16[960,256]{1,0:T(8,128)(2,1)} %add.195.refs_1_), channel_id=1, source_target_pairs={{0,8},{8,0},{16,24},{24,16},{1,9},{9,1},{17,25},{25,17},{2,10},{10... | collective-permute-start | bytes 1474568 | tf_op jit(solution)/shard_map/ppermute | solution.py:552
  187.4 52.8 %collective-permute-start.23 = (bf16[1408,256]{1,0:T(8,128)(2,1)}, bf16[1408,256]{1,0:T(8,128)(2,1)}, u32[]{:S(2)}, u32[]{:S(2)}) collective-permute-start(bf16[1408,256]{1,0:T(8,128)(2,1)} %get-tuple-element.141), channel_id=1, source_target_pairs={{0,16},{16,0},{8,24},{24,8},{1,17},{17,1},{9,25},{25,9},{2,18},{18... | collective-permute-start | bytes 2162696 | tf_op jit(solution)/shard_map/ppermute | solution.py:546
  188.9 48.5 %collective-permute-start.24 = (bf16[1408,256]{1,0:T(8,128)(2,1)}, bf16[1408,256]{1,0:T(8,128)(2,1)}, u32[]{:S(2)}, u32[]{:S(2)}) collective-permute-start(bf16[1408,256]{1,0:T(8,128)(2,1)} %get-tuple-element.143), channel_id=1, source_target_pairs={{0,8},{8,0},{16,24},{24,16},{1,9},{9,1},{17,25},{25,17},{2,10},{10... | collective-permute-start | bytes 2162696 | tf_op jit(solution)/shard_map/ppermute | solution.py:546
  195.1 29.7 %collective-permute-start.22 = (bf16[1920,256]{1,0:T(8,128)(2,1)}, bf16[1920,256]{1,0:T(8,128)(2,1)}, u32[]{:S(2)}, u32[]{:S(2)}) collective-permute-start(bf16[1920,256]{1,0:T(8,128)(2,1)} %constant_dynamic-update-slice_fusion.2), channel_id=1, source_target_pairs={{0,16},{16,0},{8,24},{24,8},{1,17},{17,1},{9,25},{25,9},{2,18},{18... | collective-permute-start | bytes 2949128 | tf_op jit(solution)/shard_map/ppermute | solution.py:558
  197.8 34.0 %collective-permute-start.21 = (bf16[1920,256]{1,0:T(8,128)(2,1)}, bf16[1920,256]{1,0:T(8,128)(2,1)}, u32[]{:S(2)}, u32[]{:S(2)}) collective-permute-start(bf16[1920,256]{1,0:T(8,128)(2,1)} %constant_dynamic-update-slice_fusion), channel_id=1, source_target_pairs={{0,8},{8,0},{16,24},{24,16},{1,9},{9,1},{17,25},{25,17},{2,10},{10... | collective-permute-start | bytes 2949128 | tf_op jit(solution)/shard_map/ppermute | solution.py:558
  201.9 44.3 %collective-permute-start.25 = (bf16[768,512]{1,0:T(8,128)(2,1)}, bf16[768,512]{1,0:T(8,128)(2,1)}, u32[]{:S(2)}, u32[]{:S(2)}) collective-permute-start(bf16[768,512]{1,0:T(8,128)(2,1)} %get-tuple-element.148), channel_id=1, source_target_pairs={{0,8},{8,0},{16,24},{24,16},{1,9},{9,1},{17,25},{25,17},{2,10},{10... | collective-permute-start | bytes 2359304 | tf_op jit(solution)/shard_map/ppermute | solution.py:528
  224.8 21.4 %collective-permute-start.26 = (bf16[768,512]{1,0:T(8,128)(2,1)}, bf16[768,512]{1,0:T(8,128)(2,1)S(1)}, u32[]{:S(2)}, u32[]{:S(2)}) collective-permute-start(bf16[768,512]{1,0:T(8,128)(2,1)} %copy-done.28), channel_id=1, source_target_pairs={{0,16},{16,0},{8,24},{24,8},{1,17},{17,1},{9,25},{25,9},{2,18},{18... | collective-permute-start | bytes 2359304 | tf_op jit(solution)/shard_map/ppermute | solution.py:528
  239.7 22.7 %collective-permute-start.28 = (bf16[1408,256]{1,0:T(8,128)(2,1)}, bf16[1408,256]{1,0:T(8,128)(2,1)}, u32[]{:S(2)}, u32[]{:S(2)}) collective-permute-start(bf16[1408,256]{1,0:T(8,128)(2,1)} %add.217.refs_1_), channel_id=1, source_target_pairs={{0,8},{8,0},{16,24},{24,16},{1,9},{9,1},{17,25},{25,17},{2,10},{10... | collective-permute-start | bytes 2162696 | tf_op jit(solution)/shard_map/ppermute | solution.py:552
  242.4 18.8 %collective-permute-start.27 = (bf16[1408,256]{1,0:T(8,128)(2,1)}, bf16[1408,256]{1,0:T(8,128)(2,1)}, u32[]{:S(2)}, u32[]{:S(2)}) collective-permute-start(bf16[1408,256]{1,0:T(8,128)(2,1)} %add.216.refs_0_), channel_id=1, source_target_pairs={{0,16},{16,0},{8,24},{24,8},{1,17},{17,1},{9,25},{25,9},{2,18},{18... | collective-permute-start | bytes 2162696 | tf_op jit(solution)/shard_map/ppermute | solution.py:552
  249.2 17.3 %collective-permute-start.29 = (bf16[768,256]{1,0:T(8,128)(2,1)S(1)}, bf16[768,256]{1,0:T(8,128)(2,1)S(1)}, u32[]{:S(2)}, u32[]{:S(2)}) collective-permute-start(bf16[768,256]{1,0:T(8,128)(2,1)S(1)} %get-tuple-element.167), channel_id=1, source_target_pairs={{0,16},{16,0},{8,24},{24,8},{1,17},{17,1},{9,25},{25,9},{2,18},{18... | collective-permute-start | bytes 1179656 | tf_op jit(solution)/shard_map/ppermute | solution.py:546
  249.9 18.0 %collective-permute-start.30 = (bf16[768,256]{1,0:T(8,128)(2,1)S(1)}, bf16[768,256]{1,0:T(8,128)(2,1)S(1)}, u32[]{:S(2)}, u32[]{:S(2)}) collective-permute-start(bf16[768,256]{1,0:T(8,128)(2,1)S(1)} %get-tuple-element.168), channel_id=1, source_target_pairs={{0,8},{8,0},{16,24},{24,16},{1,9},{9,1},{17,25},{25,17},{2,10},{10... | collective-permute-start | bytes 1179656 | tf_op jit(solution)/shard_map/ppermute | solution.py:546
  266.7 12.1 %collective-permute-start.31 = (bf16[768,256]{1,0:T(8,128)(2,1)S(1)}, bf16[768,256]{1,0:T(8,128)(2,1)S(1)}, u32[]{:S(2)}, u32[]{:S(2)}) collective-permute-start(bf16[768,256]{1,0:T(8,128)(2,1)S(1)} %add.218.refs_0_), channel_id=1, source_target_pairs={{0,16},{16,0},{8,24},{24,8},{1,17},{17,1},{9,25},{25,9},{2,18},{18... | collective-permute-start | bytes 1179656 | tf_op jit(solution)/shard_map/ppermute | solution.py:552
  268.0 12.1 %collective-permute-start.32 = (bf16[768,256]{1,0:T(8,128)(2,1)S(1)}, bf16[768,256]{1,0:T(8,128)(2,1)S(1)}, u32[]{:S(2)}, u32[]{:S(2)}) collective-permute-start(bf16[768,256]{1,0:T(8,128)(2,1)S(1)} %add.219.refs_1_), channel_id=1, source_target_pairs={{0,8},{8,0},{16,24},{24,16},{1,9},{9,1},{17,25},{25,17},{2,10},{10... | collective-permute-start | bytes 1179656 | tf_op jit(solution)/shard_map/ppermute | solution.py:552
  269.8 37.4 %collective-permute-start.41 = (bf16[2816,256]{1,0:T(8,128)(2,1)}, bf16[2816,256]{1,0:T(8,128)(2,1)}, u32[]{:S(2)}, u32[]{:S(2)}) collective-permute-start(bf16[2816,256]{1,0:T(8,128)(2,1)} %copy-done.63), channel_id=1, source_target_pairs={{0,16},{16,0},{8,24},{24,8},{1,17},{17,1},{9,25},{25,9},{2,18},{18... | collective-permute-start | bytes 4325384 | tf_op jit(solution)/shard_map/ppermute | solution.py:558
  271.3 38.0 %collective-permute-start.40 = (bf16[2816,256]{1,0:T(8,128)(2,1)}, bf16[2816,256]{1,0:T(8,128)(2,1)}, u32[]{:S(2)}, u32[]{:S(2)}) collective-permute-start(bf16[2816,256]{1,0:T(8,128)(2,1)} %copy-done.64), channel_id=1, source_target_pairs={{0,8},{8,0},{16,24},{24,16},{1,9},{9,1},{17,25},{25,17},{2,10},{10... | collective-permute-start | bytes 4325384 | tf_op jit(solution)/shard_map/ppermute | solution.py:558
  293.9 1.2 collective-permute-start.33
  295.0 3.7 %collective-permute-start.34 = (f32[4096]{0:T(1024)S(1)}, f32[4096]{0:T(1024)S(1)}, u32[]{:S(2)}, u32[]{:S(2)}) collective-permute-start(f32[4096]{0:T(1024)S(1)} %add.220), channel_id=1, source_target_pairs={{0,2},{1,3},{2,0},{3,1},{4,6},{5,7},{6,4},{7,5},{8,10},{9,11},{10,... | collective-permute-start | bytes 49160 | tf_op jit(solution)/shard_map/ppermute | solution.py:587
  298.8 4.6 %collective-permute-start.35 = (f32[4096]{0:T(1024)S(1)}, f32[4096]{0:T(1024)S(1)}, u32[]{:S(2)}, u32[]{:S(2)}) collective-permute-start(f32[4096]{0:T(1024)S(1)} %add.221), channel_id=1, source_target_pairs={{0,4},{1,5},{2,6},{3,7},{4,0},{5,1},{6,2},{7,3},{8,12},{9,13},{10,... | collective-permute-start | bytes 49160 | tf_op jit(solution)/shard_map/ppermute | solution.py:587
  300.1 21.4 %collective-permute-start.39 = (bf16[1536,256]{1,0:T(8,128)(2,1)}, bf16[1536,256]{1,0:T(8,128)(2,1)S(1)}, u32[]{:S(2)}, u32[]{:S(2)}) collective-permute-start(bf16[1536,256]{1,0:T(8,128)(2,1)} %constant_dynamic-update-slice_fusion.10), channel_id=1, source_target_pairs={{0,16},{16,0},{8,24},{24,8},{1,17},{17,1},{9,25},{25,9},{2,18},{18... | collective-permute-start | bytes 2359304 | tf_op jit(solution)/shard_map/ppermute | solution.py:558
  300.9 22.0 %collective-permute-start.38 = (bf16[1536,256]{1,0:T(8,128)(2,1)S(1)}, bf16[1536,256]{1,0:T(8,128)(2,1)S(1)}, u32[]{:S(2)}, u32[]{:S(2)}) collective-permute-start(bf16[1536,256]{1,0:T(8,128)(2,1)S(1)} %copy-done.66), channel_id=1, source_target_pairs={{0,8},{8,0},{16,24},{24,16},{1,9},{9,1},{17,25},{25,17},{2,10},{10... | collective-permute-start | bytes 2359304 | tf_op jit(solution)/shard_map/ppermute | solution.py:558
  309.3 13.8 %collective-permute-start.36 = (f32[4864]{0:T(1024)S(1)}, f32[4864]{0:T(1024)S(1)}, u32[]{:S(2)}, u32[]{:S(2)}) collective-permute-start(f32[4864]{0:T(1024)S(1)} %pad_maximum_fusion.1), channel_id=1, source_target_pairs={{0,8},{8,0},{16,24},{24,16},{1,9},{9,1},{17,25},{25,17},{2,10},{10... | collective-permute-start | bytes 58376 | tf_op jit(solution)/shard_map/ppermute | solution.py:587
  323.1 3.8 %collective-permute-start.37 = (f32[4864]{0:T(1024)S(1)}, f32[4864]{0:T(1024)S(1)}, u32[]{:S(2)}, u32[]{:S(2)}) collective-permute-start(f32[4864]{0:T(1024)S(1)} %fusion.19), channel_id=1, source_target_pairs={{0,16},{8,24},{16,0},{24,8},{1,17},{9,25},{17,1},{25,9},{2,18},{10... | collective-permute-start | bytes 58376 | tf_op jit(solution)/shard_map/ppermute | solution.py:587
  (68 other events, 335.1 us)
Sparse Core Ops, SparseCore 0:
  13.3 59.7 all-gather.2
  75.3 28.4 all-gather.4
  164.7 47.9 reduce-scatter.4
  215.4 48.1 reduce-scatter.2
where the time goes:
time: 342 us; the launch traced here: 335 us
  Pallas kernels  107 us (31%)
  waiting for transfers between devices  89.3 us (26%)
  starting transfers between devices  59.7 us (17%)
  local copies, waits for them, and re-layouts  47 us (14%)
  other arithmetic  17 us (5%)
  between operations  15 us (4%)
    unnamed x147, local copies, waits for them, and re-layouts  36.3 us
    ppermute x11, starting transfers between devices, move(): return lax.ppermute(pieces, 'tp', pairs)  30.8 us
    ppermute x6, waiting for transfers between devices, share(): lax.ppermute(both[half], 'rows', PATHS[half][0])  28.7 us
    pallas_call x6, Pallas kernels, place(): pl.pallas_call(functools.partial(place_kernel, takes, len(old)), grid_spe...  27 us
    ppermute x11, waiting for transfers between devices, move(): return lax.ppermute(pieces, 'tp', pairs)  27 us
    ppermute x6, waiting for transfers between devices, total(): lax.ppermute(self.mine[half], 'rows', PATHS[half][1])  16.1 us
    pallas_call x2, Pallas kernels, merge(): pl.pallas_call(functools.partial(merge_kernel, count), grid=(tokens // bl...  15.7 us
    pallas_call x3, Pallas kernels, join(): pl.pallas_call(functools.partial(join_kernel, len(self.lhs), len(self.par...  13.5 us
  transfers between devices with their start and end apart: 46, of which 19 were waited for; matrix products, arithmetic and copies ran while one was open for 10% of the time, Pallas kernels for 31%

commit v1 on v0

--- a/solution.py
+++ b/solution.py
@@ -12,6 +12,7 @@
 LONG = 1000
 EPSILON = 1e-05
 ROOM = 16 * 2**20
+SMALL = 10 * 2**20
 IN_VMEM = pl.BlockSpec(memory_space=pltpu.VMEM)
 IN_SMEM = pl.BlockSpec(memory_space=pltpu.SMEM)
 
@@ -349,7 +350,7 @@
         ],
         out_specs=pl.BlockSpec((block, features), lambda step: (step, 0)),
         out_shape=jax.ShapeDtypeStruct((tokens, features), jnp.bfloat16),
-        compiler_params=pltpu.CompilerParams(vmem_limit_bytes=ROOM),
+        compiler_params=pltpu.CompilerParams(vmem_limit_bytes=SMALL),
         cost_estimate=busy(8),
         name="merge",
     )(*lhs, *weights)
@@ -424,7 +425,7 @@
         ),
         out_shape=[jax.ShapeDtypeStruct((size, features), jnp.float32) for size in sizes],
         input_output_aliases={1 + len(pieces) + index: index for index in range(len(old))},
-        compiler_params=pltpu.CompilerParams(vmem_limit_bytes=ROOM),
+        compiler_params=pltpu.CompilerParams(vmem_limit_bytes=SMALL),
         cost_estimate=busy(sum(sizes) * len(takes) * narrow / 300_000),
         name="place",
     )(jnp.stack(order).astype(jnp.int32), *pieces, *old)
@@ -510,7 +511,7 @@
         return jax.ShapeDtypeStruct((self.rows, wide), jnp.bfloat16)
 
     def room(self):
-        return pltpu.CompilerParams(vmem_limit_bytes=ROOM + 2048 * self.lhs[0].shape[1])
+        return pltpu.CompilerParams(vmem_limit_bytes=SMALL + 4096 * self.lhs[0].shape[1])
 
     def send(self, part, *earlier):
         rhs = self.parts[part]
@@ -624,7 +625,7 @@
             part,
             part,
         ],
-        compiler_params=pltpu.CompilerParams(vmem_limit_bytes=ROOM),
+        compiler_params=pltpu.CompilerParams(vmem_limit_bytes=SMALL),
         cost_estimate=busy(2),
         name="norm",
     )(place, lengths, values, gain[None], shift[None], cotangent)

time: 342 us -> 340 us (level)
  starting transfers between devices: 59.7 us -> 63.4 us
  waiting for transfers between devices: 89.3 us -> 85.8 us
  transfers between devices with their start and end apart: 46 -> 46, of which waited for: 19 -> 19; matrix products, arithmetic and copies ran while one was open for 10% -> 10% of each run, Pallas kernels for 31% -> 32%
where the time goes in v1:
time: 340 us; the launch traced here: 333 us
  Pallas kernels  107 us (31%)
  waiting for transfers between devices  85.8 us (25%)
  starting transfers between devices  63.4 us (19%)
  local copies, waits for them, and re-layouts  45.2 us (13%)
  other arithmetic  17 us (5%)
  between operations  15 us (4%)
    unnamed x147, local copies, waits for them, and re-layouts  34.5 us
    ppermute x11, starting transfers between devices, move(): return lax.ppermute(pieces, 'tp', pairs)  30.8 us
    pallas_call x6, Pallas kernels, place(): pl.pallas_call(functools.partial(place_kernel, takes, len(old)), grid_spe...  27 us
    ppermute x11, waiting for transfers between devices, move(): return lax.ppermute(pieces, 'tp', pairs)  27 us
    ppermute x6, waiting for transfers between devices, share(): lax.ppermute(both[half], 'rows', PATHS[half][0])  26.4 us
    ppermute x6, waiting for transfers between devices, total(): lax.ppermute(self.mine[half], 'rows', PATHS[half][1])  15.9 us
    pallas_call x2, Pallas kernels, merge(): pl.pallas_call(functools.partial(merge_kernel, count), grid=(tokens // bl...  15.7 us
    pallas_call x3, Pallas kernels, join(): pl.pallas_call(functools.partial(join_kernel, len(self.lhs), len(self.par...  13.5 us
  transfers between devices with their start and end apart: 46, of which 19 were waited for; matrix products, arithmetic and copies ran while one was open for 10% of the time, Pallas kernels for 32%

profile of v1, /device:TPU:0, one launch (start us, length us, event | category | flops | bytes accessed | tf_op | source)
XLA Modules:
  0.0 333.5 jit_solution(10353571994060906692)
XLA Ops:
  11.4 1.8 norm.1
  14.5 5.5 %collective-permute-start = (bf16[128,1024]{1,0:T(8,128)(2,1)S(1)}, bf16[128,1024]{1,0:T(8,128)(2,1)S(1)}, u32[]{:S(2)}, u32[]{:S(2)}) collective-permute-start(bf16[128,1024]{1,0:T(8,128)(2,1)S(1)} %get-tuple-element.103.refs_0_), channel_id=1, source_target_pairs={{0,2},{1,3},{2,0},{3,1},{4,6},{5,7},{6,4},{7,5},{8,10},{9,11},{10,... | collective-permute-start | bytes 786440 | tf_op jit(solution)/shard_map/ppermute | solution.py:463
  20.1 7.9 %collective-permute-done.refs_1_ = bf16[128,1024]{1,0:T(8,128)(2,1)S(1)} collective-permute-done((bf16[128,1024]{1,0:T(8,128)(2,1)S(1)}, bf16[128,1024]{1,0:T(8,128)(2,1)S(1)}, u32[]{:S(2)}, u32[]{:S(2)}) %collective-permute-start) | collective-permute-done | bytes 262176 | tf_op jit(solution)/shard_map/ppermute | solution.py:463
  28.8 3.8 %collective-permute-start.2 = (bf16[128,1024]{1,0:T(8,128)(2,1)S(1)}, bf16[128,1024]{1,0:T(8,128)(2,1)S(1)}, u32[]{:S(2)}, u32[]{:S(2)}) collective-permute-start(bf16[128,1024]{1,0:T(8,128)(2,1)S(1)} %collective-permute-done.1.refs_2_), channel_id=1, source_target_pairs={{0,2},{1,3},{2,0},{3,1},{4,6},{5,7},{6,4},{7,5},{8,10},{9,11},{10,... | collective-permute-start | bytes 786440 | tf_op jit(solution)/shard_map/ppermute | solution.py:463
  32.6 18.7 %collective-permute-start.4 = (bf16[128,1024]{1,0:T(8,128)(2,1)S(1)}, bf16[128,1024]{1,0:T(8,128)(2,1)S(1)}, u32[]{:S(2)}, u32[]{:S(2)}) collective-permute-start(bf16[128,1024]{1,0:T(8,128)(2,1)S(1)} %collective-permute-done.3.refs_4_), channel_id=1, source_target_pairs={{0,2},{1,3},{2,0},{3,1},{4,6},{5,7},{6,4},{7,5},{8,10},{9,11},{10,... | collective-permute-start | bytes 786440 | tf_op jit(solution)/shard_map/ppermute | solution.py:463
  52.4 18.0 %collective-permute-done.4.refs_5_ = bf16[128,1024]{1,0:T(8,128)(2,1)S(1)} collective-permute-done((bf16[128,1024]{1,0:T(8,128)(2,1)S(1)}, bf16[128,1024]{1,0:T(8,128)(2,1)S(1)}, u32[]{:S(2)}, u32[]{:S(2)}) %collective-permute-start.4) | collective-permute-done | bytes 262176 | tf_op jit(solution)/shard_map/ppermute | solution.py:463
  75.4 2.0 fusion.9
  79.9 1.9 copy-done.20
  81.7 7.6 %gated_forward.1 = (f32[704,1024]{1,0:T(8,128)S(1)}, f32[704,1024]{1,0:T(8,128)S(1)}, bf16[1024,704]{1,0:T(8,128)(2,1)S(1)}, bf16[704,1024]{1,0:T(8,128)(2,1)S(1)}) custom-call(bf16[1024,2048]{1,0:T(8,128)(2,1)S(1)} %copy-done.12, bf16[704,2048]{1,0:T(8,128)(2,1)S(1)} %copy-done.18, bf16[704,2048]{1,0:T(8,128)(2,1)S(1)} %copy-done.20), custom_call_target="tpu_custom_call" | custom-call | flops 11249999872 | tf_op jit(solution)/shard_map/gated_forward/pallas_call | solution.py:281
  91.2 8.6 %attend_forward.1 = (bf16[1024,256]{1,0:T(8,128)(2,1)S(1)}, bf16[1024,256]{1,0:T(8,128)(2,1)S(1)}, bf16[1024,256]{1,0:T(8,128)(2,1)S(1)}, bf16[1024,256]{1,0:T(8...) custom-call(bf16[1024,2048]{1,0:T(8,128)(2,1)S(1)} %copy-done.12, bf16[768,2048]{1,0:T(8,128)(2,1)S(1)} %bitcast.55, ...), custom_call_target="tpu_custom_call" | custom-call | flops 12750000128 | tf_op jit(solution)/shard_map/attend_forward/pallas_call | solution.py:126
  99.9 2.6 send_terms.4
  115.2 5.6 %gated_backward.1 = (bf16[1024,704]{1,0:T(8,128)(2,1)S(1)}, bf16[704,1024]{1,0:T(8,128)(2,1)S(1)}, bf16[1024,704]{1,0:T(8,128)(2,1)S(1)}, bf16[704,1024]{1,0:T(8,128)(2,1)S(1)}) custom-call(bf16[1024,1024]{1,0:T(8,128)(2,1)S(1)} %bitcast.59, bf16[1024,1024]{1,0:T(8,128)(2,1)S(1)} %copy-done.25, bf16[704,2048]{1,0:T(8,128)(2,1)S(1)} %copy-done.22, ...), custom_call_target="tpu_custom_call" | custom-call | flops 8099999744 | tf_op jit(solution)/shard_map/gated_backward/pallas_call | solution.py:322
  120.8 5.2 %send_terms.6 = (bf16[1408,512]{1,0:T(8,128)(2,1)}, bf16[1408,512]{1,0:T(8,128)(2,1)}) custom-call(s32[2]{0:T(128)S(1)} %pad_add_fusion.2.order, bf16[704,1024]{1,0:T(8,128)(2,1)S(1)} %get-tuple-element.140.refs_0_, bf16[704,1024]{1,0:T(8,128)(2,1)S(1)} %get-tuple-element.124.refs_1_, bf16[1024,2048]{1,0:T(8,128)(2,1)S(1)} %copy-done.13), custom_call_target="tpu_custom_call" | custom-call | flops 8249999872 | tf_op jit(solution)/shard_map/send_terms/pallas_call | solution.py:521
  128.1 4.4 %join_terms.3 = (bf16[960,256]{1,0:T(8,128)(2,1)}, bf16[960,256]{1,0:T(8,128)(2,1)S(1)}, bf16[960,256]{1,0:T(8,128)(2,1)}, bf16[960,256]{1,0:T(8,128)(2,1)S(1)}) custom-call(s32[3,2]{1,0:T(4,128)S(1)} %pad_add_fusion.order, bf16[704,1024]{1,0:T(8,128)(2,1)S(1)} %copy-done.36, bf16[256,1024]{1,0:T(8,128)(2,1)S(1)} %copy-done.41, ...), custom_call_target="tpu_custom_call" | custom-call | flops 5624999936 | tf_op jit(solution)/shard_map/join_terms/pallas_call | solution.py:537
  136.2 13.2 %attend_backward.1 = (bf16[1024,768]{1,0:T(8,128)(2,1)S(1)}, bf16[768,1024]{1,0:T(8,128)(2,1)S(1)}, f32[8,768]{1,0:T(8,128)S(1)}) custom-call(bf16[1024,256]{1,0:T(8,128)(2,1)S(1)} %copy-done.55, bf16[1024,256]{1,0:T(8,128)(2,1)S(1)} %copy-done.57, bf16[1024,256]{1,0:T(8,128)(2,1)S(1)} %copy-done.59, bf16[1024,1024]{1,0:T(8,128)(2,1)S(1)} %bitcast.61, ...), custom_call_target="tpu_custom_call" | custom-call | flops 19950000128 | tf_op jit(solution)/shard_map/attend_backward/pallas_call | solution.py:215
  150.5 10.4 %merge.2 = bf16[1024,2048]{1,0:T(8,128)(2,1)S(1)} custom-call(bf16[1024,704]{1,0:T(8,128)(2,1)S(1)} %get-tuple-element.135.refs_0_, bf16[1024,704]{1,0:T(8,128)(2,1)S(1)} %get-tuple-element.136.refs_1_, bf16[1024,768]{1,0:T(8,128)(2,1)S(1)} %get-tuple-element.137.refs_2_, bf16[704,2048]{1,0:T(8,128)(2,1)S(1)} %copy-done.19, ...), custom_call_target="tpu_custom_call" | custom-call | flops 12000000000 | tf_op jit(solution)/shard_map/merge/pallas_call | solution.py:344
  160.9 2.0 copy-done
  163.0 7.2 %collective-permute-done.15 = bf16[960,256]{1,0:T(8,128)(2,1)} collective-permute-done((bf16[960,256]{1,0:T(8,128)(2,1)}, bf16[960,256]{1,0:T(8,128)(2,1)}, u32[]{:S(2)}, u32[]{:S(2)}) %collective-permute-start.15) | collective-permute-done | bytes 491552 | tf_op jit(solution)/shard_map/ppermute | solution.py:547
  170.3 1.9 add.194.refs_0_
  173.6 1.9 add.195.refs_1_
  176.2 2.2 copy-done.14
  179.8 6.0 %join_terms.4 = (bf16[1408,256]{1,0:T(8,128)(2,1)}, bf16[1408,256]{1,0:T(8,128)(2,1)S(1)}, bf16[1408,256]{1,0:T(8,128)(2,1)}, bf16[1408,256]{1,0:T(8,128)(2,1)S(1)}) custom-call(s32[2,2]{1,0:T(2,128)S(1)} %pad_add_fusion.1.order, bf16[704,1024]{1,0:T(8,128)(2,1)S(1)} %copy-done.47, bf16[704,1024]{1,0:T(8,128)(2,1)S(1)} %copy-done.49, ...), custom_call_target="tpu_custom_call" | custom-call | flops 1500000026624 | tf_op jit(solution)/shard_map/join_terms/pallas_call | solution.py:537
  187.8 1.8 constant_dynamic-update-slice_fusion.1
  189.7 2.0 constant_dynamic-update-slice_fusion.3
  191.7 1.8 constant_dynamic-update-slice_fusion.2
  194.9 1.8 constant_dynamic-update-slice_fusion
  197.4 2.8 send_terms.7
  201.7 5.3 %merge.3 = bf16[1024,2048]{1,0:T(8,128)(2,1)S(1)} custom-call(bf16[1024,256]{1,0:T(8,128)(2,1)S(1)} %copy-done.53, bf16[1024,704]{1,0:T(8,128)(2,1)S(1)} %copy-done.51, bf16[256,2048]{1,0:T(8,128)(2,1)S(1)} %copy-done.27, bf16[704,2048]{1,0:T(8,128)(2,1)S(1)} %copy-done.23), custom_call_target="tpu_custom_call" | custom-call | flops 12000000000 | tf_op jit(solution)/shard_map/merge/pallas_call | solution.py:344
  207.0 2.0 copy-done.1
  209.1 14.2 %collective-permute-done.22.refs_1_ = bf16[1920,256]{1,0:T(8,128)(2,1)} collective-permute-done((bf16[1920,256]{1,0:T(8,128)(2,1)}, bf16[1920,256]{1,0:T(8,128)(2,1)}, u32[]{:S(2)}, u32[]{:S(2)}) %collective-permute-start.22) | collective-permute-done | bytes 983072 | tf_op jit(solution)/shard_map/ppermute | solution.py:559
  224.7 5.6 %place.6 = (f32[704,2048]{1,0:T(8,128)}, f32[256,2048]{1,0:T(8,128)}) custom-call(s32[8]{0:T(128)S(1)} %stack.165.order, bf16[960,256]{1,0:T(8,128)(2,1)} %add.194.refs_0_, bf16[960,256]{1,0:T(8,128)(2,1)} %add.195.refs_1_, bf16[960,256]{1,0:T(8,128)(2,1)} %collective-permute-done.19.refs_2_, bf16[960,256]{1,0:T(8,128)(2,1)} %collective-permute-done.20.refs_3_), custom_call_target="tpu_custom_call" | custom-call | flops 4915200000 | tf_op jit(solution)/shard_map/place/pallas_call | solution.py:415
  230.3 5.6 %place.7 = (f32[704,2048]{1,0:T(8,128)}, f32[256,2048]{1,0:T(8,128)}) custom-call(s32[8]{0:T(128)S(1)} %stack.160.order, bf16[1920,256]{1,0:T(8,128)(2,1)} %collective-permute-done.21.refs_0_, bf16[1920,256]{1,0:T(8,128)(2,1)} %collective-permute-done.22.refs_1_, ...), custom_call_target="tpu_custom_call", output_to_operand_aliasing={{0}: (3, {}), {1}: (4, {})} | custom-call | flops 4915200000 | tf_op jit(solution)/shard_map/place/pallas_call | solution.py:415
  235.8 2.3 add.217.refs_1_
  238.7 2.2 add.216.refs_0_
  242.3 2.4 collective-permute-done.25.refs_2_
  244.6 3.0 join_terms.5
  252.0 7.6 %collective-permute-done.27.refs_2_ = bf16[1408,256]{1,0:T(8,128)(2,1)} collective-permute-done((bf16[1408,256]{1,0:T(8,128)(2,1)}, bf16[1408,256]{1,0:T(8,128)(2,1)}, u32[]{:S(2)}, u32[]{:S(2)}) %collective-permute-start.27) | collective-permute-done | bytes 720928 | tf_op jit(solution)/shard_map/ppermute | solution.py:553
  263.6 1.9 collective-permute-done.29
  271.0 6.7 %collective-permute-done.31.refs_2_ = bf16[768,256]{1,0:T(8,128)(2,1)S(1)} collective-permute-done((bf16[768,256]{1,0:T(8,128)(2,1)S(1)}, bf16[768,256]{1,0:T(8,128)(2,1)S(1)}, u32[]{:S(2)}, u32[]{:S(2)}) %collective-permute-start.31) | collective-permute-done | bytes 393248 | tf_op jit(solution)/shard_map/ppermute | solution.py:553
  283.2 2.1 add_convert_fusion
  285.3 5.2 %place.8 = (f32[704,2048]{1,0:T(8,128)}, f32[704,2048]{1,0:T(8,128)}) custom-call(s32[4]{0:T(128)S(1)} %pad_add_fusion.4.order, bf16[1408,256]{1,0:T(8,128)(2,1)} %add.216.refs_0_, bf16[1408,256]{1,0:T(8,128)(2,1)} %add.217.refs_1_, bf16[1408,256]{1,0:T(8,128)(2,1)} %collective-permute-done.27.refs_2_, bf16[1408,256]{1,0:T(8,128)(2,1)} %collective-permute-done.28.refs_3_), custom_call_target="tpu_custom_call" | custom-call | flops 7208960000 | tf_op jit(solution)/shard_map/place/pallas_call | solution.py:415
  290.5 2.7 place.9.refs_2_
  294.4 2.3 collective-permute-start.34
  298.4 2.3 collective-permute-start.35
  303.4 2.2 collective-permute-done.40.refs_0_
  306.4 5.2 %place.10 = (f32[704,2048]{1,0:T(8,128)}, f32[704,2048]{1,0:T(8,128)}) custom-call(s32[4]{0:T(128)S(1)} %pad_add_fusion.5.order, bf16[2816,256]{1,0:T(8,128)(2,1)} %collective-permute-done.40.refs_0_, bf16[2816,256]{1,0:T(8,128)(2,1)} %collective-permute-done.41.refs_1_, ...), custom_call_target="tpu_custom_call", output_to_operand_aliasing={{0}: (3, {}), {1}: (4, {})} | custom-call | flops 7208960000 | tf_op jit(solution)/shard_map/place/pallas_call | solution.py:415
  311.6 8.3 %collective-permute-done.39.refs_1_ = bf16[1536,256]{1,0:T(8,128)(2,1)S(1)} collective-permute-done((bf16[1536,256]{1,0:T(8,128)(2,1)}, bf16[1536,256]{1,0:T(8,128)(2,1)S(1)}, u32[]{:S(2)}, u32[]{:S(2)}) %collective-permute-start.39) | collective-permute-done | bytes 786464 | tf_op jit(solution)/shard_map/ppermute | solution.py:559
  322.1 2.7 place.11
  (274 shorter events, 78.1 us)
Async XLA Ops:
  7.2 68.0 %all-gather.3.cloned.1.call-start = ((), (), s32[]{:S(2)}) async-start(), calls=%async_computation.2 | async-start | bytes 4718592 | tf_op jit(solution)/shard_map/all_gather | solution.py:663
  11.4 40.0 %copy-start.68 = (bf16[3,256]{1,0:T(4,128)(2,1)S(1)}, bf16[3,256]{1,0:T(4,128)(2,1)}, u32[]{:S(2)}) copy-start(bf16[3,256]{1,0:T(4,128)(2,1)} %param.15) | copy-start | bytes 4612
  11.4 59.1 %copy-start.30 = (s32[1,8]{1,0:T(1,128)S(1)}, s32[1,8]{1,0:T(1,128)}, u32[]{:S(2)}) copy-start(s32[1,8]{1,0:T(1,128)} %lengths.1) | copy-start | bytes 100
  13.2 92.2 %all-gather.5.cloned.1.call-start = ((), (), s32[]{:S(2)}) async-start(), calls=%async_computation.3 | async-start | bytes 2359296 | tf_op jit(solution)/shard_map/all_gather | solution.py:669
  13.3 38.6 %collective-permute-start.5 = (bf16[128,1024]{1,0:T(8,128)(2,1)S(1)}, bf16[128,1024]{1,0:T(8,128)(2,1)S(1)}, u32[]{:S(2)}, u32[]{:S(2)}) collective-permute-start(bf16[128,1024]{1,0:T(8,128)(2,1)S(1)} %get-tuple-element.103.refs_0_), channel_id=1, source_target_pairs={{0,1},{1,0},{2,3},{3,2},{4,5},{5,4},{6,7},{7,6},{8,9},{9,8},{10,11... | collective-permute-start | bytes 786440 | tf_op jit(solution)/shard_map/ppermute | solution.py:463
  13.8 15.0 %collective-permute-start.1 = (bf16[128,1024]{1,0:T(8,128)(2,1)S(1)}, bf16[128,1024]{1,0:T(8,128)(2,1)S(1)}, u32[]{:S(2)}, u32[]{:S(2)}) collective-permute-start(bf16[128,1024]{1,0:T(8,128)(2,1)S(1)} %get-tuple-element.103.refs_0_), channel_id=1, source_target_pairs={{0,0},{1,1},{2,4},{3,5},{4,2},{5,3},{6,6},{7,7},{8,8},{9,9},{10,12... | collective-permute-start | bytes 786440 | tf_op jit(solution)/shard_map/ppermute | solution.py:463
  14.5 13.6 %collective-permute-start = (bf16[128,1024]{1,0:T(8,128)(2,1)S(1)}, bf16[128,1024]{1,0:T(8,128)(2,1)S(1)}, u32[]{:S(2)}, u32[]{:S(2)}) collective-permute-start(bf16[128,1024]{1,0:T(8,128)(2,1)S(1)} %get-tuple-element.103.refs_0_), channel_id=1, source_target_pairs={{0,2},{1,3},{2,0},{3,1},{4,6},{5,7},{6,4},{7,5},{8,10},{9,11},{10,... | collective-permute-start | bytes 786440 | tf_op jit(solution)/shard_map/ppermute | solution.py:463
  28.0 4.6 %collective-permute-start.3 = (bf16[128,1024]{1,0:T(8,128)(2,1)S(1)}, bf16[128,1024]{1,0:T(8,128)(2,1)S(1)}, u32[]{:S(2)}, u32[]{:S(2)}) collective-permute-start(bf16[128,1024]{1,0:T(8,128)(2,1)S(1)} %collective-permute-done.refs_1_), channel_id=1, source_target_pairs={{0,0},{1,1},{2,4},{3,5},{4,2},{5,3},{6,6},{7,7},{8,8},{9,9},{10,12... | collective-permute-start | bytes 786440 | tf_op jit(solution)/shard_map/ppermute | solution.py:463
  28.8 23.2 %collective-permute-start.2 = (bf16[128,1024]{1,0:T(8,128)(2,1)S(1)}, bf16[128,1024]{1,0:T(8,128)(2,1)S(1)}, u32[]{:S(2)}, u32[]{:S(2)}) collective-permute-start(bf16[128,1024]{1,0:T(8,128)(2,1)S(1)} %collective-permute-done.1.refs_2_), channel_id=1, source_target_pairs={{0,2},{1,3},{2,0},{3,1},{4,6},{5,7},{6,4},{7,5},{8,10},{9,11},{10,... | collective-permute-start | bytes 786440 | tf_op jit(solution)/shard_map/ppermute | solution.py:463
  32.6 37.8 %collective-permute-start.4 = (bf16[128,1024]{1,0:T(8,128)(2,1)S(1)}, bf16[128,1024]{1,0:T(8,128)(2,1)S(1)}, u32[]{:S(2)}, u32[]{:S(2)}) collective-permute-start(bf16[128,1024]{1,0:T(8,128)(2,1)S(1)} %collective-permute-done.3.refs_4_), channel_id=1, source_target_pairs={{0,2},{1,3},{2,0},{3,1},{4,6},{5,7},{6,4},{7,5},{8,10},{9,11},{10,... | collective-permute-start | bytes 786440 | tf_op jit(solution)/shard_map/ppermute | solution.py:463
  51.4 19.7 %collective-permute-start.7 = (bf16[128,1024]{1,0:T(8,128)(2,1)S(1)}, bf16[128,1024]{1,0:T(8,128)(2,1)S(1)}, u32[]{:S(2)}, u32[]{:S(2)}) collective-permute-start(bf16[128,1024]{1,0:T(8,128)(2,1)S(1)} %collective-permute-done.1.refs_2_), channel_id=1, source_target_pairs={{0,1},{1,0},{2,3},{3,2},{4,5},{5,4},{6,7},{7,6},{8,9},{9,8},{10,11... | collective-permute-start | bytes 786440 | tf_op jit(solution)/shard_map/ppermute | solution.py:463
  51.4 19.7 %collective-permute-start.6 = (bf16[128,1024]{1,0:T(8,128)(2,1)S(1)}, bf16[128,1024]{1,0:T(8,128)(2,1)}, u32[]{:S(2)}, u32[]{:S(2)}) collective-permute-start(bf16[128,1024]{1,0:T(8,128)(2,1)S(1)} %collective-permute-done.refs_1_), channel_id=1, source_target_pairs={{0,1},{1,0},{2,3},{3,2},{4,5},{5,4},{6,7},{7,6},{8,9},{9,8},{10,11... | collective-permute-start | bytes 786440 | tf_op jit(solution)/shard_map/ppermute | solution.py:463
  51.9 19.2 %collective-permute-start.9 = (bf16[128,1024]{1,0:T(8,128)(2,1)S(1)}, bf16[128,1024]{1,0:T(8,128)(2,1)}, u32[]{:S(2)}, u32[]{:S(2)}) collective-permute-start(bf16[128,1024]{1,0:T(8,128)(2,1)S(1)} %collective-permute-done.3.refs_4_), channel_id=1, source_target_pairs={{0,1},{1,0},{2,3},{3,2},{4,5},{5,4},{6,7},{7,6},{8,9},{9,8},{10,11... | collective-permute-start | bytes 786440 | tf_op jit(solution)/shard_map/ppermute | solution.py:463
  52.0 19.1 %collective-permute-start.8 = (bf16[128,1024]{1,0:T(8,128)(2,1)S(1)}, bf16[128,1024]{1,0:T(8,128)(2,1)}, u32[]{:S(2)}, u32[]{:S(2)}) collective-permute-start(bf16[128,1024]{1,0:T(8,128)(2,1)S(1)} %collective-permute-done.2.refs_3_), channel_id=1, source_target_pairs={{0,1},{1,0},{2,3},{3,2},{4,5},{5,4},{6,7},{7,6},{8,9},{9,8},{10,11... | collective-permute-start | bytes 786440 | tf_op jit(solution)/shard_map/ppermute | solution.py:463
  70.4 1.7 collective-permute-start.10
  75.2 205.1 %reduce-scatter.5.cloned.1.call-start = ((), (), s32[]{:S(2)}) async-start(), calls=%async_computation.5 | async-start | bytes 4718592 | tf_op jit(solution)/shard_map/reduce_scatter | solution.py:721
  102.5 24.1 %collective-permute-start.11 = (bf16[960,256]{1,0:T(8,128)(2,1)}, bf16[960,256]{1,0:T(8,128)(2,1)}, u32[]{:S(2)}, u32[]{:S(2)}) collective-permute-start(bf16[960,256]{1,0:T(8,128)(2,1)} %get-tuple-element.115), channel_id=1, source_target_pairs={{0,8},{8,0},{16,24},{24,16},{1,9},{9,1},{17,25},{25,17},{2,10},{10... | collective-permute-start | bytes 1474568 | tf_op jit(solution)/shard_map/ppermute | solution.py:529
  104.0 24.1 %collective-permute-start.12 = (bf16[960,256]{1,0:T(8,128)(2,1)}, bf16[960,256]{1,0:T(8,128)(2,1)}, u32[]{:S(2)}, u32[]{:S(2)}) collective-permute-start(bf16[960,256]{1,0:T(8,128)(2,1)} %get-tuple-element.116), channel_id=1, source_target_pairs={{0,16},{16,0},{8,24},{24,8},{1,17},{17,1},{9,25},{25,9},{2,18},{18... | collective-permute-start | bytes 1474568 | tf_op jit(solution)/shard_map/ppermute | solution.py:529
  111.2 16.8 %collective-permute-start.13 = (bf16[960,256]{1,0:T(8,128)(2,1)S(1)}, bf16[960,256]{1,0:T(8,128)(2,1)S(1)}, u32[]{:S(2)}, u32[]{:S(2)}) collective-permute-start(bf16[960,256]{1,0:T(8,128)(2,1)S(1)} %get-tuple-element.118), channel_id=1, source_target_pairs={{0,8},{8,0},{16,24},{24,16},{1,9},{9,1},{17,25},{25,17},{2,10},{10... | collective-permute-start | bytes 1474568 | tf_op jit(solution)/shard_map/ppermute | solution.py:529
  111.8 16.2 %collective-permute-start.14 = (bf16[960,256]{1,0:T(8,128)(2,1)S(1)}, bf16[960,256]{1,0:T(8,128)(2,1)S(1)}, u32[]{:S(2)}, u32[]{:S(2)}) collective-permute-start(bf16[960,256]{1,0:T(8,128)(2,1)S(1)} %get-tuple-element.119), channel_id=1, source_target_pairs={{0,16},{16,0},{8,24},{24,8},{1,17},{17,1},{9,25},{25,9},{2,18},{18... | collective-permute-start | bytes 1474568 | tf_op jit(solution)/shard_map/ppermute | solution.py:529
  126.0 50.2 %collective-permute-start.17 = (bf16[1408,512]{1,0:T(8,128)(2,1)}, bf16[1408,512]{1,0:T(8,128)(2,1)}, u32[]{:S(2)}, u32[]{:S(2)}) collective-permute-start(bf16[1408,512]{1,0:T(8,128)(2,1)} %get-tuple-element.125), channel_id=1, source_target_pairs={{0,8},{8,0},{16,24},{24,16},{1,9},{9,1},{17,25},{25,17},{2,10},{10... | collective-permute-start | bytes 4325384 | tf_op jit(solution)/shard_map/ppermute | solution.py:529
  126.6 49.6 %collective-permute-start.18 = (bf16[1408,512]{1,0:T(8,128)(2,1)}, bf16[1408,512]{1,0:T(8,128)(2,1)}, u32[]{:S(2)}, u32[]{:S(2)}) collective-permute-start(bf16[1408,512]{1,0:T(8,128)(2,1)} %get-tuple-element.126), channel_id=1, source_target_pairs={{0,16},{16,0},{8,24},{24,8},{1,17},{17,1},{9,25},{25,9},{2,18},{18... | collective-permute-start | bytes 4325384 | tf_op jit(solution)/shard_map/ppermute | solution.py:529
  134.0 36.2 %collective-permute-start.15 = (bf16[960,256]{1,0:T(8,128)(2,1)}, bf16[960,256]{1,0:T(8,128)(2,1)}, u32[]{:S(2)}, u32[]{:S(2)}) collective-permute-start(bf16[960,256]{1,0:T(8,128)(2,1)} %get-tuple-element.128), channel_id=1, source_target_pairs={{0,16},{16,0},{8,24},{24,8},{1,17},{17,1},{9,25},{25,9},{2,18},{18... | collective-permute-start | bytes 1474568 | tf_op jit(solution)/shard_map/ppermute | solution.py:547
  135.1 38.5 %collective-permute-start.16 = (bf16[960,256]{1,0:T(8,128)(2,1)}, bf16[960,256]{1,0:T(8,128)(2,1)}, u32[]{:S(2)}, u32[]{:S(2)}) collective-permute-start(bf16[960,256]{1,0:T(8,128)(2,1)} %get-tuple-element.130), channel_id=1, source_target_pairs={{0,8},{8,0},{16,24},{24,16},{1,9},{9,1},{17,25},{25,17},{2,10},{10... | collective-permute-start | bytes 1474568 | tf_op jit(solution)/shard_map/ppermute | solution.py:547
  163.0 120.2 %reduce-scatter.3.cloned.1.call-start = ((), (), s32[]{:S(2)}) async-start(), calls=%async_computation.4 | async-start | bytes 4718592 | tf_op jit(solution)/shard_map/reduce_scatter | solution.py:723
  172.2 22.8 %collective-permute-start.19 = (bf16[960,256]{1,0:T(8,128)(2,1)}, bf16[960,256]{1,0:T(8,128)(2,1)}, u32[]{:S(2)}, u32[]{:S(2)}) collective-permute-start(bf16[960,256]{1,0:T(8,128)(2,1)} %add.194.refs_0_), channel_id=1, source_target_pairs={{0,16},{16,0},{8,24},{24,8},{1,17},{17,1},{9,25},{25,9},{2,18},{18... | collective-permute-start | bytes 1474568 | tf_op jit(solution)/shard_map/ppermute | solution.py:553
  175.5 16.1 %collective-permute-start.20 = (bf16[960,256]{1,0:T(8,128)(2,1)}, bf16[960,256]{1,0:T(8,128)(2,1)}, u32[]{:S(2)}, u32[]{:S(2)}) collective-permute-start(bf16[960,256]{1,0:T(8,128)(2,1)} %add.195.refs_1_), channel_id=1, source_target_pairs={{0,8},{8,0},{16,24},{24,16},{1,9},{9,1},{17,25},{25,17},{2,10},{10... | collective-permute-start | bytes 1474568 | tf_op jit(solution)/shard_map/ppermute | solution.py:553
  185.8 52.8 %collective-permute-start.23 = (bf16[1408,256]{1,0:T(8,128)(2,1)}, bf16[1408,256]{1,0:T(8,128)(2,1)}, u32[]{:S(2)}, u32[]{:S(2)}) collective-permute-start(bf16[1408,256]{1,0:T(8,128)(2,1)} %get-tuple-element.141), channel_id=1, source_target_pairs={{0,16},{16,0},{8,24},{24,8},{1,17},{17,1},{9,25},{25,9},{2,18},{18... | collective-permute-start | bytes 2162696 | tf_op jit(solution)/shard_map/ppermute | solution.py:547
  187.3 48.5 %collective-permute-start.24 = (bf16[1408,256]{1,0:T(8,128)(2,1)}, bf16[1408,256]{1,0:T(8,128)(2,1)}, u32[]{:S(2)}, u32[]{:S(2)}) collective-permute-start(bf16[1408,256]{1,0:T(8,128)(2,1)} %get-tuple-element.143), channel_id=1, source_target_pairs={{0,8},{8,0},{16,24},{24,16},{1,9},{9,1},{17,25},{25,17},{2,10},{10... | collective-permute-start | bytes 2162696 | tf_op jit(solution)/shard_map/ppermute | solution.py:547
  193.5 29.7 %collective-permute-start.22 = (bf16[1920,256]{1,0:T(8,128)(2,1)}, bf16[1920,256]{1,0:T(8,128)(2,1)}, u32[]{:S(2)}, u32[]{:S(2)}) collective-permute-start(bf16[1920,256]{1,0:T(8,128)(2,1)} %constant_dynamic-update-slice_fusion.2), channel_id=1, source_target_pairs={{0,16},{16,0},{8,24},{24,8},{1,17},{17,1},{9,25},{25,9},{2,18},{18... | collective-permute-start | bytes 2949128 | tf_op jit(solution)/shard_map/ppermute | solution.py:559
  196.8 33.5 %collective-permute-start.21 = (bf16[1920,256]{1,0:T(8,128)(2,1)}, bf16[1920,256]{1,0:T(8,128)(2,1)}, u32[]{:S(2)}, u32[]{:S(2)}) collective-permute-start(bf16[1920,256]{1,0:T(8,128)(2,1)} %constant_dynamic-update-slice_fusion), channel_id=1, source_target_pairs={{0,8},{8,0},{16,24},{24,16},{1,9},{9,1},{17,25},{25,17},{2,10},{10... | collective-permute-start | bytes 2949128 | tf_op jit(solution)/shard_map/ppermute | solution.py:559
  200.3 44.4 %collective-permute-start.25 = (bf16[768,512]{1,0:T(8,128)(2,1)}, bf16[768,512]{1,0:T(8,128)(2,1)}, u32[]{:S(2)}, u32[]{:S(2)}) collective-permute-start(bf16[768,512]{1,0:T(8,128)(2,1)} %get-tuple-element.148), channel_id=1, source_target_pairs={{0,8},{8,0},{16,24},{24,16},{1,9},{9,1},{17,25},{25,17},{2,10},{10... | collective-permute-start | bytes 2359304 | tf_op jit(solution)/shard_map/ppermute | solution.py:529
  223.2 21.4 %collective-permute-start.26 = (bf16[768,512]{1,0:T(8,128)(2,1)}, bf16[768,512]{1,0:T(8,128)(2,1)S(1)}, u32[]{:S(2)}, u32[]{:S(2)}) collective-permute-start(bf16[768,512]{1,0:T(8,128)(2,1)} %copy-done.28), channel_id=1, source_target_pairs={{0,16},{16,0},{8,24},{24,8},{1,17},{17,1},{9,25},{25,9},{2,18},{18... | collective-permute-start | bytes 2359304 | tf_op jit(solution)/shard_map/ppermute | solution.py:529
  238.2 22.6 %collective-permute-start.28 = (bf16[1408,256]{1,0:T(8,128)(2,1)}, bf16[1408,256]{1,0:T(8,128)(2,1)}, u32[]{:S(2)}, u32[]{:S(2)}) collective-permute-start(bf16[1408,256]{1,0:T(8,128)(2,1)} %add.217.refs_1_), channel_id=1, source_target_pairs={{0,8},{8,0},{16,24},{24,16},{1,9},{9,1},{17,25},{25,17},{2,10},{10... | collective-permute-start | bytes 2162696 | tf_op jit(solution)/shard_map/ppermute | solution.py:553
  240.8 18.8 %collective-permute-start.27 = (bf16[1408,256]{1,0:T(8,128)(2,1)}, bf16[1408,256]{1,0:T(8,128)(2,1)}, u32[]{:S(2)}, u32[]{:S(2)}) collective-permute-start(bf16[1408,256]{1,0:T(8,128)(2,1)} %add.216.refs_0_), channel_id=1, source_target_pairs={{0,16},{16,0},{8,24},{24,8},{1,17},{17,1},{9,25},{25,9},{2,18},{18... | collective-permute-start | bytes 2162696 | tf_op jit(solution)/shard_map/ppermute | solution.py:553
  247.7 17.8 %collective-permute-start.29 = (bf16[768,256]{1,0:T(8,128)(2,1)S(1)}, bf16[768,256]{1,0:T(8,128)(2,1)S(1)}, u32[]{:S(2)}, u32[]{:S(2)}) collective-permute-start(bf16[768,256]{1,0:T(8,128)(2,1)S(1)} %get-tuple-element.167), channel_id=1, source_target_pairs={{0,16},{16,0},{8,24},{24,8},{1,17},{17,1},{9,25},{25,9},{2,18},{18... | collective-permute-start | bytes 1179656 | tf_op jit(solution)/shard_map/ppermute | solution.py:547
  248.3 18.9 %collective-permute-start.30 = (bf16[768,256]{1,0:T(8,128)(2,1)S(1)}, bf16[768,256]{1,0:T(8,128)(2,1)S(1)}, u32[]{:S(2)}, u32[]{:S(2)}) collective-permute-start(bf16[768,256]{1,0:T(8,128)(2,1)S(1)} %get-tuple-element.168), channel_id=1, source_target_pairs={{0,8},{8,0},{16,24},{24,16},{1,9},{9,1},{17,25},{25,17},{2,10},{10... | collective-permute-start | bytes 1179656 | tf_op jit(solution)/shard_map/ppermute | solution.py:547
  265.6 12.1 %collective-permute-start.31 = (bf16[768,256]{1,0:T(8,128)(2,1)S(1)}, bf16[768,256]{1,0:T(8,128)(2,1)S(1)}, u32[]{:S(2)}, u32[]{:S(2)}) collective-permute-start(bf16[768,256]{1,0:T(8,128)(2,1)S(1)} %add.218.refs_0_), channel_id=1, source_target_pairs={{0,16},{16,0},{8,24},{24,8},{1,17},{17,1},{9,25},{25,9},{2,18},{18... | collective-permute-start | bytes 1179656 | tf_op jit(solution)/shard_map/ppermute | solution.py:553
  267.3 12.1 %collective-permute-start.32 = (bf16[768,256]{1,0:T(8,128)(2,1)S(1)}, bf16[768,256]{1,0:T(8,128)(2,1)S(1)}, u32[]{:S(2)}, u32[]{:S(2)}) collective-permute-start(bf16[768,256]{1,0:T(8,128)(2,1)S(1)} %add.219.refs_1_), channel_id=1, source_target_pairs={{0,8},{8,0},{16,24},{24,16},{1,9},{9,1},{17,25},{25,17},{2,10},{10... | collective-permute-start | bytes 1179656 | tf_op jit(solution)/shard_map/ppermute | solution.py:553
  268.2 35.2 %collective-permute-start.41 = (bf16[2816,256]{1,0:T(8,128)(2,1)}, bf16[2816,256]{1,0:T(8,128)(2,1)}, u32[]{:S(2)}, u32[]{:S(2)}) collective-permute-start(bf16[2816,256]{1,0:T(8,128)(2,1)} %copy-done.63), channel_id=1, source_target_pairs={{0,16},{16,0},{8,24},{24,8},{1,17},{17,1},{9,25},{25,9},{2,18},{18... | collective-permute-start | bytes 4325384 | tf_op jit(solution)/shard_map/ppermute | solution.py:559
  269.7 35.9 %collective-permute-start.40 = (bf16[2816,256]{1,0:T(8,128)(2,1)}, bf16[2816,256]{1,0:T(8,128)(2,1)}, u32[]{:S(2)}, u32[]{:S(2)}) collective-permute-start(bf16[2816,256]{1,0:T(8,128)(2,1)} %copy-done.64), channel_id=1, source_target_pairs={{0,8},{8,0},{16,24},{24,16},{1,9},{9,1},{17,25},{25,17},{2,10},{10... | collective-permute-start | bytes 4325384 | tf_op jit(solution)/shard_map/ppermute | solution.py:559
  293.2 1.2 collective-permute-start.33
  294.4 4.0 %collective-permute-start.34 = (f32[4096]{0:T(1024)S(1)}, f32[4096]{0:T(1024)S(1)}, u32[]{:S(2)}, u32[]{:S(2)}) collective-permute-start(f32[4096]{0:T(1024)S(1)} %add.220), channel_id=1, source_target_pairs={{0,2},{1,3},{2,0},{3,1},{4,6},{5,7},{6,4},{7,5},{8,10},{9,11},{10,... | collective-permute-start | bytes 49160 | tf_op jit(solution)/shard_map/ppermute | solution.py:588
  298.4 4.7 %collective-permute-start.35 = (f32[4096]{0:T(1024)S(1)}, f32[4096]{0:T(1024)S(1)}, u32[]{:S(2)}, u32[]{:S(2)}) collective-permute-start(f32[4096]{0:T(1024)S(1)} %add.221), channel_id=1, source_target_pairs={{0,4},{1,5},{2,6},{3,7},{4,0},{5,1},{6,2},{7,3},{8,12},{9,13},{10,... | collective-permute-start | bytes 49160 | tf_op jit(solution)/shard_map/ppermute | solution.py:588
  300.7 19.2 %collective-permute-start.39 = (bf16[1536,256]{1,0:T(8,128)(2,1)}, bf16[1536,256]{1,0:T(8,128)(2,1)S(1)}, u32[]{:S(2)}, u32[]{:S(2)}) collective-permute-start(bf16[1536,256]{1,0:T(8,128)(2,1)} %constant_dynamic-update-slice_fusion.10), channel_id=1, source_target_pairs={{0,16},{16,0},{8,24},{24,8},{1,17},{17,1},{9,25},{25,9},{2,18},{18... | collective-permute-start | bytes 2359304 | tf_op jit(solution)/shard_map/ppermute | solution.py:559
  301.4 19.9 %collective-permute-start.38 = (bf16[1536,256]{1,0:T(8,128)(2,1)S(1)}, bf16[1536,256]{1,0:T(8,128)(2,1)S(1)}, u32[]{:S(2)}, u32[]{:S(2)}) collective-permute-start(bf16[1536,256]{1,0:T(8,128)(2,1)S(1)} %copy-done.66), channel_id=1, source_target_pairs={{0,8},{8,0},{16,24},{24,16},{1,9},{9,1},{17,25},{25,17},{2,10},{10... | collective-permute-start | bytes 2359304 | tf_op jit(solution)/shard_map/ppermute | solution.py:559
  305.6 15.9 %collective-permute-start.36 = (f32[4864]{0:T(1024)S(1)}, f32[4864]{0:T(1024)S(1)}, u32[]{:S(2)}, u32[]{:S(2)}) collective-permute-start(f32[4864]{0:T(1024)S(1)} %pad_maximum_fusion.1), channel_id=1, source_target_pairs={{0,8},{8,0},{16,24},{24,16},{1,9},{9,1},{17,25},{25,17},{2,10},{10... | collective-permute-start | bytes 58376 | tf_op jit(solution)/shard_map/ppermute | solution.py:588
  321.5 3.8 %collective-permute-start.37 = (f32[4864]{0:T(1024)S(1)}, f32[4864]{0:T(1024)S(1)}, u32[]{:S(2)}, u32[]{:S(2)}) collective-permute-start(f32[4864]{0:T(1024)S(1)} %fusion.19), channel_id=1, source_target_pairs={{0,16},{8,24},{16,0},{24,8},{1,17},{9,25},{17,1},{25,9},{2,18},{10... | collective-permute-start | bytes 58376 | tf_op jit(solution)/shard_map/ppermute | solution.py:588
  (68 other events, 347.2 us)
Sparse Core Ops, SparseCore 0:
  13.3 59.7 all-gather.2
  75.3 28.4 all-gather.4
  163.1 48.0 reduce-scatter.4
  213.9 48.1 reduce-scatter.2

commit v2 on v1

--- a/solution.py
+++ b/solution.py
@@ -11,8 +11,8 @@
 MASKED = -1e30
 LONG = 1000
 EPSILON = 1e-05
-ROOM = 16 * 2**20
-SMALL = 10 * 2**20
+ROOM = 13 * 2**20
+SMALL = 8 * 2**20
 IN_VMEM = pl.BlockSpec(memory_space=pltpu.VMEM)
 IN_SMEM = pl.BlockSpec(memory_space=pltpu.SMEM)
 

time: 340 us -> 340 us (level)
    unnamed x147 -> x151, local copies, waits for them, and re-layouts: 34.5 us -> 36 us
where the time goes in v2:
time: 340 us; the launch traced here: 333 us
  Pallas kernels  107 us (31%)
  waiting for transfers between devices  84.2 us (25%)
  starting transfers between devices  63.6 us (19%)
  local copies, waits for them, and re-layouts  46.7 us (14%)
  other arithmetic  17 us (5%)
  between operations  15 us (4%)
    unnamed x151, local copies, waits for them, and re-layouts  36 us
    ppermute x11, starting transfers between devices, move(): return lax.ppermute(pieces, 'tp', pairs)  30.8 us
    pallas_call x6, Pallas kernels, place(): pl.pallas_call(functools.partial(place_kernel, takes, len(old)), grid_spe...  27 us
    ppermute x11, waiting for transfers between devices, move(): return lax.ppermute(pieces, 'tp', pairs)  27 us
    ppermute x6, waiting for transfers between devices, share(): lax.ppermute(both[half], 'rows', PATHS[half][0])  24.1 us
    ppermute x6, waiting for transfers between devices, total(): lax.ppermute(self.mine[half], 'rows', PATHS[half][1])  15.9 us
    pallas_call x2, Pallas kernels, merge(): pl.pallas_call(functools.partial(merge_kernel, count), grid=(tokens // bl...  15.7 us
    pallas_call x3, Pallas kernels, join(): pl.pallas_call(functools.partial(join_kernel, len(self.lhs), len(self.par...  13.5 us
  transfers between devices with their start and end apart: 46, of which 19 were waited for; matrix products, arithmetic and copies ran while one was open for 10% of the time, Pallas kernels for 32%

profile of v2, /device:TPU:0, one launch (start us, length us, event | category | flops | bytes accessed | tf_op | source)
XLA Modules:
  0.0 333.5 jit_solution(16645464544570111664)
XLA Ops:
  14.5 5.5 %collective-permute-start = (bf16[128,1024]{1,0:T(8,128)(2,1)S(1)}, bf16[128,1024]{1,0:T(8,128)(2,1)S(1)}, u32[]{:S(2)}, u32[]{:S(2)}) collective-permute-start(bf16[128,1024]{1,0:T(8,128)(2,1)S(1)} %get-tuple-element.103.refs_0_), channel_id=1, source_target_pairs={{0,2},{1,3},{2,0},{3,1},{4,6},{5,7},{6,4},{7,5},{8,10},{9,11},{10,... | collective-permute-start | bytes 786440 | tf_op jit(solution)/shard_map/ppermute | solution.py:463
  20.1 7.9 %collective-permute-done.refs_1_ = bf16[128,1024]{1,0:T(8,128)(2,1)S(1)} collective-permute-done((bf16[128,1024]{1,0:T(8,128)(2,1)S(1)}, bf16[128,1024]{1,0:T(8,128)(2,1)S(1)}, u32[]{:S(2)}, u32[]{:S(2)}) %collective-permute-start) | collective-permute-done | bytes 262176 | tf_op jit(solution)/shard_map/ppermute | solution.py:463
  28.8 3.8 %collective-permute-start.2 = (bf16[128,1024]{1,0:T(8,128)(2,1)S(1)}, bf16[128,1024]{1,0:T(8,128)(2,1)S(1)}, u32[]{:S(2)}, u32[]{:S(2)}) collective-permute-start(bf16[128,1024]{1,0:T(8,128)(2,1)S(1)} %collective-permute-done.1.refs_2_), channel_id=1, source_target_pairs={{0,2},{1,3},{2,0},{3,1},{4,6},{5,7},{6,4},{7,5},{8,10},{9,11},{10,... | collective-permute-start | bytes 786440 | tf_op jit(solution)/shard_map/ppermute | solution.py:463
  32.6 18.7 %collective-permute-start.4 = (bf16[128,1024]{1,0:T(8,128)(2,1)S(1)}, bf16[128,1024]{1,0:T(8,128)(2,1)S(1)}, u32[]{:S(2)}, u32[]{:S(2)}) collective-permute-start(bf16[128,1024]{1,0:T(8,128)(2,1)S(1)} %collective-permute-done.3.refs_4_), channel_id=1, source_target_pairs={{0,2},{1,3},{2,0},{3,1},{4,6},{5,7},{6,4},{7,5},{8,10},{9,11},{10,... | collective-permute-start | bytes 786440 | tf_op jit(solution)/shard_map/ppermute | solution.py:463
  52.4 18.0 %collective-permute-done.4.refs_5_ = bf16[128,1024]{1,0:T(8,128)(2,1)S(1)} collective-permute-done((bf16[128,1024]{1,0:T(8,128)(2,1)S(1)}, bf16[128,1024]{1,0:T(8,128)(2,1)S(1)}, u32[]{:S(2)}, u32[]{:S(2)}) %collective-permute-start.4) | collective-permute-done | bytes 262176 | tf_op jit(solution)/shard_map/ppermute | solution.py:463
  75.4 2.0 fusion.9
  79.9 1.9 copy-done.21
  81.7 7.6 %gated_forward.1 = (f32[704,1024]{1,0:T(8,128)S(1)}, f32[704,1024]{1,0:T(8,128)S(1)}, bf16[1024,704]{1,0:T(8,128)(2,1)S(1)}, bf16[704,1024]{1,0:T(8,128)(2,1)S(1)}) custom-call(bf16[1024,2048]{1,0:T(8,128)(2,1)S(1)} %copy-done.12, bf16[704,2048]{1,0:T(8,128)(2,1)S(1)} %copy-done.19, bf16[704,2048]{1,0:T(8,128)(2,1)S(1)} %copy-done.21), custom_call_target="tpu_custom_call" | custom-call | flops 11249999872 | tf_op jit(solution)/shard_map/gated_forward/pallas_call | solution.py:281
  91.2 8.6 %attend_forward.1 = (bf16[1024,256]{1,0:T(8,128)(2,1)S(1)}, bf16[1024,256]{1,0:T(8,128)(2,1)S(1)}, bf16[1024,256]{1,0:T(8,128)(2,1)S(1)}, bf16[1024,256]{1,0:T(8...) custom-call(bf16[1024,2048]{1,0:T(8,128)(2,1)S(1)} %copy-done.12, bf16[768,2048]{1,0:T(8,128)(2,1)S(1)} %bitcast.55, ...), custom_call_target="tpu_custom_call" | custom-call | flops 12750000128 | tf_op jit(solution)/shard_map/attend_forward/pallas_call | solution.py:126
  99.9 2.6 send_terms.4
  115.2 5.6 %gated_backward.1 = (bf16[1024,704]{1,0:T(8,128)(2,1)S(1)}, bf16[704,1024]{1,0:T(8,128)(2,1)S(1)}, bf16[1024,704]{1,0:T(8,128)(2,1)S(1)}, bf16[704,1024]{1,0:T(8,128)(2,1)S(1)}) custom-call(bf16[1024,1024]{1,0:T(8,128)(2,1)S(1)} %bitcast.59, bf16[1024,1024]{1,0:T(8,128)(2,1)S(1)} %copy-done.26, bf16[704,2048]{1,0:T(8,128)(2,1)S(1)} %copy-done.23, ...), custom_call_target="tpu_custom_call" | custom-call | flops 8099999744 | tf_op jit(solution)/shard_map/gated_backward/pallas_call | solution.py:322
  120.8 5.2 %send_terms.6 = (bf16[1408,512]{1,0:T(8,128)(2,1)}, bf16[1408,512]{1,0:T(8,128)(2,1)}) custom-call(s32[2]{0:T(128)S(1)} %pad_add_fusion.2.order, bf16[704,1024]{1,0:T(8,128)(2,1)S(1)} %get-tuple-element.140.refs_0_, bf16[704,1024]{1,0:T(8,128)(2,1)S(1)} %get-tuple-element.124.refs_1_, bf16[1024,2048]{1,0:T(8,128)(2,1)S(1)} %copy-done.13), custom_call_target="tpu_custom_call" | custom-call | flops 8249999872 | tf_op jit(solution)/shard_map/send_terms/pallas_call | solution.py:521
  128.1 4.4 %join_terms.3 = (bf16[960,256]{1,0:T(8,128)(2,1)}, bf16[960,256]{1,0:T(8,128)(2,1)S(1)}, bf16[960,256]{1,0:T(8,128)(2,1)}, bf16[960,256]{1,0:T(8,128)(2,1)S(1)}) custom-call(s32[3,2]{1,0:T(4,128)S(1)} %pad_add_fusion.order, bf16[704,1024]{1,0:T(8,128)(2,1)S(1)} %copy-done.37, bf16[256,1024]{1,0:T(8,128)(2,1)S(1)} %copy-done.43, ...), custom_call_target="tpu_custom_call" | custom-call | flops 5624999936 | tf_op jit(solution)/shard_map/join_terms/pallas_call | solution.py:537
  135.4 13.2 %attend_backward.1 = (bf16[1024,768]{1,0:T(8,128)(2,1)S(1)}, bf16[768,1024]{1,0:T(8,128)(2,1)S(1)}, f32[8,768]{1,0:T(8,128)S(1)}) custom-call(bf16[1024,256]{1,0:T(8,128)(2,1)S(1)} %copy-done.57, bf16[1024,256]{1,0:T(8,128)(2,1)S(1)} %copy-done.59, bf16[1024,256]{1,0:T(8,128)(2,1)S(1)} %copy-done.61, bf16[1024,1024]{1,0:T(8,128)(2,1)S(1)} %bitcast.61, ...), custom_call_target="tpu_custom_call" | custom-call | flops 19950000128 | tf_op jit(solution)/shard_map/attend_backward/pallas_call | solution.py:215
  149.7 10.4 %merge.2 = bf16[1024,2048]{1,0:T(8,128)(2,1)S(1)} custom-call(bf16[1024,704]{1,0:T(8,128)(2,1)S(1)} %get-tuple-element.135.refs_0_, bf16[1024,704]{1,0:T(8,128)(2,1)S(1)} %get-tuple-element.136.refs_1_, bf16[1024,768]{1,0:T(8,128)(2,1)S(1)} %get-tuple-element.137.refs_2_, bf16[704,2048]{1,0:T(8,128)(2,1)S(1)} %copy-done.20, ...), custom_call_target="tpu_custom_call" | custom-call | flops 12000000000 | tf_op jit(solution)/shard_map/merge/pallas_call | solution.py:344
  160.2 2.0 copy-done
  162.3 8.0 %collective-permute-done.15 = bf16[960,256]{1,0:T(8,128)(2,1)} collective-permute-done((bf16[960,256]{1,0:T(8,128)(2,1)}, bf16[960,256]{1,0:T(8,128)(2,1)}, u32[]{:S(2)}, u32[]{:S(2)}) %collective-permute-start.15) | collective-permute-done | bytes 491552 | tf_op jit(solution)/shard_map/ppermute | solution.py:547
  170.3 1.9 add.194.refs_0_
  173.6 2.0 add.195.refs_1_
  176.2 2.2 copy-done.14
  179.8 6.0 %join_terms.4 = (bf16[1408,256]{1,0:T(8,128)(2,1)}, bf16[1408,256]{1,0:T(8,128)(2,1)S(1)}, bf16[1408,256]{1,0:T(8,128)(2,1)}, bf16[1408,256]{1,0:T(8,128)(2,1)S(1)}) custom-call(s32[2,2]{1,0:T(2,128)S(1)} %pad_add_fusion.1.order, bf16[704,1024]{1,0:T(8,128)(2,1)S(1)} %copy-done.49, bf16[704,1024]{1,0:T(8,128)(2,1)S(1)} %copy-done.51, ...), custom_call_target="tpu_custom_call" | custom-call | flops 1500000026624 | tf_op jit(solution)/shard_map/join_terms/pallas_call | solution.py:537
  187.9 1.8 constant_dynamic-update-slice_fusion.1
  189.7 2.0 constant_dynamic-update-slice_fusion.3
  191.7 1.9 constant_dynamic-update-slice_fusion.2
  194.9 1.8 constant_dynamic-update-slice_fusion
  197.4 2.2 copy-done.15
  199.6 2.9 send_terms.7
  203.9 5.3 %merge.3 = bf16[1024,2048]{1,0:T(8,128)(2,1)S(1)} custom-call(bf16[1024,256]{1,0:T(8,128)(2,1)S(1)} %copy-done.55, bf16[1024,704]{1,0:T(8,128)(2,1)S(1)} %copy-done.53, bf16[256,2048]{1,0:T(8,128)(2,1)S(1)} %copy-done.28, bf16[704,2048]{1,0:T(8,128)(2,1)S(1)} %copy-done.24), custom_call_target="tpu_custom_call" | custom-call | flops 12000000000 | tf_op jit(solution)/shard_map/merge/pallas_call | solution.py:344
  209.2 2.0 copy-done.1
  211.3 11.9 %collective-permute-done.22.refs_1_ = bf16[1920,256]{1,0:T(8,128)(2,1)} collective-permute-done((bf16[1920,256]{1,0:T(8,128)(2,1)}, bf16[1920,256]{1,0:T(8,128)(2,1)}, u32[]{:S(2)}, u32[]{:S(2)}) %collective-permute-start.22) | collective-permute-done | bytes 983072 | tf_op jit(solution)/shard_map/ppermute | solution.py:559
  224.7 5.6 %place.6 = (f32[704,2048]{1,0:T(8,128)}, f32[256,2048]{1,0:T(8,128)}) custom-call(s32[8]{0:T(128)S(1)} %stack.165.order, bf16[960,256]{1,0:T(8,128)(2,1)} %add.194.refs_0_, bf16[960,256]{1,0:T(8,128)(2,1)} %add.195.refs_1_, bf16[960,256]{1,0:T(8,128)(2,1)} %collective-permute-done.19.refs_2_, bf16[960,256]{1,0:T(8,128)(2,1)} %collective-permute-done.20.refs_3_), custom_call_target="tpu_custom_call" | custom-call | flops 4915200000 | tf_op jit(solution)/shard_map/place/pallas_call | solution.py:415
  230.2 5.6 %place.7 = (f32[704,2048]{1,0:T(8,128)}, f32[256,2048]{1,0:T(8,128)}) custom-call(s32[8]{0:T(128)S(1)} %stack.160.order, bf16[1920,256]{1,0:T(8,128)(2,1)} %collective-permute-done.21.refs_0_, bf16[1920,256]{1,0:T(8,128)(2,1)} %collective-permute-done.22.refs_1_, ...), custom_call_target="tpu_custom_call", output_to_operand_aliasing={{0}: (3, {}), {1}: (4, {})} | custom-call | flops 4915200000 | tf_op jit(solution)/shard_map/place/pallas_call | solution.py:415
  235.8 2.3 add.217.refs_1_
  238.8 2.2 add.216.refs_0_
  242.3 2.3 collective-permute-done.25.refs_2_
  244.6 3.0 join_terms.5
  252.1 7.6 %collective-permute-done.27.refs_2_ = bf16[1408,256]{1,0:T(8,128)(2,1)} collective-permute-done((bf16[1408,256]{1,0:T(8,128)(2,1)}, bf16[1408,256]{1,0:T(8,128)(2,1)}, u32[]{:S(2)}, u32[]{:S(2)}) %collective-permute-start.27) | collective-permute-done | bytes 720928 | tf_op jit(solution)/shard_map/ppermute | solution.py:553
  263.6 2.0 collective-permute-done.29
  271.2 6.7 %collective-permute-done.31.refs_2_ = bf16[768,256]{1,0:T(8,128)(2,1)S(1)} collective-permute-done((bf16[768,256]{1,0:T(8,128)(2,1)S(1)}, bf16[768,256]{1,0:T(8,128)(2,1)S(1)}, u32[]{:S(2)}, u32[]{:S(2)}) %collective-permute-start.31) | collective-permute-done | bytes 393248 | tf_op jit(solution)/shard_map/ppermute | solution.py:553
  283.3 2.1 add_convert_fusion
  285.3 5.2 %place.8 = (f32[704,2048]{1,0:T(8,128)}, f32[704,2048]{1,0:T(8,128)}) custom-call(s32[4]{0:T(128)S(1)} %pad_add_fusion.4.order, bf16[1408,256]{1,0:T(8,128)(2,1)} %add.216.refs_0_, bf16[1408,256]{1,0:T(8,128)(2,1)} %add.217.refs_1_, bf16[1408,256]{1,0:T(8,128)(2,1)} %collective-permute-done.27.refs_2_, bf16[1408,256]{1,0:T(8,128)(2,1)} %collective-permute-done.28.refs_3_), custom_call_target="tpu_custom_call" | custom-call | flops 7208960000 | tf_op jit(solution)/shard_map/place/pallas_call | solution.py:415
  290.5 2.7 place.9.refs_2_
  294.4 2.2 collective-permute-start.34
  298.3 2.5 collective-permute-start.35
  303.3 2.2 collective-permute-done.40.refs_0_
  306.4 5.2 %place.10 = (f32[704,2048]{1,0:T(8,128)}, f32[704,2048]{1,0:T(8,128)}) custom-call(s32[4]{0:T(128)S(1)} %pad_add_fusion.5.order, bf16[2816,256]{1,0:T(8,128)(2,1)} %collective-permute-done.40.refs_0_, bf16[2816,256]{1,0:T(8,128)(2,1)} %collective-permute-done.41.refs_1_, ...), custom_call_target="tpu_custom_call", output_to_operand_aliasing={{0}: (3, {}), {1}: (4, {})} | custom-call | flops 7208960000 | tf_op jit(solution)/shard_map/place/pallas_call | solution.py:415
  311.6 8.3 %collective-permute-done.39.refs_1_ = bf16[1536,256]{1,0:T(8,128)(2,1)S(1)} collective-permute-done((bf16[1536,256]{1,0:T(8,128)(2,1)}, bf16[1536,256]{1,0:T(8,128)(2,1)S(1)}, u32[]{:S(2)}, u32[]{:S(2)}) %collective-permute-start.39) | collective-permute-done | bytes 786464 | tf_op jit(solution)/shard_map/ppermute | solution.py:559
  322.0 2.7 place.11
  (278 shorter events, 79.1 us)
Async XLA Ops:
  7.2 68.0 %all-gather.3.cloned.1.call-start = ((), (), s32[]{:S(2)}) async-start(), calls=%async_computation.2 | async-start | bytes 4718592 | tf_op jit(solution)/shard_map/all_gather | solution.py:663
  11.4 40.0 %copy-start.70 = (bf16[3,256]{1,0:T(4,128)(2,1)S(1)}, bf16[3,256]{1,0:T(4,128)(2,1)}, u32[]{:S(2)}) copy-start(bf16[3,256]{1,0:T(4,128)(2,1)} %param.15) | copy-start | bytes 4612
  11.4 59.1 %copy-start.31 = (s32[1,8]{1,0:T(1,128)S(1)}, s32[1,8]{1,0:T(1,128)}, u32[]{:S(2)}) copy-start(s32[1,8]{1,0:T(1,128)} %lengths.1) | copy-start | bytes 100
  13.2 92.2 %all-gather.5.cloned.1.call-start = ((), (), s32[]{:S(2)}) async-start(), calls=%async_computation.3 | async-start | bytes 2359296 | tf_op jit(solution)/shard_map/all_gather | solution.py:669
  13.3 38.6 %collective-permute-start.5 = (bf16[128,1024]{1,0:T(8,128)(2,1)S(1)}, bf16[128,1024]{1,0:T(8,128)(2,1)S(1)}, u32[]{:S(2)}, u32[]{:S(2)}) collective-permute-start(bf16[128,1024]{1,0:T(8,128)(2,1)S(1)} %get-tuple-element.103.refs_0_), channel_id=1, source_target_pairs={{0,1},{1,0},{2,3},{3,2},{4,5},{5,4},{6,7},{7,6},{8,9},{9,8},{10,11... | collective-permute-start | bytes 786440 | tf_op jit(solution)/shard_map/ppermute | solution.py:463
  13.8 15.0 %collective-permute-start.1 = (bf16[128,1024]{1,0:T(8,128)(2,1)S(1)}, bf16[128,1024]{1,0:T(8,128)(2,1)S(1)}, u32[]{:S(2)}, u32[]{:S(2)}) collective-permute-start(bf16[128,1024]{1,0:T(8,128)(2,1)S(1)} %get-tuple-element.103.refs_0_), channel_id=1, source_target_pairs={{0,0},{1,1},{2,4},{3,5},{4,2},{5,3},{6,6},{7,7},{8,8},{9,9},{10,12... | collective-permute-start | bytes 786440 | tf_op jit(solution)/shard_map/ppermute | solution.py:463
  14.5 13.6 %collective-permute-start = (bf16[128,1024]{1,0:T(8,128)(2,1)S(1)}, bf16[128,1024]{1,0:T(8,128)(2,1)S(1)}, u32[]{:S(2)}, u32[]{:S(2)}) collective-permute-start(bf16[128,1024]{1,0:T(8,128)(2,1)S(1)} %get-tuple-element.103.refs_0_), channel_id=1, source_target_pairs={{0,2},{1,3},{2,0},{3,1},{4,6},{5,7},{6,4},{7,5},{8,10},{9,11},{10,... | collective-permute-start | bytes 786440 | tf_op jit(solution)/shard_map/ppermute | solution.py:463
  28.0 4.6 %collective-permute-start.3 = (bf16[128,1024]{1,0:T(8,128)(2,1)S(1)}, bf16[128,1024]{1,0:T(8,128)(2,1)S(1)}, u32[]{:S(2)}, u32[]{:S(2)}) collective-permute-start(bf16[128,1024]{1,0:T(8,128)(2,1)S(1)} %collective-permute-done.refs_1_), channel_id=1, source_target_pairs={{0,0},{1,1},{2,4},{3,5},{4,2},{5,3},{6,6},{7,7},{8,8},{9,9},{10,12... | collective-permute-start | bytes 786440 | tf_op jit(solution)/shard_map/ppermute | solution.py:463
  28.8 23.2 %collective-permute-start.2 = (bf16[128,1024]{1,0:T(8,128)(2,1)S(1)}, bf16[128,1024]{1,0:T(8,128)(2,1)S(1)}, u32[]{:S(2)}, u32[]{:S(2)}) collective-permute-start(bf16[128,1024]{1,0:T(8,128)(2,1)S(1)} %collective-permute-done.1.refs_2_), channel_id=1, source_target_pairs={{0,2},{1,3},{2,0},{3,1},{4,6},{5,7},{6,4},{7,5},{8,10},{9,11},{10,... | collective-permute-start | bytes 786440 | tf_op jit(solution)/shard_map/ppermute | solution.py:463
  32.6 37.8 %collective-permute-start.4 = (bf16[128,1024]{1,0:T(8,128)(2,1)S(1)}, bf16[128,1024]{1,0:T(8,128)(2,1)S(1)}, u32[]{:S(2)}, u32[]{:S(2)}) collective-permute-start(bf16[128,1024]{1,0:T(8,128)(2,1)S(1)} %collective-permute-done.3.refs_4_), channel_id=1, source_target_pairs={{0,2},{1,3},{2,0},{3,1},{4,6},{5,7},{6,4},{7,5},{8,10},{9,11},{10,... | collective-permute-start | bytes 786440 | tf_op jit(solution)/shard_map/ppermute | solution.py:463
  51.4 19.7 %collective-permute-start.7 = (bf16[128,1024]{1,0:T(8,128)(2,1)S(1)}, bf16[128,1024]{1,0:T(8,128)(2,1)S(1)}, u32[]{:S(2)}, u32[]{:S(2)}) collective-permute-start(bf16[128,1024]{1,0:T(8,128)(2,1)S(1)} %collective-permute-done.1.refs_2_), channel_id=1, source_target_pairs={{0,1},{1,0},{2,3},{3,2},{4,5},{5,4},{6,7},{7,6},{8,9},{9,8},{10,11... | collective-permute-start | bytes 786440 | tf_op jit(solution)/shard_map/ppermute | solution.py:463
  51.4 19.7 %collective-permute-start.6 = (bf16[128,1024]{1,0:T(8,128)(2,1)S(1)}, bf16[128,1024]{1,0:T(8,128)(2,1)}, u32[]{:S(2)}, u32[]{:S(2)}) collective-permute-start(bf16[128,1024]{1,0:T(8,128)(2,1)S(1)} %collective-permute-done.refs_1_), channel_id=1, source_target_pairs={{0,1},{1,0},{2,3},{3,2},{4,5},{5,4},{6,7},{7,6},{8,9},{9,8},{10,11... | collective-permute-start | bytes 786440 | tf_op jit(solution)/shard_map/ppermute | solution.py:463
  51.9 19.2 %collective-permute-start.9 = (bf16[128,1024]{1,0:T(8,128)(2,1)S(1)}, bf16[128,1024]{1,0:T(8,128)(2,1)}, u32[]{:S(2)}, u32[]{:S(2)}) collective-permute-start(bf16[128,1024]{1,0:T(8,128)(2,1)S(1)} %collective-permute-done.3.refs_4_), channel_id=1, source_target_pairs={{0,1},{1,0},{2,3},{3,2},{4,5},{5,4},{6,7},{7,6},{8,9},{9,8},{10,11... | collective-permute-start | bytes 786440 | tf_op jit(solution)/shard_map/ppermute | solution.py:463
  52.0 19.1 %collective-permute-start.8 = (bf16[128,1024]{1,0:T(8,128)(2,1)S(1)}, bf16[128,1024]{1,0:T(8,128)(2,1)}, u32[]{:S(2)}, u32[]{:S(2)}) collective-permute-start(bf16[128,1024]{1,0:T(8,128)(2,1)S(1)} %collective-permute-done.2.refs_3_), channel_id=1, source_target_pairs={{0,1},{1,0},{2,3},{3,2},{4,5},{5,4},{6,7},{7,6},{8,9},{9,8},{10,11... | collective-permute-start | bytes 786440 | tf_op jit(solution)/shard_map/ppermute | solution.py:463
  70.4 1.7 collective-permute-start.10
  75.2 205.2 %reduce-scatter.5.cloned.1.call-start = ((), (), s32[]{:S(2)}) async-start(), calls=%async_computation.5 | async-start | bytes 4718592 | tf_op jit(solution)/shard_map/reduce_scatter | solution.py:721
  102.5 24.1 %collective-permute-start.11 = (bf16[960,256]{1,0:T(8,128)(2,1)}, bf16[960,256]{1,0:T(8,128)(2,1)}, u32[]{:S(2)}, u32[]{:S(2)}) collective-permute-start(bf16[960,256]{1,0:T(8,128)(2,1)} %get-tuple-element.115), channel_id=1, source_target_pairs={{0,8},{8,0},{16,24},{24,16},{1,9},{9,1},{17,25},{25,17},{2,10},{10... | collective-permute-start | bytes 1474568 | tf_op jit(solution)/shard_map/ppermute | solution.py:529
  104.0 24.1 %collective-permute-start.12 = (bf16[960,256]{1,0:T(8,128)(2,1)}, bf16[960,256]{1,0:T(8,128)(2,1)}, u32[]{:S(2)}, u32[]{:S(2)}) collective-permute-start(bf16[960,256]{1,0:T(8,128)(2,1)} %get-tuple-element.116), channel_id=1, source_target_pairs={{0,16},{16,0},{8,24},{24,8},{1,17},{17,1},{9,25},{25,9},{2,18},{18... | collective-permute-start | bytes 1474568 | tf_op jit(solution)/shard_map/ppermute | solution.py:529
  111.2 16.8 %collective-permute-start.13 = (bf16[960,256]{1,0:T(8,128)(2,1)S(1)}, bf16[960,256]{1,0:T(8,128)(2,1)S(1)}, u32[]{:S(2)}, u32[]{:S(2)}) collective-permute-start(bf16[960,256]{1,0:T(8,128)(2,1)S(1)} %get-tuple-element.118), channel_id=1, source_target_pairs={{0,8},{8,0},{16,24},{24,16},{1,9},{9,1},{17,25},{25,17},{2,10},{10... | collective-permute-start | bytes 1474568 | tf_op jit(solution)/shard_map/ppermute | solution.py:529
  111.9 16.2 %collective-permute-start.14 = (bf16[960,256]{1,0:T(8,128)(2,1)S(1)}, bf16[960,256]{1,0:T(8,128)(2,1)S(1)}, u32[]{:S(2)}, u32[]{:S(2)}) collective-permute-start(bf16[960,256]{1,0:T(8,128)(2,1)S(1)} %get-tuple-element.119), channel_id=1, source_target_pairs={{0,16},{16,0},{8,24},{24,8},{1,17},{17,1},{9,25},{25,9},{2,18},{18... | collective-permute-start | bytes 1474568 | tf_op jit(solution)/shard_map/ppermute | solution.py:529
  126.0 50.2 %collective-permute-start.17 = (bf16[1408,512]{1,0:T(8,128)(2,1)}, bf16[1408,512]{1,0:T(8,128)(2,1)}, u32[]{:S(2)}, u32[]{:S(2)}) collective-permute-start(bf16[1408,512]{1,0:T(8,128)(2,1)} %get-tuple-element.125), channel_id=1, source_target_pairs={{0,8},{8,0},{16,24},{24,16},{1,9},{9,1},{17,25},{25,17},{2,10},{10... | collective-permute-start | bytes 4325384 | tf_op jit(solution)/shard_map/ppermute | solution.py:529
  126.6 49.5 %collective-permute-start.18 = (bf16[1408,512]{1,0:T(8,128)(2,1)}, bf16[1408,512]{1,0:T(8,128)(2,1)}, u32[]{:S(2)}, u32[]{:S(2)}) collective-permute-start(bf16[1408,512]{1,0:T(8,128)(2,1)} %get-tuple-element.126), channel_id=1, source_target_pairs={{0,16},{16,0},{8,24},{24,8},{1,17},{17,1},{9,25},{25,9},{2,18},{18... | collective-permute-start | bytes 4325384 | tf_op jit(solution)/shard_map/ppermute | solution.py:529
  133.2 37.0 %collective-permute-start.15 = (bf16[960,256]{1,0:T(8,128)(2,1)}, bf16[960,256]{1,0:T(8,128)(2,1)}, u32[]{:S(2)}, u32[]{:S(2)}) collective-permute-start(bf16[960,256]{1,0:T(8,128)(2,1)} %get-tuple-element.128), channel_id=1, source_target_pairs={{0,16},{16,0},{8,24},{24,8},{1,17},{17,1},{9,25},{25,9},{2,18},{18... | collective-permute-start | bytes 1474568 | tf_op jit(solution)/shard_map/ppermute | solution.py:547
  134.4 39.2 %collective-permute-start.16 = (bf16[960,256]{1,0:T(8,128)(2,1)}, bf16[960,256]{1,0:T(8,128)(2,1)}, u32[]{:S(2)}, u32[]{:S(2)}) collective-permute-start(bf16[960,256]{1,0:T(8,128)(2,1)} %get-tuple-element.130), channel_id=1, source_target_pairs={{0,8},{8,0},{16,24},{24,16},{1,9},{9,1},{17,25},{25,17},{2,10},{10... | collective-permute-start | bytes 1474568 | tf_op jit(solution)/shard_map/ppermute | solution.py:547
  162.2 121.1 %reduce-scatter.3.cloned.1.call-start = ((), (), s32[]{:S(2)}) async-start(), calls=%async_computation.4 | async-start | bytes 4718592 | tf_op jit(solution)/shard_map/reduce_scatter | solution.py:723
  172.2 22.8 %collective-permute-start.19 = (bf16[960,256]{1,0:T(8,128)(2,1)}, bf16[960,256]{1,0:T(8,128)(2,1)}, u32[]{:S(2)}, u32[]{:S(2)}) collective-permute-start(bf16[960,256]{1,0:T(8,128)(2,1)} %add.194.refs_0_), channel_id=1, source_target_pairs={{0,16},{16,0},{8,24},{24,8},{1,17},{17,1},{9,25},{25,9},{2,18},{18... | collective-permute-start | bytes 1474568 | tf_op jit(solution)/shard_map/ppermute | solution.py:553
  175.6 16.1 %collective-permute-start.20 = (bf16[960,256]{1,0:T(8,128)(2,1)}, bf16[960,256]{1,0:T(8,128)(2,1)}, u32[]{:S(2)}, u32[]{:S(2)}) collective-permute-start(bf16[960,256]{1,0:T(8,128)(2,1)} %add.195.refs_1_), channel_id=1, source_target_pairs={{0,8},{8,0},{16,24},{24,16},{1,9},{9,1},{17,25},{25,17},{2,10},{10... | collective-permute-start | bytes 1474568 | tf_op jit(solution)/shard_map/ppermute | solution.py:553
  185.8 52.9 %collective-permute-start.23 = (bf16[1408,256]{1,0:T(8,128)(2,1)}, bf16[1408,256]{1,0:T(8,128)(2,1)}, u32[]{:S(2)}, u32[]{:S(2)}) collective-permute-start(bf16[1408,256]{1,0:T(8,128)(2,1)} %get-tuple-element.141), channel_id=1, source_target_pairs={{0,16},{16,0},{8,24},{24,8},{1,17},{17,1},{9,25},{25,9},{2,18},{18... | collective-permute-start | bytes 2162696 | tf_op jit(solution)/shard_map/ppermute | solution.py:547
  187.3 48.5 %collective-permute-start.24 = (bf16[1408,256]{1,0:T(8,128)(2,1)}, bf16[1408,256]{1,0:T(8,128)(2,1)}, u32[]{:S(2)}, u32[]{:S(2)}) collective-permute-start(bf16[1408,256]{1,0:T(8,128)(2,1)} %get-tuple-element.143), channel_id=1, source_target_pairs={{0,8},{8,0},{16,24},{24,16},{1,9},{9,1},{17,25},{25,17},{2,10},{10... | collective-permute-start | bytes 2162696 | tf_op jit(solution)/shard_map/ppermute | solution.py:547
  193.5 29.6 %collective-permute-start.22 = (bf16[1920,256]{1,0:T(8,128)(2,1)}, bf16[1920,256]{1,0:T(8,128)(2,1)}, u32[]{:S(2)}, u32[]{:S(2)}) collective-permute-start(bf16[1920,256]{1,0:T(8,128)(2,1)} %constant_dynamic-update-slice_fusion.2), channel_id=1, source_target_pairs={{0,16},{16,0},{8,24},{24,8},{1,17},{17,1},{9,25},{25,9},{2,18},{18... | collective-permute-start | bytes 2949128 | tf_op jit(solution)/shard_map/ppermute | solution.py:559
  196.8 33.4 %collective-permute-start.21 = (bf16[1920,256]{1,0:T(8,128)(2,1)}, bf16[1920,256]{1,0:T(8,128)(2,1)}, u32[]{:S(2)}, u32[]{:S(2)}) collective-permute-start(bf16[1920,256]{1,0:T(8,128)(2,1)} %constant_dynamic-update-slice_fusion), channel_id=1, source_target_pairs={{0,8},{8,0},{16,24},{24,16},{1,9},{9,1},{17,25},{25,17},{2,10},{10... | collective-permute-start | bytes 2949128 | tf_op jit(solution)/shard_map/ppermute | solution.py:559
  202.5 42.1 %collective-permute-start.25 = (bf16[768,512]{1,0:T(8,128)(2,1)}, bf16[768,512]{1,0:T(8,128)(2,1)}, u32[]{:S(2)}, u32[]{:S(2)}) collective-permute-start(bf16[768,512]{1,0:T(8,128)(2,1)} %get-tuple-element.148), channel_id=1, source_target_pairs={{0,8},{8,0},{16,24},{24,16},{1,9},{9,1},{17,25},{25,17},{2,10},{10... | collective-permute-start | bytes 2359304 | tf_op jit(solution)/shard_map/ppermute | solution.py:529
  223.2 21.4 %collective-permute-start.26 = (bf16[768,512]{1,0:T(8,128)(2,1)}, bf16[768,512]{1,0:T(8,128)(2,1)S(1)}, u32[]{:S(2)}, u32[]{:S(2)}) collective-permute-start(bf16[768,512]{1,0:T(8,128)(2,1)} %copy-done.29), channel_id=1, source_target_pairs={{0,16},{16,0},{8,24},{24,8},{1,17},{17,1},{9,25},{25,9},{2,18},{18... | collective-permute-start | bytes 2359304 | tf_op jit(solution)/shard_map/ppermute | solution.py:529
  238.2 22.6 %collective-permute-start.28 = (bf16[1408,256]{1,0:T(8,128)(2,1)}, bf16[1408,256]{1,0:T(8,128)(2,1)}, u32[]{:S(2)}, u32[]{:S(2)}) collective-permute-start(bf16[1408,256]{1,0:T(8,128)(2,1)} %add.217.refs_1_), channel_id=1, source_target_pairs={{0,8},{8,0},{16,24},{24,16},{1,9},{9,1},{17,25},{25,17},{2,10},{10... | collective-permute-start | bytes 2162696 | tf_op jit(solution)/shard_map/ppermute | solution.py:553
  240.9 18.7 %collective-permute-start.27 = (bf16[1408,256]{1,0:T(8,128)(2,1)}, bf16[1408,256]{1,0:T(8,128)(2,1)}, u32[]{:S(2)}, u32[]{:S(2)}) collective-permute-start(bf16[1408,256]{1,0:T(8,128)(2,1)} %add.216.refs_0_), channel_id=1, source_target_pairs={{0,16},{16,0},{8,24},{24,8},{1,17},{17,1},{9,25},{25,9},{2,18},{18... | collective-permute-start | bytes 2162696 | tf_op jit(solution)/shard_map/ppermute | solution.py:553
  247.6 18.0 %collective-permute-start.29 = (bf16[768,256]{1,0:T(8,128)(2,1)S(1)}, bf16[768,256]{1,0:T(8,128)(2,1)S(1)}, u32[]{:S(2)}, u32[]{:S(2)}) collective-permute-start(bf16[768,256]{1,0:T(8,128)(2,1)S(1)} %get-tuple-element.167), channel_id=1, source_target_pairs={{0,16},{16,0},{8,24},{24,8},{1,17},{17,1},{9,25},{25,9},{2,18},{18... | collective-permute-start | bytes 1179656 | tf_op jit(solution)/shard_map/ppermute | solution.py:547
  248.3 19.0 %collective-permute-start.30 = (bf16[768,256]{1,0:T(8,128)(2,1)S(1)}, bf16[768,256]{1,0:T(8,128)(2,1)S(1)}, u32[]{:S(2)}, u32[]{:S(2)}) collective-permute-start(bf16[768,256]{1,0:T(8,128)(2,1)S(1)} %get-tuple-element.168), channel_id=1, source_target_pairs={{0,8},{8,0},{16,24},{24,16},{1,9},{9,1},{17,25},{25,17},{2,10},{10... | collective-permute-start | bytes 1179656 | tf_op jit(solution)/shard_map/ppermute | solution.py:547
  265.7 12.1 %collective-permute-start.31 = (bf16[768,256]{1,0:T(8,128)(2,1)S(1)}, bf16[768,256]{1,0:T(8,128)(2,1)S(1)}, u32[]{:S(2)}, u32[]{:S(2)}) collective-permute-start(bf16[768,256]{1,0:T(8,128)(2,1)S(1)} %add.218.refs_0_), channel_id=1, source_target_pairs={{0,16},{16,0},{8,24},{24,8},{1,17},{17,1},{9,25},{25,9},{2,18},{18... | collective-permute-start | bytes 1179656 | tf_op jit(solution)/shard_map/ppermute | solution.py:553
  267.4 12.1 %collective-permute-start.32 = (bf16[768,256]{1,0:T(8,128)(2,1)S(1)}, bf16[768,256]{1,0:T(8,128)(2,1)S(1)}, u32[]{:S(2)}, u32[]{:S(2)}) collective-permute-start(bf16[768,256]{1,0:T(8,128)(2,1)S(1)} %add.219.refs_1_), channel_id=1, source_target_pairs={{0,8},{8,0},{16,24},{24,16},{1,9},{9,1},{17,25},{25,17},{2,10},{10... | collective-permute-start | bytes 1179656 | tf_op jit(solution)/shard_map/ppermute | solution.py:553
  268.2 35.1 %collective-permute-start.41 = (bf16[2816,256]{1,0:T(8,128)(2,1)}, bf16[2816,256]{1,0:T(8,128)(2,1)}, u32[]{:S(2)}, u32[]{:S(2)}) collective-permute-start(bf16[2816,256]{1,0:T(8,128)(2,1)} %copy-done.65), channel_id=1, source_target_pairs={{0,16},{16,0},{8,24},{24,8},{1,17},{17,1},{9,25},{25,9},{2,18},{18... | collective-permute-start | bytes 4325384 | tf_op jit(solution)/shard_map/ppermute | solution.py:559
  269.7 35.8 %collective-permute-start.40 = (bf16[2816,256]{1,0:T(8,128)(2,1)}, bf16[2816,256]{1,0:T(8,128)(2,1)}, u32[]{:S(2)}, u32[]{:S(2)}) collective-permute-start(bf16[2816,256]{1,0:T(8,128)(2,1)} %copy-done.66), channel_id=1, source_target_pairs={{0,8},{8,0},{16,24},{24,16},{1,9},{9,1},{17,25},{25,17},{2,10},{10... | collective-permute-start | bytes 4325384 | tf_op jit(solution)/shard_map/ppermute | solution.py:559
  293.2 1.2 collective-permute-start.33
  294.4 3.9 %collective-permute-start.34 = (f32[4096]{0:T(1024)S(1)}, f32[4096]{0:T(1024)S(1)}, u32[]{:S(2)}, u32[]{:S(2)}) collective-permute-start(f32[4096]{0:T(1024)S(1)} %add.220), channel_id=1, source_target_pairs={{0,2},{1,3},{2,0},{3,1},{4,6},{5,7},{6,4},{7,5},{8,10},{9,11},{10,... | collective-permute-start | bytes 49160 | tf_op jit(solution)/shard_map/ppermute | solution.py:588
  298.3 4.7 %collective-permute-start.35 = (f32[4096]{0:T(1024)S(1)}, f32[4096]{0:T(1024)S(1)}, u32[]{:S(2)}, u32[]{:S(2)}) collective-permute-start(f32[4096]{0:T(1024)S(1)} %add.221), channel_id=1, source_target_pairs={{0,4},{1,5},{2,6},{3,7},{4,0},{5,1},{6,2},{7,3},{8,12},{9,13},{10,... | collective-permute-start | bytes 49160 | tf_op jit(solution)/shard_map/ppermute | solution.py:588
  300.8 19.1 %collective-permute-start.39 = (bf16[1536,256]{1,0:T(8,128)(2,1)}, bf16[1536,256]{1,0:T(8,128)(2,1)S(1)}, u32[]{:S(2)}, u32[]{:S(2)}) collective-permute-start(bf16[1536,256]{1,0:T(8,128)(2,1)} %constant_dynamic-update-slice_fusion.10), channel_id=1, source_target_pairs={{0,16},{16,0},{8,24},{24,8},{1,17},{17,1},{9,25},{25,9},{2,18},{18... | collective-permute-start | bytes 2359304 | tf_op jit(solution)/shard_map/ppermute | solution.py:559
  301.5 19.8 %collective-permute-start.38 = (bf16[1536,256]{1,0:T(8,128)(2,1)S(1)}, bf16[1536,256]{1,0:T(8,128)(2,1)S(1)}, u32[]{:S(2)}, u32[]{:S(2)}) collective-permute-start(bf16[1536,256]{1,0:T(8,128)(2,1)S(1)} %copy-done.68), channel_id=1, source_target_pairs={{0,8},{8,0},{16,24},{24,16},{1,9},{9,1},{17,25},{25,17},{2,10},{10... | collective-permute-start | bytes 2359304 | tf_op jit(solution)/shard_map/ppermute | solution.py:559
  305.5 16.0 %collective-permute-start.36 = (f32[4864]{0:T(1024)S(1)}, f32[4864]{0:T(1024)S(1)}, u32[]{:S(2)}, u32[]{:S(2)}) collective-permute-start(f32[4864]{0:T(1024)S(1)} %pad_maximum_fusion.1), channel_id=1, source_target_pairs={{0,8},{8,0},{16,24},{24,16},{1,9},{9,1},{17,25},{25,17},{2,10},{10... | collective-permute-start | bytes 58376 | tf_op jit(solution)/shard_map/ppermute | solution.py:588
  321.5 3.8 %collective-permute-start.37 = (f32[4864]{0:T(1024)S(1)}, f32[4864]{0:T(1024)S(1)}, u32[]{:S(2)}, u32[]{:S(2)}) collective-permute-start(f32[4864]{0:T(1024)S(1)} %fusion.19), channel_id=1, source_target_pairs={{0,16},{8,24},{16,0},{24,8},{1,17},{9,25},{17,1},{25,9},{2,18},{10... | collective-permute-start | bytes 58376 | tf_op jit(solution)/shard_map/ppermute | solution.py:588
  (70 other events, 369.6 us)
Sparse Core Ops, SparseCore 0:
  13.3 59.7 all-gather.2
  75.3 28.4 all-gather.4
  162.3 47.9 reduce-scatter.4
  213.1 48.1 reduce-scatter.2

commit v3 on v2

--- a/solution.py
+++ b/solution.py
@@ -452,7 +452,7 @@
                 copy.wait()
 
 
-def gather(values):
+def gather(values, ready):
     line = [(2 * i + c, 2 * (i ^ 1) + c) for i in range(4) for c in range(2)]
     middle = [(2 * i + c, 2 * j + c) for i, j in ((0, 0), (1, 2), (2, 1), (3, 3)) for c in range(2)]
     core = [(i, i ^ 1) for i in range(8)]
@@ -466,6 +466,7 @@
     across = move(values, middle)
     far = move(across, line)
     beyond = move(near, middle)
+    beyond = after(beyond, ready)
     last = move(beyond, line)
     mine = [values, near, across, far, beyond, last]
     theirs = [move(pieces, core) for pieces in mine]
@@ -660,9 +661,12 @@
     normed, inverse, normed_low, left_mine, right_mine = norm(
         first[None].astype(jnp.int32), doc_lengths, block_input, norm_gain, norm_bias, cotangent
     )
+    tables = turns(position)
+    seg_col = jnp.broadcast_to(segment[:, None], (tokens, 128))
+    seg_row = jnp.broadcast_to(segment[None, :], (8, tokens))
     hidden_in = lax.all_gather(normed_low, "tp", axis=0, tiled=True)
     if group == 8:
-        grad_left = gather(left_mine)
+        grad_left = gather(left_mine, position)
         hidden_in = after(hidden_in, grad_left)
     else:
         grad_left = lax.all_gather(after(left_mine, hidden_in), "tp", axis=0, tiled=True)
@@ -671,10 +675,6 @@
     live_mine = lax.dynamic_slice_in_dim(live, first, shard)[:, None]
     input_wide = block_input.astype(jnp.float32)
     gain = norm_gain.astype(jnp.float32)
-    tables = turns(position)
-    seg_col = jnp.broadcast_to(segment[:, None], (tokens, 128))
-    seg_row = jnp.broadcast_to(segment[None, :], (8, tokens))
-
     projection = widen(qkv_weight, padded).reshape(3 * padded, features)
     shift_lines = widen(qkv_bias[..., None], padded).reshape(1, 3 * padded).astype(jnp.float32)
     out_wide = widen(out_weight[None], padded)[0]

time: 340 us -> 340 us (level)
  no operation moved by 1% of the time
where the time goes in v3:
time: 340 us; the launch traced here: 333 us
  Pallas kernels  107 us (31%)
  waiting for transfers between devices  84.2 us (25%)
  starting transfers between devices  63.6 us (19%)
  local copies, waits for them, and re-layouts  46.7 us (14%)
  other arithmetic  17 us (5%)
  between operations  15 us (4%)
    unnamed x151, local copies, waits for them, and re-layouts  36 us
    ppermute x11, starting transfers between devices, move(): return lax.ppermute(pieces, 'tp', pairs)  30.8 us
    pallas_call x6, Pallas kernels, place(): pl.pallas_call(functools.partial(place_kernel, takes, len(old)), grid_spe...  27 us
    ppermute x11, waiting for transfers between devices, move(): return lax.ppermute(pieces, 'tp', pairs)  27 us
    ppermute x6, waiting for transfers between devices, share(): lax.ppermute(both[half], 'rows', PATHS[half][0])  24.1 us
    ppermute x6, waiting for transfers between devices, total(): lax.ppermute(self.mine[half], 'rows', PATHS[half][1])  15.9 us
    pallas_call x2, Pallas kernels, merge(): pl.pallas_call(functools.partial(merge_kernel, count), grid=(tokens // bl...  15.7 us
    pallas_call x3, Pallas kernels, join(): pl.pallas_call(functools.partial(join_kernel, len(self.lhs), len(self.par...  13.5 us
  transfers between devices with their start and end apart: 46, of which 19 were waited for; matrix products, arithmetic and copies ran while one was open for 10% of the time, Pallas kernels for 32%

profile of v3, /device:TPU:0, one launch (start us, length us, event | category | flops | bytes accessed | tf_op | source)
XLA Modules:
  0.0 333.5 jit_solution(16645464544570111664)
XLA Ops:
  14.5 5.5 %collective-permute-start = (bf16[128,1024]{1,0:T(8,128)(2,1)S(1)}, bf16[128,1024]{1,0:T(8,128)(2,1)S(1)}, u32[]{:S(2)}, u32[]{:S(2)}) collective-permute-start(bf16[128,1024]{1,0:T(8,128)(2,1)S(1)} %get-tuple-element.103.refs_0_), channel_id=1, source_target_pairs={{0,2},{1,3},{2,0},{3,1},{4,6},{5,7},{6,4},{7,5},{8,10},{9,11},{10,... | collective-permute-start | bytes 786440 | tf_op jit(solution)/shard_map/ppermute | solution.py:463
  20.1 7.9 %collective-permute-done.refs_1_ = bf16[128,1024]{1,0:T(8,128)(2,1)S(1)} collective-permute-done((bf16[128,1024]{1,0:T(8,128)(2,1)S(1)}, bf16[128,1024]{1,0:T(8,128)(2,1)S(1)}, u32[]{:S(2)}, u32[]{:S(2)}) %collective-permute-start) | collective-permute-done | bytes 262176 | tf_op jit(solution)/shard_map/ppermute | solution.py:463
  28.8 3.8 %collective-permute-start.2 = (bf16[128,1024]{1,0:T(8,128)(2,1)S(1)}, bf16[128,1024]{1,0:T(8,128)(2,1)S(1)}, u32[]{:S(2)}, u32[]{:S(2)}) collective-permute-start(bf16[128,1024]{1,0:T(8,128)(2,1)S(1)} %collective-permute-done.1.refs_2_), channel_id=1, source_target_pairs={{0,2},{1,3},{2,0},{3,1},{4,6},{5,7},{6,4},{7,5},{8,10},{9,11},{10,... | collective-permute-start | bytes 786440 | tf_op jit(solution)/shard_map/ppermute | solution.py:463
  32.6 18.7 %collective-permute-start.4 = (bf16[128,1024]{1,0:T(8,128)(2,1)S(1)}, bf16[128,1024]{1,0:T(8,128)(2,1)S(1)}, u32[]{:S(2)}, u32[]{:S(2)}) collective-permute-start(bf16[128,1024]{1,0:T(8,128)(2,1)S(1)} %collective-permute-done.3.refs_4_), channel_id=1, source_target_pairs={{0,2},{1,3},{2,0},{3,1},{4,6},{5,7},{6,4},{7,5},{8,10},{9,11},{10,... | collective-permute-start | bytes 786440 | tf_op jit(solution)/shard_map/ppermute | solution.py:463
  52.4 18.0 %collective-permute-done.4.refs_5_ = bf16[128,1024]{1,0:T(8,128)(2,1)S(1)} collective-permute-done((bf16[128,1024]{1,0:T(8,128)(2,1)S(1)}, bf16[128,1024]{1,0:T(8,128)(2,1)S(1)}, u32[]{:S(2)}, u32[]{:S(2)}) %collective-permute-start.4) | collective-permute-done | bytes 262176 | tf_op jit(solution)/shard_map/ppermute | solution.py:463
  75.4 2.0 fusion.9
  79.9 1.9 copy-done.21
  81.7 7.6 %gated_forward.1 = (f32[704,1024]{1,0:T(8,128)S(1)}, f32[704,1024]{1,0:T(8,128)S(1)}, bf16[1024,704]{1,0:T(8,128)(2,1)S(1)}, bf16[704,1024]{1,0:T(8,128)(2,1)S(1)}) custom-call(bf16[1024,2048]{1,0:T(8,128)(2,1)S(1)} %copy-done.12, bf16[704,2048]{1,0:T(8,128)(2,1)S(1)} %copy-done.19, bf16[704,2048]{1,0:T(8,128)(2,1)S(1)} %copy-done.21), custom_call_target="tpu_custom_call" | custom-call | flops 11249999872 | tf_op jit(solution)/shard_map/gated_forward/pallas_call | solution.py:281
  91.2 8.6 %attend_forward.1 = (bf16[1024,256]{1,0:T(8,128)(2,1)S(1)}, bf16[1024,256]{1,0:T(8,128)(2,1)S(1)}, bf16[1024,256]{1,0:T(8,128)(2,1)S(1)}, bf16[1024,256]{1,0:T(8...) custom-call(bf16[1024,2048]{1,0:T(8,128)(2,1)S(1)} %copy-done.12, bf16[768,2048]{1,0:T(8,128)(2,1)S(1)} %bitcast.55, ...), custom_call_target="tpu_custom_call" | custom-call | flops 12750000128 | tf_op jit(solution)/shard_map/attend_forward/pallas_call | solution.py:126
  99.9 2.6 send_terms.4
  115.2 5.6 %gated_backward.1 = (bf16[1024,704]{1,0:T(8,128)(2,1)S(1)}, bf16[704,1024]{1,0:T(8,128)(2,1)S(1)}, bf16[1024,704]{1,0:T(8,128)(2,1)S(1)}, bf16[704,1024]{1,0:T(8,128)(2,1)S(1)}) custom-call(bf16[1024,1024]{1,0:T(8,128)(2,1)S(1)} %bitcast.59, bf16[1024,1024]{1,0:T(8,128)(2,1)S(1)} %copy-done.26, bf16[704,2048]{1,0:T(8,128)(2,1)S(1)} %copy-done.23, ...), custom_call_target="tpu_custom_call" | custom-call | flops 8099999744 | tf_op jit(solution)/shard_map/gated_backward/pallas_call | solution.py:322
  120.8 5.2 %send_terms.6 = (bf16[1408,512]{1,0:T(8,128)(2,1)}, bf16[1408,512]{1,0:T(8,128)(2,1)}) custom-call(s32[2]{0:T(128)S(1)} %pad_add_fusion.2.order, bf16[704,1024]{1,0:T(8,128)(2,1)S(1)} %get-tuple-element.140.refs_0_, bf16[704,1024]{1,0:T(8,128)(2,1)S(1)} %get-tuple-element.124.refs_1_, bf16[1024,2048]{1,0:T(8,128)(2,1)S(1)} %copy-done.13), custom_call_target="tpu_custom_call" | custom-call | flops 8249999872 | tf_op jit(solution)/shard_map/send_terms/pallas_call | solution.py:522
  128.1 4.4 %join_terms.3 = (bf16[960,256]{1,0:T(8,128)(2,1)}, bf16[960,256]{1,0:T(8,128)(2,1)S(1)}, bf16[960,256]{1,0:T(8,128)(2,1)}, bf16[960,256]{1,0:T(8,128)(2,1)S(1)}) custom-call(s32[3,2]{1,0:T(4,128)S(1)} %pad_add_fusion.order, bf16[704,1024]{1,0:T(8,128)(2,1)S(1)} %copy-done.37, bf16[256,1024]{1,0:T(8,128)(2,1)S(1)} %copy-done.43, ...), custom_call_target="tpu_custom_call" | custom-call | flops 5624999936 | tf_op jit(solution)/shard_map/join_terms/pallas_call | solution.py:538
  135.4 13.2 %attend_backward.1 = (bf16[1024,768]{1,0:T(8,128)(2,1)S(1)}, bf16[768,1024]{1,0:T(8,128)(2,1)S(1)}, f32[8,768]{1,0:T(8,128)S(1)}) custom-call(bf16[1024,256]{1,0:T(8,128)(2,1)S(1)} %copy-done.57, bf16[1024,256]{1,0:T(8,128)(2,1)S(1)} %copy-done.59, bf16[1024,256]{1,0:T(8,128)(2,1)S(1)} %copy-done.61, bf16[1024,1024]{1,0:T(8,128)(2,1)S(1)} %bitcast.61, ...), custom_call_target="tpu_custom_call" | custom-call | flops 19950000128 | tf_op jit(solution)/shard_map/attend_backward/pallas_call | solution.py:215
  149.7 10.4 %merge.2 = bf16[1024,2048]{1,0:T(8,128)(2,1)S(1)} custom-call(bf16[1024,704]{1,0:T(8,128)(2,1)S(1)} %get-tuple-element.135.refs_0_, bf16[1024,704]{1,0:T(8,128)(2,1)S(1)} %get-tuple-element.136.refs_1_, bf16[1024,768]{1,0:T(8,128)(2,1)S(1)} %get-tuple-element.137.refs_2_, bf16[704,2048]{1,0:T(8,128)(2,1)S(1)} %copy-done.20, ...), custom_call_target="tpu_custom_call" | custom-call | flops 12000000000 | tf_op jit(solution)/shard_map/merge/pallas_call | solution.py:344
  160.2 2.0 copy-done
  162.3 8.0 %collective-permute-done.15 = bf16[960,256]{1,0:T(8,128)(2,1)} collective-permute-done((bf16[960,256]{1,0:T(8,128)(2,1)}, bf16[960,256]{1,0:T(8,128)(2,1)}, u32[]{:S(2)}, u32[]{:S(2)}) %collective-permute-start.15) | collective-permute-done | bytes 491552 | tf_op jit(solution)/shard_map/ppermute | solution.py:548
  170.3 1.9 add.194.refs_0_
  173.6 2.0 add.195.refs_1_
  176.2 2.2 copy-done.14
  179.8 6.0 %join_terms.4 = (bf16[1408,256]{1,0:T(8,128)(2,1)}, bf16[1408,256]{1,0:T(8,128)(2,1)S(1)}, bf16[1408,256]{1,0:T(8,128)(2,1)}, bf16[1408,256]{1,0:T(8,128)(2,1)S(1)}) custom-call(s32[2,2]{1,0:T(2,128)S(1)} %pad_add_fusion.1.order, bf16[704,1024]{1,0:T(8,128)(2,1)S(1)} %copy-done.49, bf16[704,1024]{1,0:T(8,128)(2,1)S(1)} %copy-done.51, ...), custom_call_target="tpu_custom_call" | custom-call | flops 1500000026624 | tf_op jit(solution)/shard_map/join_terms/pallas_call | solution.py:538
  187.9 1.8 constant_dynamic-update-slice_fusion.1
  189.7 2.0 constant_dynamic-update-slice_fusion.3
  191.7 1.9 constant_dynamic-update-slice_fusion.2
  194.9 1.8 constant_dynamic-update-slice_fusion
  197.4 2.2 copy-done.15
  199.6 2.9 send_terms.7
  203.9 5.3 %merge.3 = bf16[1024,2048]{1,0:T(8,128)(2,1)S(1)} custom-call(bf16[1024,256]{1,0:T(8,128)(2,1)S(1)} %copy-done.55, bf16[1024,704]{1,0:T(8,128)(2,1)S(1)} %copy-done.53, bf16[256,2048]{1,0:T(8,128)(2,1)S(1)} %copy-done.28, bf16[704,2048]{1,0:T(8,128)(2,1)S(1)} %copy-done.24), custom_call_target="tpu_custom_call" | custom-call | flops 12000000000 | tf_op jit(solution)/shard_map/merge/pallas_call | solution.py:344
  209.2 2.0 copy-done.1
  211.3 11.9 %collective-permute-done.22.refs_1_ = bf16[1920,256]{1,0:T(8,128)(2,1)} collective-permute-done((bf16[1920,256]{1,0:T(8,128)(2,1)}, bf16[1920,256]{1,0:T(8,128)(2,1)}, u32[]{:S(2)}, u32[]{:S(2)}) %collective-permute-start.22) | collective-permute-done | bytes 983072 | tf_op jit(solution)/shard_map/ppermute | solution.py:560
  224.7 5.6 %place.6 = (f32[704,2048]{1,0:T(8,128)}, f32[256,2048]{1,0:T(8,128)}) custom-call(s32[8]{0:T(128)S(1)} %stack.165.order, bf16[960,256]{1,0:T(8,128)(2,1)} %add.194.refs_0_, bf16[960,256]{1,0:T(8,128)(2,1)} %add.195.refs_1_, bf16[960,256]{1,0:T(8,128)(2,1)} %collective-permute-done.19.refs_2_, bf16[960,256]{1,0:T(8,128)(2,1)} %collective-permute-done.20.refs_3_), custom_call_target="tpu_custom_call" | custom-call | flops 4915200000 | tf_op jit(solution)/shard_map/place/pallas_call | solution.py:415
  230.2 5.6 %place.7 = (f32[704,2048]{1,0:T(8,128)}, f32[256,2048]{1,0:T(8,128)}) custom-call(s32[8]{0:T(128)S(1)} %stack.160.order, bf16[1920,256]{1,0:T(8,128)(2,1)} %collective-permute-done.21.refs_0_, bf16[1920,256]{1,0:T(8,128)(2,1)} %collective-permute-done.22.refs_1_, ...), custom_call_target="tpu_custom_call", output_to_operand_aliasing={{0}: (3, {}), {1}: (4, {})} | custom-call | flops 4915200000 | tf_op jit(solution)/shard_map/place/pallas_call | solution.py:415
  235.8 2.3 add.217.refs_1_
  238.8 2.2 add.216.refs_0_
  242.3 2.3 collective-permute-done.25.refs_2_
  244.6 3.0 join_terms.5
  252.1 7.6 %collective-permute-done.27.refs_2_ = bf16[1408,256]{1,0:T(8,128)(2,1)} collective-permute-done((bf16[1408,256]{1,0:T(8,128)(2,1)}, bf16[1408,256]{1,0:T(8,128)(2,1)}, u32[]{:S(2)}, u32[]{:S(2)}) %collective-permute-start.27) | collective-permute-done | bytes 720928 | tf_op jit(solution)/shard_map/ppermute | solution.py:554
  263.6 2.0 collective-permute-done.29
  271.2 6.7 %collective-permute-done.31.refs_2_ = bf16[768,256]{1,0:T(8,128)(2,1)S(1)} collective-permute-done((bf16[768,256]{1,0:T(8,128)(2,1)S(1)}, bf16[768,256]{1,0:T(8,128)(2,1)S(1)}, u32[]{:S(2)}, u32[]{:S(2)}) %collective-permute-start.31) | collective-permute-done | bytes 393248 | tf_op jit(solution)/shard_map/ppermute | solution.py:554
  283.3 2.1 add_convert_fusion
  285.3 5.2 %place.8 = (f32[704,2048]{1,0:T(8,128)}, f32[704,2048]{1,0:T(8,128)}) custom-call(s32[4]{0:T(128)S(1)} %pad_add_fusion.4.order, bf16[1408,256]{1,0:T(8,128)(2,1)} %add.216.refs_0_, bf16[1408,256]{1,0:T(8,128)(2,1)} %add.217.refs_1_, bf16[1408,256]{1,0:T(8,128)(2,1)} %collective-permute-done.27.refs_2_, bf16[1408,256]{1,0:T(8,128)(2,1)} %collective-permute-done.28.refs_3_), custom_call_target="tpu_custom_call" | custom-call | flops 7208960000 | tf_op jit(solution)/shard_map/place/pallas_call | solution.py:415
  290.5 2.7 place.9.refs_2_
  294.4 2.2 collective-permute-start.34
  298.3 2.5 collective-permute-start.35
  303.3 2.2 collective-permute-done.40.refs_0_
  306.4 5.2 %place.10 = (f32[704,2048]{1,0:T(8,128)}, f32[704,2048]{1,0:T(8,128)}) custom-call(s32[4]{0:T(128)S(1)} %pad_add_fusion.5.order, bf16[2816,256]{1,0:T(8,128)(2,1)} %collective-permute-done.40.refs_0_, bf16[2816,256]{1,0:T(8,128)(2,1)} %collective-permute-done.41.refs_1_, ...), custom_call_target="tpu_custom_call", output_to_operand_aliasing={{0}: (3, {}), {1}: (4, {})} | custom-call | flops 7208960000 | tf_op jit(solution)/shard_map/place/pallas_call | solution.py:415
  311.6 8.3 %collective-permute-done.39.refs_1_ = bf16[1536,256]{1,0:T(8,128)(2,1)S(1)} collective-permute-done((bf16[1536,256]{1,0:T(8,128)(2,1)}, bf16[1536,256]{1,0:T(8,128)(2,1)S(1)}, u32[]{:S(2)}, u32[]{:S(2)}) %collective-permute-start.39) | collective-permute-done | bytes 786464 | tf_op jit(solution)/shard_map/ppermute | solution.py:560
  322.0 2.7 place.11
  (278 shorter events, 79.1 us)
Async XLA Ops:
  7.2 68.0 %all-gather.3.cloned.1.call-start = ((), (), s32[]{:S(2)}) async-start(), calls=%async_computation.2 | async-start | bytes 4718592 | tf_op jit(solution)/shard_map/all_gather | solution.py:667
  11.4 40.0 %copy-start.70 = (bf16[3,256]{1,0:T(4,128)(2,1)S(1)}, bf16[3,256]{1,0:T(4,128)(2,1)}, u32[]{:S(2)}) copy-start(bf16[3,256]{1,0:T(4,128)(2,1)} %param.15) | copy-start | bytes 4612
  11.4 59.1 %copy-start.31 = (s32[1,8]{1,0:T(1,128)S(1)}, s32[1,8]{1,0:T(1,128)}, u32[]{:S(2)}) copy-start(s32[1,8]{1,0:T(1,128)} %lengths.1) | copy-start | bytes 100
  13.2 92.2 %all-gather.5.cloned.1.call-start = ((), (), s32[]{:S(2)}) async-start(), calls=%async_computation.3 | async-start | bytes 2359296 | tf_op jit(solution)/shard_map/all_gather | solution.py:673
  13.3 38.6 %collective-permute-start.5 = (bf16[128,1024]{1,0:T(8,128)(2,1)S(1)}, bf16[128,1024]{1,0:T(8,128)(2,1)S(1)}, u32[]{:S(2)}, u32[]{:S(2)}) collective-permute-start(bf16[128,1024]{1,0:T(8,128)(2,1)S(1)} %get-tuple-element.103.refs_0_), channel_id=1, source_target_pairs={{0,1},{1,0},{2,3},{3,2},{4,5},{5,4},{6,7},{7,6},{8,9},{9,8},{10,11... | collective-permute-start | bytes 786440 | tf_op jit(solution)/shard_map/ppermute | solution.py:463
  13.8 15.0 %collective-permute-start.1 = (bf16[128,1024]{1,0:T(8,128)(2,1)S(1)}, bf16[128,1024]{1,0:T(8,128)(2,1)S(1)}, u32[]{:S(2)}, u32[]{:S(2)}) collective-permute-start(bf16[128,1024]{1,0:T(8,128)(2,1)S(1)} %get-tuple-element.103.refs_0_), channel_id=1, source_target_pairs={{0,0},{1,1},{2,4},{3,5},{4,2},{5,3},{6,6},{7,7},{8,8},{9,9},{10,12... | collective-permute-start | bytes 786440 | tf_op jit(solution)/shard_map/ppermute | solution.py:463
  14.5 13.6 %collective-permute-start = (bf16[128,1024]{1,0:T(8,128)(2,1)S(1)}, bf16[128,1024]{1,0:T(8,128)(2,1)S(1)}, u32[]{:S(2)}, u32[]{:S(2)}) collective-permute-start(bf16[128,1024]{1,0:T(8,128)(2,1)S(1)} %get-tuple-element.103.refs_0_), channel_id=1, source_target_pairs={{0,2},{1,3},{2,0},{3,1},{4,6},{5,7},{6,4},{7,5},{8,10},{9,11},{10,... | collective-permute-start | bytes 786440 | tf_op jit(solution)/shard_map/ppermute | solution.py:463
  28.0 4.6 %collective-permute-start.3 = (bf16[128,1024]{1,0:T(8,128)(2,1)S(1)}, bf16[128,1024]{1,0:T(8,128)(2,1)S(1)}, u32[]{:S(2)}, u32[]{:S(2)}) collective-permute-start(bf16[128,1024]{1,0:T(8,128)(2,1)S(1)} %collective-permute-done.refs_1_), channel_id=1, source_target_pairs={{0,0},{1,1},{2,4},{3,5},{4,2},{5,3},{6,6},{7,7},{8,8},{9,9},{10,12... | collective-permute-start | bytes 786440 | tf_op jit(solution)/shard_map/ppermute | solution.py:463
  28.8 23.2 %collective-permute-start.2 = (bf16[128,1024]{1,0:T(8,128)(2,1)S(1)}, bf16[128,1024]{1,0:T(8,128)(2,1)S(1)}, u32[]{:S(2)}, u32[]{:S(2)}) collective-permute-start(bf16[128,1024]{1,0:T(8,128)(2,1)S(1)} %collective-permute-done.1.refs_2_), channel_id=1, source_target_pairs={{0,2},{1,3},{2,0},{3,1},{4,6},{5,7},{6,4},{7,5},{8,10},{9,11},{10,... | collective-permute-start | bytes 786440 | tf_op jit(solution)/shard_map/ppermute | solution.py:463
  32.6 37.8 %collective-permute-start.4 = (bf16[128,1024]{1,0:T(8,128)(2,1)S(1)}, bf16[128,1024]{1,0:T(8,128)(2,1)S(1)}, u32[]{:S(2)}, u32[]{:S(2)}) collective-permute-start(bf16[128,1024]{1,0:T(8,128)(2,1)S(1)} %collective-permute-done.3.refs_4_), channel_id=1, source_target_pairs={{0,2},{1,3},{2,0},{3,1},{4,6},{5,7},{6,4},{7,5},{8,10},{9,11},{10,... | collective-permute-start | bytes 786440 | tf_op jit(solution)/shard_map/ppermute | solution.py:463
  51.4 19.7 %collective-permute-start.7 = (bf16[128,1024]{1,0:T(8,128)(2,1)S(1)}, bf16[128,1024]{1,0:T(8,128)(2,1)S(1)}, u32[]{:S(2)}, u32[]{:S(2)}) collective-permute-start(bf16[128,1024]{1,0:T(8,128)(2,1)S(1)} %collective-permute-done.1.refs_2_), channel_id=1, source_target_pairs={{0,1},{1,0},{2,3},{3,2},{4,5},{5,4},{6,7},{7,6},{8,9},{9,8},{10,11... | collective-permute-start | bytes 786440 | tf_op jit(solution)/shard_map/ppermute | solution.py:463
  51.4 19.7 %collective-permute-start.6 = (bf16[128,1024]{1,0:T(8,128)(2,1)S(1)}, bf16[128,1024]{1,0:T(8,128)(2,1)}, u32[]{:S(2)}, u32[]{:S(2)}) collective-permute-start(bf16[128,1024]{1,0:T(8,128)(2,1)S(1)} %collective-permute-done.refs_1_), channel_id=1, source_target_pairs={{0,1},{1,0},{2,3},{3,2},{4,5},{5,4},{6,7},{7,6},{8,9},{9,8},{10,11... | collective-permute-start | bytes 786440 | tf_op jit(solution)/shard_map/ppermute | solution.py:463
  51.9 19.2 %collective-permute-start.9 = (bf16[128,1024]{1,0:T(8,128)(2,1)S(1)}, bf16[128,1024]{1,0:T(8,128)(2,1)}, u32[]{:S(2)}, u32[]{:S(2)}) collective-permute-start(bf16[128,1024]{1,0:T(8,128)(2,1)S(1)} %collective-permute-done.3.refs_4_), channel_id=1, source_target_pairs={{0,1},{1,0},{2,3},{3,2},{4,5},{5,4},{6,7},{7,6},{8,9},{9,8},{10,11... | collective-permute-start | bytes 786440 | tf_op jit(solution)/shard_map/ppermute | solution.py:463
  52.0 19.1 %collective-permute-start.8 = (bf16[128,1024]{1,0:T(8,128)(2,1)S(1)}, bf16[128,1024]{1,0:T(8,128)(2,1)}, u32[]{:S(2)}, u32[]{:S(2)}) collective-permute-start(bf16[128,1024]{1,0:T(8,128)(2,1)S(1)} %collective-permute-done.2.refs_3_), channel_id=1, source_target_pairs={{0,1},{1,0},{2,3},{3,2},{4,5},{5,4},{6,7},{7,6},{8,9},{9,8},{10,11... | collective-permute-start | bytes 786440 | tf_op jit(solution)/shard_map/ppermute | solution.py:463
  70.4 1.7 collective-permute-start.10
  75.2 205.2 %reduce-scatter.5.cloned.1.call-start = ((), (), s32[]{:S(2)}) async-start(), calls=%async_computation.5 | async-start | bytes 4718592 | tf_op jit(solution)/shard_map/reduce_scatter | solution.py:721
  102.5 24.1 %collective-permute-start.11 = (bf16[960,256]{1,0:T(8,128)(2,1)}, bf16[960,256]{1,0:T(8,128)(2,1)}, u32[]{:S(2)}, u32[]{:S(2)}) collective-permute-start(bf16[960,256]{1,0:T(8,128)(2,1)} %get-tuple-element.115), channel_id=1, source_target_pairs={{0,8},{8,0},{16,24},{24,16},{1,9},{9,1},{17,25},{25,17},{2,10},{10... | collective-permute-start | bytes 1474568 | tf_op jit(solution)/shard_map/ppermute | solution.py:530
  104.0 24.1 %collective-permute-start.12 = (bf16[960,256]{1,0:T(8,128)(2,1)}, bf16[960,256]{1,0:T(8,128)(2,1)}, u32[]{:S(2)}, u32[]{:S(2)}) collective-permute-start(bf16[960,256]{1,0:T(8,128)(2,1)} %get-tuple-element.116), channel_id=1, source_target_pairs={{0,16},{16,0},{8,24},{24,8},{1,17},{17,1},{9,25},{25,9},{2,18},{18... | collective-permute-start | bytes 1474568 | tf_op jit(solution)/shard_map/ppermute | solution.py:530
  111.2 16.8 %collective-permute-start.13 = (bf16[960,256]{1,0:T(8,128)(2,1)S(1)}, bf16[960,256]{1,0:T(8,128)(2,1)S(1)}, u32[]{:S(2)}, u32[]{:S(2)}) collective-permute-start(bf16[960,256]{1,0:T(8,128)(2,1)S(1)} %get-tuple-element.118), channel_id=1, source_target_pairs={{0,8},{8,0},{16,24},{24,16},{1,9},{9,1},{17,25},{25,17},{2,10},{10... | collective-permute-start | bytes 1474568 | tf_op jit(solution)/shard_map/ppermute | solution.py:530
  111.9 16.2 %collective-permute-start.14 = (bf16[960,256]{1,0:T(8,128)(2,1)S(1)}, bf16[960,256]{1,0:T(8,128)(2,1)S(1)}, u32[]{:S(2)}, u32[]{:S(2)}) collective-permute-start(bf16[960,256]{1,0:T(8,128)(2,1)S(1)} %get-tuple-element.119), channel_id=1, source_target_pairs={{0,16},{16,0},{8,24},{24,8},{1,17},{17,1},{9,25},{25,9},{2,18},{18... | collective-permute-start | bytes 1474568 | tf_op jit(solution)/shard_map/ppermute | solution.py:530
  126.0 50.2 %collective-permute-start.17 = (bf16[1408,512]{1,0:T(8,128)(2,1)}, bf16[1408,512]{1,0:T(8,128)(2,1)}, u32[]{:S(2)}, u32[]{:S(2)}) collective-permute-start(bf16[1408,512]{1,0:T(8,128)(2,1)} %get-tuple-element.125), channel_id=1, source_target_pairs={{0,8},{8,0},{16,24},{24,16},{1,9},{9,1},{17,25},{25,17},{2,10},{10... | collective-permute-start | bytes 4325384 | tf_op jit(solution)/shard_map/ppermute | solution.py:530
  126.6 49.5 %collective-permute-start.18 = (bf16[1408,512]{1,0:T(8,128)(2,1)}, bf16[1408,512]{1,0:T(8,128)(2,1)}, u32[]{:S(2)}, u32[]{:S(2)}) collective-permute-start(bf16[1408,512]{1,0:T(8,128)(2,1)} %get-tuple-element.126), channel_id=1, source_target_pairs={{0,16},{16,0},{8,24},{24,8},{1,17},{17,1},{9,25},{25,9},{2,18},{18... | collective-permute-start | bytes 4325384 | tf_op jit(solution)/shard_map/ppermute | solution.py:530
  133.2 37.0 %collective-permute-start.15 = (bf16[960,256]{1,0:T(8,128)(2,1)}, bf16[960,256]{1,0:T(8,128)(2,1)}, u32[]{:S(2)}, u32[]{:S(2)}) collective-permute-start(bf16[960,256]{1,0:T(8,128)(2,1)} %get-tuple-element.128), channel_id=1, source_target_pairs={{0,16},{16,0},{8,24},{24,8},{1,17},{17,1},{9,25},{25,9},{2,18},{18... | collective-permute-start | bytes 1474568 | tf_op jit(solution)/shard_map/ppermute | solution.py:548
  134.4 39.2 %collective-permute-start.16 = (bf16[960,256]{1,0:T(8,128)(2,1)}, bf16[960,256]{1,0:T(8,128)(2,1)}, u32[]{:S(2)}, u32[]{:S(2)}) collective-permute-start(bf16[960,256]{1,0:T(8,128)(2,1)} %get-tuple-element.130), channel_id=1, source_target_pairs={{0,8},{8,0},{16,24},{24,16},{1,9},{9,1},{17,25},{25,17},{2,10},{10... | collective-permute-start | bytes 1474568 | tf_op jit(solution)/shard_map/ppermute | solution.py:548
  162.2 121.1 %reduce-scatter.3.cloned.1.call-start = ((), (), s32[]{:S(2)}) async-start(), calls=%async_computation.4 | async-start | bytes 4718592 | tf_op jit(solution)/shard_map/reduce_scatter | solution.py:723
  172.2 22.8 %collective-permute-start.19 = (bf16[960,256]{1,0:T(8,128)(2,1)}, bf16[960,256]{1,0:T(8,128)(2,1)}, u32[]{:S(2)}, u32[]{:S(2)}) collective-permute-start(bf16[960,256]{1,0:T(8,128)(2,1)} %add.194.refs_0_), channel_id=1, source_target_pairs={{0,16},{16,0},{8,24},{24,8},{1,17},{17,1},{9,25},{25,9},{2,18},{18... | collective-permute-start | bytes 1474568 | tf_op jit(solution)/shard_map/ppermute | solution.py:554
  175.6 16.1 %collective-permute-start.20 = (bf16[960,256]{1,0:T(8,128)(2,1)}, bf16[960,256]{1,0:T(8,128)(2,1)}, u32[]{:S(2)}, u32[]{:S(2)}) collective-permute-start(bf16[960,256]{1,0:T(8,128)(2,1)} %add.195.refs_1_), channel_id=1, source_target_pairs={{0,8},{8,0},{16,24},{24,16},{1,9},{9,1},{17,25},{25,17},{2,10},{10... | collective-permute-start | bytes 1474568 | tf_op jit(solution)/shard_map/ppermute | solution.py:554
  185.8 52.9 %collective-permute-start.23 = (bf16[1408,256]{1,0:T(8,128)(2,1)}, bf16[1408,256]{1,0:T(8,128)(2,1)}, u32[]{:S(2)}, u32[]{:S(2)}) collective-permute-start(bf16[1408,256]{1,0:T(8,128)(2,1)} %get-tuple-element.141), channel_id=1, source_target_pairs={{0,16},{16,0},{8,24},{24,8},{1,17},{17,1},{9,25},{25,9},{2,18},{18... | collective-permute-start | bytes 2162696 | tf_op jit(solution)/shard_map/ppermute | solution.py:548
  187.3 48.5 %collective-permute-start.24 = (bf16[1408,256]{1,0:T(8,128)(2,1)}, bf16[1408,256]{1,0:T(8,128)(2,1)}, u32[]{:S(2)}, u32[]{:S(2)}) collective-permute-start(bf16[1408,256]{1,0:T(8,128)(2,1)} %get-tuple-element.143), channel_id=1, source_target_pairs={{0,8},{8,0},{16,24},{24,16},{1,9},{9,1},{17,25},{25,17},{2,10},{10... | collective-permute-start | bytes 2162696 | tf_op jit(solution)/shard_map/ppermute | solution.py:548
  193.5 29.6 %collective-permute-start.22 = (bf16[1920,256]{1,0:T(8,128)(2,1)}, bf16[1920,256]{1,0:T(8,128)(2,1)}, u32[]{:S(2)}, u32[]{:S(2)}) collective-permute-start(bf16[1920,256]{1,0:T(8,128)(2,1)} %constant_dynamic-update-slice_fusion.2), channel_id=1, source_target_pairs={{0,16},{16,0},{8,24},{24,8},{1,17},{17,1},{9,25},{25,9},{2,18},{18... | collective-permute-start | bytes 2949128 | tf_op jit(solution)/shard_map/ppermute | solution.py:560
  196.8 33.4 %collective-permute-start.21 = (bf16[1920,256]{1,0:T(8,128)(2,1)}, bf16[1920,256]{1,0:T(8,128)(2,1)}, u32[]{:S(2)}, u32[]{:S(2)}) collective-permute-start(bf16[1920,256]{1,0:T(8,128)(2,1)} %constant_dynamic-update-slice_fusion), channel_id=1, source_target_pairs={{0,8},{8,0},{16,24},{24,16},{1,9},{9,1},{17,25},{25,17},{2,10},{10... | collective-permute-start | bytes 2949128 | tf_op jit(solution)/shard_map/ppermute | solution.py:560
  202.5 42.1 %collective-permute-start.25 = (bf16[768,512]{1,0:T(8,128)(2,1)}, bf16[768,512]{1,0:T(8,128)(2,1)}, u32[]{:S(2)}, u32[]{:S(2)}) collective-permute-start(bf16[768,512]{1,0:T(8,128)(2,1)} %get-tuple-element.148), channel_id=1, source_target_pairs={{0,8},{8,0},{16,24},{24,16},{1,9},{9,1},{17,25},{25,17},{2,10},{10... | collective-permute-start | bytes 2359304 | tf_op jit(solution)/shard_map/ppermute | solution.py:530
  223.2 21.4 %collective-permute-start.26 = (bf16[768,512]{1,0:T(8,128)(2,1)}, bf16[768,512]{1,0:T(8,128)(2,1)S(1)}, u32[]{:S(2)}, u32[]{:S(2)}) collective-permute-start(bf16[768,512]{1,0:T(8,128)(2,1)} %copy-done.29), channel_id=1, source_target_pairs={{0,16},{16,0},{8,24},{24,8},{1,17},{17,1},{9,25},{25,9},{2,18},{18... | collective-permute-start | bytes 2359304 | tf_op jit(solution)/shard_map/ppermute | solution.py:530
  238.2 22.6 %collective-permute-start.28 = (bf16[1408,256]{1,0:T(8,128)(2,1)}, bf16[1408,256]{1,0:T(8,128)(2,1)}, u32[]{:S(2)}, u32[]{:S(2)}) collective-permute-start(bf16[1408,256]{1,0:T(8,128)(2,1)} %add.217.refs_1_), channel_id=1, source_target_pairs={{0,8},{8,0},{16,24},{24,16},{1,9},{9,1},{17,25},{25,17},{2,10},{10... | collective-permute-start | bytes 2162696 | tf_op jit(solution)/shard_map/ppermute | solution.py:554
  240.9 18.7 %collective-permute-start.27 = (bf16[1408,256]{1,0:T(8,128)(2,1)}, bf16[1408,256]{1,0:T(8,128)(2,1)}, u32[]{:S(2)}, u32[]{:S(2)}) collective-permute-start(bf16[1408,256]{1,0:T(8,128)(2,1)} %add.216.refs_0_), channel_id=1, source_target_pairs={{0,16},{16,0},{8,24},{24,8},{1,17},{17,1},{9,25},{25,9},{2,18},{18... | collective-permute-start | bytes 2162696 | tf_op jit(solution)/shard_map/ppermute | solution.py:554
  247.6 18.0 %collective-permute-start.29 = (bf16[768,256]{1,0:T(8,128)(2,1)S(1)}, bf16[768,256]{1,0:T(8,128)(2,1)S(1)}, u32[]{:S(2)}, u32[]{:S(2)}) collective-permute-start(bf16[768,256]{1,0:T(8,128)(2,1)S(1)} %get-tuple-element.167), channel_id=1, source_target_pairs={{0,16},{16,0},{8,24},{24,8},{1,17},{17,1},{9,25},{25,9},{2,18},{18... | collective-permute-start | bytes 1179656 | tf_op jit(solution)/shard_map/ppermute | solution.py:548
  248.3 19.0 %collective-permute-start.30 = (bf16[768,256]{1,0:T(8,128)(2,1)S(1)}, bf16[768,256]{1,0:T(8,128)(2,1)S(1)}, u32[]{:S(2)}, u32[]{:S(2)}) collective-permute-start(bf16[768,256]{1,0:T(8,128)(2,1)S(1)} %get-tuple-element.168), channel_id=1, source_target_pairs={{0,8},{8,0},{16,24},{24,16},{1,9},{9,1},{17,25},{25,17},{2,10},{10... | collective-permute-start | bytes 1179656 | tf_op jit(solution)/shard_map/ppermute | solution.py:548
  265.7 12.1 %collective-permute-start.31 = (bf16[768,256]{1,0:T(8,128)(2,1)S(1)}, bf16[768,256]{1,0:T(8,128)(2,1)S(1)}, u32[]{:S(2)}, u32[]{:S(2)}) collective-permute-start(bf16[768,256]{1,0:T(8,128)(2,1)S(1)} %add.218.refs_0_), channel_id=1, source_target_pairs={{0,16},{16,0},{8,24},{24,8},{1,17},{17,1},{9,25},{25,9},{2,18},{18... | collective-permute-start | bytes 1179656 | tf_op jit(solution)/shard_map/ppermute | solution.py:554
  267.4 12.1 %collective-permute-start.32 = (bf16[768,256]{1,0:T(8,128)(2,1)S(1)}, bf16[768,256]{1,0:T(8,128)(2,1)S(1)}, u32[]{:S(2)}, u32[]{:S(2)}) collective-permute-start(bf16[768,256]{1,0:T(8,128)(2,1)S(1)} %add.219.refs_1_), channel_id=1, source_target_pairs={{0,8},{8,0},{16,24},{24,16},{1,9},{9,1},{17,25},{25,17},{2,10},{10... | collective-permute-start | bytes 1179656 | tf_op jit(solution)/shard_map/ppermute | solution.py:554
  268.2 35.1 %collective-permute-start.41 = (bf16[2816,256]{1,0:T(8,128)(2,1)}, bf16[2816,256]{1,0:T(8,128)(2,1)}, u32[]{:S(2)}, u32[]{:S(2)}) collective-permute-start(bf16[2816,256]{1,0:T(8,128)(2,1)} %copy-done.65), channel_id=1, source_target_pairs={{0,16},{16,0},{8,24},{24,8},{1,17},{17,1},{9,25},{25,9},{2,18},{18... | collective-permute-start | bytes 4325384 | tf_op jit(solution)/shard_map/ppermute | solution.py:560
  269.7 35.8 %collective-permute-start.40 = (bf16[2816,256]{1,0:T(8,128)(2,1)}, bf16[2816,256]{1,0:T(8,128)(2,1)}, u32[]{:S(2)}, u32[]{:S(2)}) collective-permute-start(bf16[2816,256]{1,0:T(8,128)(2,1)} %copy-done.66), channel_id=1, source_target_pairs={{0,8},{8,0},{16,24},{24,16},{1,9},{9,1},{17,25},{25,17},{2,10},{10... | collective-permute-start | bytes 4325384 | tf_op jit(solution)/shard_map/ppermute | solution.py:560
  293.2 1.2 collective-permute-start.33
  294.4 3.9 %collective-permute-start.34 = (f32[4096]{0:T(1024)S(1)}, f32[4096]{0:T(1024)S(1)}, u32[]{:S(2)}, u32[]{:S(2)}) collective-permute-start(f32[4096]{0:T(1024)S(1)} %add.220), channel_id=1, source_target_pairs={{0,2},{1,3},{2,0},{3,1},{4,6},{5,7},{6,4},{7,5},{8,10},{9,11},{10,... | collective-permute-start | bytes 49160 | tf_op jit(solution)/shard_map/ppermute | solution.py:589
  298.3 4.7 %collective-permute-start.35 = (f32[4096]{0:T(1024)S(1)}, f32[4096]{0:T(1024)S(1)}, u32[]{:S(2)}, u32[]{:S(2)}) collective-permute-start(f32[4096]{0:T(1024)S(1)} %add.221), channel_id=1, source_target_pairs={{0,4},{1,5},{2,6},{3,7},{4,0},{5,1},{6,2},{7,3},{8,12},{9,13},{10,... | collective-permute-start | bytes 49160 | tf_op jit(solution)/shard_map/ppermute | solution.py:589
  300.8 19.1 %collective-permute-start.39 = (bf16[1536,256]{1,0:T(8,128)(2,1)}, bf16[1536,256]{1,0:T(8,128)(2,1)S(1)}, u32[]{:S(2)}, u32[]{:S(2)}) collective-permute-start(bf16[1536,256]{1,0:T(8,128)(2,1)} %constant_dynamic-update-slice_fusion.10), channel_id=1, source_target_pairs={{0,16},{16,0},{8,24},{24,8},{1,17},{17,1},{9,25},{25,9},{2,18},{18... | collective-permute-start | bytes 2359304 | tf_op jit(solution)/shard_map/ppermute | solution.py:560
  301.5 19.8 %collective-permute-start.38 = (bf16[1536,256]{1,0:T(8,128)(2,1)S(1)}, bf16[1536,256]{1,0:T(8,128)(2,1)S(1)}, u32[]{:S(2)}, u32[]{:S(2)}) collective-permute-start(bf16[1536,256]{1,0:T(8,128)(2,1)S(1)} %copy-done.68), channel_id=1, source_target_pairs={{0,8},{8,0},{16,24},{24,16},{1,9},{9,1},{17,25},{25,17},{2,10},{10... | collective-permute-start | bytes 2359304 | tf_op jit(solution)/shard_map/ppermute | solution.py:560
  305.5 16.0 %collective-permute-start.36 = (f32[4864]{0:T(1024)S(1)}, f32[4864]{0:T(1024)S(1)}, u32[]{:S(2)}, u32[]{:S(2)}) collective-permute-start(f32[4864]{0:T(1024)S(1)} %pad_maximum_fusion.1), channel_id=1, source_target_pairs={{0,8},{8,0},{16,24},{24,16},{1,9},{9,1},{17,25},{25,17},{2,10},{10... | collective-permute-start | bytes 58376 | tf_op jit(solution)/shard_map/ppermute | solution.py:589
  321.5 3.8 %collective-permute-start.37 = (f32[4864]{0:T(1024)S(1)}, f32[4864]{0:T(1024)S(1)}, u32[]{:S(2)}, u32[]{:S(2)}) collective-permute-start(f32[4864]{0:T(1024)S(1)} %fusion.19), channel_id=1, source_target_pairs={{0,16},{8,24},{16,0},{24,8},{1,17},{9,25},{17,1},{25,9},{2,18},{10... | collective-permute-start | bytes 58376 | tf_op jit(solution)/shard_map/ppermute | solution.py:589
  (70 other events, 369.6 us)
Sparse Core Ops, SparseCore 0:
  13.3 59.7 all-gather.2
  75.3 28.4 all-gather.4
  162.3 47.9 reduce-scatter.4
  213.1 48.1 reduce-scatter.2
